TPU v7x, 32 devices: a whole 2x2x4 slice. The times are simulated.
32 devices in a mesh: seq: 16 (over z, x, core), tp: 2 (over y).
Axes of the slice: x: 2, y: 2, z: 4, core: 2. Of those that a mesh axis runs over, the one named last changes fastest.
Arguments:
- queries: bfloat16 [4096, 3072], P(('seq', 'tp')), may hold values from -42 to 42
- keys: bfloat16 [4096, 3072], P(('seq', 'tp')), may hold values from -6 to 6
- values: bfloat16 [4096, 3072], P(('seq', 'tp')), may hold values from -6 to 6
- pool_keys: bfloat16 [16, 128, 3072], P('seq', None, 'tp'), may hold values from -6 to 6
- pool_values: bfloat16 [16, 128, 3072], P('seq', None, 'tp'), may hold values from -6 to 6
- page_table: int32 [16], replicated, may hold values from 0 to 15, each once
- lengths: int32 [32], replicated, may hold values from 1 to 256, 4096 in all
- group_of: int32 [32], replicated, may hold values from 0 to 1
Outputs:
- context: bfloat16 [4096, 3072], P(('seq', 'tp'))
- new_keys: bfloat16 [4096, 3072], P('seq', 'tp')
- new_values: bfloat16 [4096, 3072], P('seq', 'tp')
Inputs may be any that keep to these rules, and one draw needn't show every extreme that they name: `page_table`: each of the 16 slots appears once; entries g * 8 to (g + 1) * 8 - 1 are group g's pages; slot s lies on index s of seq. The lengths sum to 4096; each request's suffix tokens follow those of the requests before it.
All inputs are finite; a program needn't handle non-finite values.
Results may differ from a plain program's by a relative error of at most 0.0055.
Values may be sent and summed in bfloat16 or wider, within the bound.
No kernel may reach another device: no remote copies, remote signals or barrier semaphores. Data moves between devices by JAX's collectives and lax.ppermute only.
A program may use at most 64 MiB of HBM per device.

v0:
```python
import math

import jax
import jax.numpy as jnp
from jax import lax
from jax.sharding import PartitionSpec as P

HD = 96
ROT = 24


def shifted(block, axis, distance):
    devices = range(lax.axis_size(axis))
    route = [(i - distance, i) for i in devices if i - distance in devices]
    return lax.ppermute(block, axis, route)


def rotate(matrix, position):
    count = matrix.shape[0]
    split_heads = matrix.reshape(count, -1, HD)
    half_rot = ROT // 2
    inverse_freq = 10000.0 ** (-(jnp.arange(half_rot, dtype=jnp.float32) * 2.0 / ROT))
    angles = position.astype(jnp.float32)[:, None] * inverse_freq[None, :]
    cosine = jnp.cos(angles)[:, None, :]
    sine = jnp.sin(angles)[:, None, :]
    first_half = split_heads[..., :half_rot]
    second_half = split_heads[..., half_rot:ROT]
    rest_dims = split_heads[..., ROT:]
    turned = jnp.concatenate(
        [
            first_half * cosine - second_half * sine,
            second_half * cosine + first_half * sine,
            rest_dims,
        ],
        axis=-1,
    )
    return turned.reshape(count, -1)


def local(queries, keys, values, pool_keys, pool_values, page_table, lengths, group_of):
    seq_count = lax.axis_size("seq")
    head_queries, head_keys, head_values = (
        lax.all_to_all(queries, "tp", split_axis=1, concat_axis=0, tiled=True),
        lax.all_to_all(keys, "tp", split_axis=1, concat_axis=0, tiled=True),
        lax.all_to_all(values, "tp", split_axis=1, concat_axis=0, tiled=True),
    )
    tok_rows = head_queries.shape[0]
    channels = head_queries.shape[1]
    heads_here = channels // HD
    page_rows = pool_keys.shape[1]
    slots_here = pool_keys.shape[0]
    slot_count = slots_here * seq_count
    pages_group = slot_count // 2
    prefix_len = pages_group * page_rows
    request_count = lengths.shape[0]
    request_ends = jnp.cumsum(lengths)
    request_starts = request_ends - lengths
    request_ids = jnp.arange(request_count, dtype=jnp.int32)
    my_index = lax.axis_index("seq")
    row_base = my_index * tok_rows
    query_rows = row_base + jnp.arange(tok_rows, dtype=jnp.int32)
    request = jnp.sum((query_rows[:, None] >= request_ends[None, :]).astype(jnp.int32), axis=1)
    one_hot = (request[:, None] == request_ids[None, :]).astype(jnp.int32)
    offset = query_rows - jnp.sum(one_hot * request_starts[None, :], axis=1)
    group = jnp.sum(one_hot * group_of[None, :], axis=1)
    position = prefix_len + offset
    rot_queries = rotate(head_queries.astype(jnp.float32), position).astype(jnp.bfloat16)
    rot_keys = rotate(head_keys.astype(jnp.float32), position).astype(jnp.bfloat16)
    earlier_keys, earlier_values = shifted((rot_keys, head_values), "seq", 1)
    earlier_rows = query_rows - tok_rows
    earlier_request = jnp.sum(
        (earlier_rows[:, None] >= request_ends[None, :]).astype(jnp.int32), axis=1
    )
    suffix_keys = jnp.concatenate([earlier_keys, rot_keys], axis=0)
    suffix_values = jnp.concatenate([earlier_values, head_values], axis=0)
    key_rows = jnp.concatenate([earlier_rows, query_rows], axis=0)
    key_request = jnp.concatenate([earlier_request, request], axis=0)
    suffix_mask = (
        (key_request[None, :] == request[:, None])
        & (key_rows[None, :] <= query_rows[:, None])
        & (key_rows[None, :] >= 0)
    )
    slot_ids = jnp.arange(slot_count, dtype=jnp.int32)
    member = (page_table[None, :] == slot_ids[:, None]) & (slot_ids[None, :] >= pages_group)
    slot_group = jnp.any(member, axis=1).astype(jnp.int32)
    score_scale = HD ** (-0.5)

    def attend(state, query_block, key_block, value_block, allowed):
        row_max, total, accum = state
        query_heads = query_block.reshape(query_block.shape[0], heads_here, HD)
        key_heads = key_block.reshape(key_block.shape[0], heads_here, HD)
        value_heads = value_block.reshape(value_block.shape[0], heads_here, HD)
        scores = (
            jnp.einsum("qhd,khd->hqk", query_heads, key_heads, preferred_element_type=jnp.float32)
            * score_scale
        )
        scores = jnp.where(allowed[None], scores, -1e30)
        new_max = jnp.maximum(row_max, jnp.max(scores, axis=-1))
        weights = jnp.where(allowed[None], jnp.exp(scores - new_max[..., None]), 0.0)
        factor = jnp.exp(row_max - new_max)
        new_total = total * factor + jnp.sum(weights, axis=-1)
        weights_bf16 = weights.astype(jnp.bfloat16)
        new_accum = accum * factor[..., None] + jnp.einsum(
            "hqk,khd->hqd", weights_bf16, value_heads, preferred_element_type=jnp.float32
        )
        return (new_max, new_total, new_accum)

    initial = (
        jnp.full((heads_here, tok_rows), -1e30, jnp.float32),
        jnp.zeros((heads_here, tok_rows), jnp.float32),
        jnp.zeros((heads_here, tok_rows, HD), jnp.float32),
    )
    state = initial
    piece_keys = lax.all_gather(pool_keys, "seq", axis=0, tiled=True)
    piece_slots = piece_keys.shape[0]
    piece_ids = jnp.arange(piece_slots, dtype=jnp.int32)
    piece_group = jnp.sum(
        (piece_ids[:, None] == slot_ids[None, :]).astype(jnp.int32) * slot_group[None, :], axis=1
    )
    block_pages = math.gcd(piece_slots, 4)
    block_count = piece_slots // block_pages
    keys_blocked = piece_keys.reshape(block_count, block_pages * page_rows, channels)
    values_blocked = lax.all_gather(pool_values, "seq", axis=0, tiled=True).reshape(
        block_count, block_pages * page_rows, channels
    )
    groups_blocked = piece_group.reshape(block_count, block_pages)

    def one_step(running, item):
        key_block, value_block, group_block = item
        key_group = jnp.repeat(group_block, page_rows)
        allowed = group[:, None] == key_group[None, :]
        return (attend(running, rot_queries, key_block, value_block, allowed), None)

    state, _ = lax.scan(one_step, state, (keys_blocked, values_blocked, groups_blocked))
    state = attend(state, rot_queries, suffix_keys, suffix_values, suffix_mask)
    final_max, final_total, final_accum = state
    context_heads = (
        (final_accum / final_total[..., None])
        .transpose(1, 0, 2)
        .reshape(tok_rows, channels)
        .astype(jnp.bfloat16)
    )
    context = lax.all_to_all(context_heads, "tp", split_axis=0, concat_axis=1, tiled=True)
    return (context, rot_keys, head_values)


def solution(mesh):
    return jax.shard_map(
        local,
        mesh=mesh,
        in_specs=(
            P(("seq", "tp"), None),
            P(("seq", "tp"), None),
            P(("seq", "tp"), None),
            P("seq", None, "tp"),
            P("seq", None, "tp"),
            P(),
            P(),
            P(),
        ),
        out_specs=(P(("seq", "tp"), None), P("seq", "tp"), P("seq", "tp")),
        check_vma=False,
    )
```

profile of v0, /device:TPU:25, one launch (start us, length us, event | category | flops | bytes accessed | tf_op | source)
XLA Modules:
  0.0 231.1 jit_solution(7883897953230040163)
XLA Ops:
  8.7 2.4 %copy.66 = bf16[128,3072]{0,1:T(8,128)(2,1)} copy(bf16[128,3072]{1,0:T(8,128)(2,1)} %param.11) | data formatting | bytes 1572864 | tf_op args[1]
  11.1 3.5 %all-to-all-start.1 = ((bf16[128,2,1536]{0,2,1:T(8,128)(2,1)}), bf16[128,2,1536]{0,2,1:T(8,128)(2,1)S(1)}, u32[]{:S(2)}, u32[]{:S(2)}) async-start(bf16[128,2,1536]{0,2,1:T(8,128)(2,1)} %bitcast.6), calls=%async_computation.1 | async-start | bytes 1572864 | tf_op jit(solution)/shard_map/all_to_all | solution.py:44
  16.6 8.3 %all-to-all-done.1 = bf16[128,2,1536]{0,2,1:T(8,128)(2,1)S(1)} async-done(((bf16[128,2,1536]{0,2,1:T(8,128)(2,1)}), bf16[128,2,1536]{0,2,1:T(8,128)(2,1)S(1)}, u32[]{:S(2)}, u32[]{:S(2)}) %all-to-all-start.1) | async-done | bytes 786464 | tf_op jit(solution)/shard_map/all_to_all | solution.py:44
  24.9 3.5 %all-to-all-start.2 = ((bf16[128,2,1536]{0,2,1:T(8,128)(2,1)}), bf16[128,2,1536]{0,2,1:T(8,128)(2,1)S(1)}, u32[]{:S(2)}, u32[]{:S(2)}) async-start(bf16[128,2,1536]{0,2,1:T(8,128)(2,1)} %bitcast.10), calls=%async_computation.2 | async-start | bytes 1572864 | tf_op jit(solution)/shard_map/all_to_all | solution.py:45
  29.8 8.0 %all-to-all-done.2 = bf16[128,2,1536]{0,2,1:T(8,128)(2,1)S(1)} async-done(((bf16[128,2,1536]{0,2,1:T(8,128)(2,1)}), bf16[128,2,1536]{0,2,1:T(8,128)(2,1)S(1)}, u32[]{:S(2)}, u32[]{:S(2)}) %all-to-all-start.2) | async-done | bytes 786464 | tf_op jit(solution)/shard_map/all_to_all | solution.py:45
  37.8 3.5 %all-to-all-start = ((bf16[128,2,1536]{0,2,1:T(8,128)(2,1)}), bf16[128,2,1536]{0,2,1:T(8,128)(2,1)S(1)}, u32[]{:S(2)}, u32[]{:S(2)}) async-start(bf16[128,2,1536]{0,2,1:T(8,128)(2,1)} %bitcast.2), calls=%async_computation | async-start | bytes 1572864 | tf_op jit(solution)/shard_map/all_to_all | solution.py:43
  41.6 6.5 %copy.67 = bf16[2,128,1536]{1,0,2:T(2,128)(2,1)S(1)} copy(bf16[2,128,1536]{1,2,0:T(8,128)(2,1)S(1)} %bitcast.88) | data formatting | bytes 1572864 | tf_op jit(solution)/shard_map/convert_element_type | solution.py:68
  48.6 1.3 convert_element_type.81
  51.1 5.4 %collective-permute-start.1 = (bf16[256,1536]{1,0:T(8,128)(2,1)}, bf16[256,1536]{1,0:T(8,128)(2,1)}, u32[]{:S(2)}, u32[]{:S(2)}) collective-permute-start(bf16[256,1536]{1,0:T(8,128)(2,1)} %bitcast.12), channel_id=1, source_target_pairs={{0,2},{2,4},{4,6},{6,8},{8,10},{10,12},{12,14},{14,16},{16,18},{18... | collective-permute-start | bytes 2359304 | tf_op jit(solution)/shard_map/ppermute | solution.py:15
  57.8 2.1 collective-permute-start
  60.0 5.7 %copy.63 = f32[2,128,1536]{1,0,2:T(2,128)S(1)} copy(f32[2,128,1536]{1,2,0:T(8,128)S(1)} %convert_bitcast_fusion) | data formatting | bytes 3145728 | tf_op jit(solution)/shard_map/convert_element_type | solution.py:67
  65.7 2.4 %reshape.288 = f32[256,16,96]{0,2,1:T(8,128)} reshape(f32[2,128,1536]{1,0,2:T(2,128)S(1)} %copy.63) | data formatting | bytes 3145728 | tf_op jit(solution)/shard_map/convert_element_type | solution.py:67
  68.1 1.4 slice.27
  69.5 6.5 %copy.71 = bf16[2,128,1536]{1,0,2:T(2,128)(2,1)S(1)} copy(bf16[2,128,1536]{1,2,0:T(8,128)(2,1)S(1)} %bitcast.83) | data formatting | bytes 1572864 | tf_op jit(solution)/shard_map/all_to_all | solution.py:45
  76.0 1.4 concatenate.34
  78.7 2.3 copy.70
  81.0 1.2 pad_maximum_fusion
  82.3 5.0 %fusion.14 = (f32[16,256]{1,0:T(8,128)S(1)}, f32[16,256,512]{2,1,0:T(8,128)}) fusion(pred[256,512]{1,0:T(8,128)(4,1)S(1)} %and_and_fusion, bf16[256,16,96]{0,2,1:T(8,128)(2,1)S(1)} %maximum_convert_fusion, bf16[512,16,96]{0,2,1:T(8,128)(2,1)S(1)} %bitcast.87), kind=kOutput, calls=%fused_computation.24 | convolution fusion | flops 408940544 | bytes 10895360 | tf_op jit(solution)/shard_map/qhd,khd->hqk/dot_general | solution.py:94
  87.2 50.7 %all-gather.5.cloned.1.call-done = bf16[16,128,1536]{2,1,0:T(8,128)(2,1)} async-done(((bf16[1,128,1536]{2,1,0:T(8,128)(2,1)}), bf16[16,128,1536]{2,1,0:T(8,128)(2,1)}) %all-gather.5.cloned.1.call-update) | async-done | bytes 6291472 | tf_op jit(solution)/shard_map/all_gather | solution.py:123
  138.0 59.7 %while.15 = (s32[]{:T(128)}, f32[16,256]{1,0:T(8,128)S(1)}, f32[16,256]{1,0:T(8,128)S(1)}, f32[16,256,96]{1,2,0:T(8,128)}, s32[256]{0:T(256)S(1)}, /*index=5*/s3...) while((s32[]{:T(128)}, f32[16,256]{1,0:T(8,128)S(1)}, ...), condition=%wide.region_9.10_spmd.clone, body=%wide.region_6.0_spmd.clone.sunk | while | flops 833900544 | bytes 77075816 | solution.py:134
  139.0 2.1 constant_dynamic-slice_fusion.4
  141.1 1.6 copy.81
  142.7 1.6 copy.82
  144.3 2.7 %fusion.58 = (f32[16,256]{1,0:T(8,128)S(1)}, f32[16,512,256]{2,1,0:T(8,128)S(1)}) fusion(pred[256,512]{0,1:T(8,128)(4,1)S(1)} %broadcast_compare_fusion.3, bf16[512,16,96]{0,2,1:T(8,128)(2,1)S(1)} %bitcast.77, bf16[256,16,96]{0,2,1:T(8,128)(2,1)} %bitcast.80), kind=kOutput, calls=%fused_computation.2.clone.1 | convolution fusion | flops 408940544 | bytes 10895360 | tf_op jit(solution)/shard_map/while/body/eval_jaxpr/qhd,khd->hqk/dot_general | solution.py:94
  147.1 2.0 fusion.59
  149.1 2.6 %fusion.61 = f32[16,256,96]{1,2,0:T(8,128)S(1)} fusion(f32[16,256,96]{1,2,0:T(8,128)S(1)} %copy-done.12, bf16[512,16,96]{0,2,1:T(8,128)(2,1)S(1)} %bitcast.78, f32[16,512,256]{2,1,0:T(8,128)S(1)} %get-tuple-element.239, f32[16,256]{1,0:T(8,128)S(1)} %select_maximum_fusion.2, pred[256,512]{0,1:T(8,128)(4,1)S(1)} %broadcast_compare_fusion.3, ...), kind=kOutput, calls=%fused_computation.8.clone.1 | convolution fusion | flops 414318592 | bytes 13271041 | tf_op jit(solution)/shard_map/while/body/eval_jaxpr/hqk,khd->hqd/dot_general | solution.py:103
  153.9 2.1 constant_dynamic-slice_fusion.4
  156.0 1.6 copy.81
  157.6 1.6 copy.82
  159.2 2.7 %fusion.58 = (f32[16,256]{1,0:T(8,128)S(1)}, f32[16,512,256]{2,1,0:T(8,128)S(1)}) fusion(pred[256,512]{0,1:T(8,128)(4,1)S(1)} %broadcast_compare_fusion.3, bf16[512,16,96]{0,2,1:T(8,128)(2,1)S(1)} %bitcast.77, bf16[256,16,96]{0,2,1:T(8,128)(2,1)} %bitcast.80), kind=kOutput, calls=%fused_computation.2.clone.1 | convolution fusion | flops 408940544 | bytes 10895360 | tf_op jit(solution)/shard_map/while/body/eval_jaxpr/qhd,khd->hqk/dot_general | solution.py:94
  162.0 2.0 fusion.59
  164.1 2.6 %fusion.61 = f32[16,256,96]{1,2,0:T(8,128)S(1)} fusion(f32[16,256,96]{1,2,0:T(8,128)S(1)} %copy-done.12, bf16[512,16,96]{0,2,1:T(8,128)(2,1)S(1)} %bitcast.78, f32[16,512,256]{2,1,0:T(8,128)S(1)} %get-tuple-element.239, f32[16,256]{1,0:T(8,128)S(1)} %select_maximum_fusion.2, pred[256,512]{0,1:T(8,128)(4,1)S(1)} %broadcast_compare_fusion.3, ...), kind=kOutput, calls=%fused_computation.8.clone.1 | convolution fusion | flops 414318592 | bytes 13271041 | tf_op jit(solution)/shard_map/while/body/eval_jaxpr/hqk,khd->hqd/dot_general | solution.py:103
  168.8 2.1 constant_dynamic-slice_fusion.4
  170.9 1.6 copy.81
  172.5 1.6 copy.82
  174.2 2.7 %fusion.58 = (f32[16,256]{1,0:T(8,128)S(1)}, f32[16,512,256]{2,1,0:T(8,128)S(1)}) fusion(pred[256,512]{0,1:T(8,128)(4,1)S(1)} %broadcast_compare_fusion.3, bf16[512,16,96]{0,2,1:T(8,128)(2,1)S(1)} %bitcast.77, bf16[256,16,96]{0,2,1:T(8,128)(2,1)} %bitcast.80), kind=kOutput, calls=%fused_computation.2.clone.1 | convolution fusion | flops 408940544 | bytes 10895360 | tf_op jit(solution)/shard_map/while/body/eval_jaxpr/qhd,khd->hqk/dot_general | solution.py:94
  176.9 2.0 fusion.59
  179.0 2.6 %fusion.61 = f32[16,256,96]{1,2,0:T(8,128)S(1)} fusion(f32[16,256,96]{1,2,0:T(8,128)S(1)} %copy-done.12, bf16[512,16,96]{0,2,1:T(8,128)(2,1)S(1)} %bitcast.78, f32[16,512,256]{2,1,0:T(8,128)S(1)} %get-tuple-element.239, f32[16,256]{1,0:T(8,128)S(1)} %select_maximum_fusion.2, pred[256,512]{0,1:T(8,128)(4,1)S(1)} %broadcast_compare_fusion.3, ...), kind=kOutput, calls=%fused_computation.8.clone.1 | convolution fusion | flops 414318592 | bytes 13271041 | tf_op jit(solution)/shard_map/while/body/eval_jaxpr/hqk,khd->hqd/dot_general | solution.py:103
  183.8 2.1 constant_dynamic-slice_fusion.4
  185.9 1.6 copy.81
  187.5 1.6 copy.82
  189.1 2.7 %fusion.58 = (f32[16,256]{1,0:T(8,128)S(1)}, f32[16,512,256]{2,1,0:T(8,128)S(1)}) fusion(pred[256,512]{0,1:T(8,128)(4,1)S(1)} %broadcast_compare_fusion.3, bf16[512,16,96]{0,2,1:T(8,128)(2,1)S(1)} %bitcast.77, bf16[256,16,96]{0,2,1:T(8,128)(2,1)} %bitcast.80), kind=kOutput, calls=%fused_computation.2.clone.1 | convolution fusion | flops 408940544 | bytes 10895360 | tf_op jit(solution)/shard_map/while/body/eval_jaxpr/qhd,khd->hqk/dot_general | solution.py:94
  191.8 2.0 fusion.59
  193.9 2.6 %fusion.61 = f32[16,256,96]{1,2,0:T(8,128)S(1)} fusion(f32[16,256,96]{1,2,0:T(8,128)S(1)} %copy-done.12, bf16[512,16,96]{0,2,1:T(8,128)(2,1)S(1)} %bitcast.78, f32[16,512,256]{2,1,0:T(8,128)S(1)} %get-tuple-element.239, f32[16,256]{1,0:T(8,128)S(1)} %select_maximum_fusion.2, pred[256,512]{0,1:T(8,128)(4,1)S(1)} %broadcast_compare_fusion.3, ...), kind=kOutput, calls=%fused_computation.8.clone.1 | convolution fusion | flops 414318592 | bytes 13271041 | tf_op jit(solution)/shard_map/while/body/eval_jaxpr/hqk,khd->hqd/dot_general | solution.py:103
  197.7 5.0 %fusion.15 = f32[16,256]{1,0:T(8,128)S(1)} fusion(f32[16,256,512]{2,1,0:T(8,128)} %get-tuple-element.173, f32[16,256]{1,0:T(8,128)S(1)} %max.6, pred[256,512]{1,0:T(8,128)(4,1)S(1)} %and_and_fusion), kind=kLoop, calls=%fused_computation.25 | loop fusion | flops 10481664 | bytes 8552448 | tf_op jit(solution)/shard_map/reduce_sum | solution.py:101
  203.5 4.2 %fusion.27 = bf16[256,16,96]{0,2,1:T(8,128)(2,1)S(1)} fusion(bf16[256,16,96]{0,2,1:T(8,128)(2,1)} %concatenate.34, bf16[256,16,96]{0,2,1:T(8,128)(2,1)} %bitcast.90, f32[16,256,512]{2,1,0:T(8,128)S(1)} %copy-done.4, f32[16,256]{1,0:T(8,128)S(1)} %max.6, pred[256,512]{1,0:T(8,128)(4,1)S(1)} %and_and_fusion, f32[16,256,96]{1,2,0:T(8,128)} %get-tuple-element.52, ...), kind=kOutput, calls=%fused_computation.36 | convolution fusion | flops 417857536 | bytes 12500992 | tf_op jit(solution)/shard_map/hqk,khd->hqd/dot_general | solution.py:103
  208.9 3.5 %all-to-all-start.3 = ((bf16[2,128,1536]{1,2,0:T(8,128)(2,1)}), bf16[2,128,1536]{1,2,0:T(8,128)(2,1)S(1)}, u32[]{:S(2)}, u32[]{:S(2)}) async-start(bf16[2,128,1536]{1,2,0:T(8,128)(2,1)} %copy.72), calls=%async_computation.3 | async-start | bytes 1572864 | tf_op jit(solution)/shard_map/all_to_all | solution.py:143
  213.6 9.5 %all-to-all-done.3 = bf16[2,128,1536]{1,2,0:T(8,128)(2,1)S(1)} async-done(((bf16[2,128,1536]{1,2,0:T(8,128)(2,1)}), bf16[2,128,1536]{1,2,0:T(8,128)(2,1)S(1)}, u32[]{:S(2)}, u32[]{:S(2)}) %all-to-all-start.3) | async-done | bytes 786464 | tf_op jit(solution)/shard_map/all_to_all | solution.py:143
  (134 shorter events, 22.5 us)
Async XLA Ops:
  7.2 7.4 %copy-start.9 = (s32[32]{0:T(128)S(1)}, s32[32]{0:T(128)}, u32[]{:S(2)}) copy-start(s32[32]{0:T(128)} %param.16) | copy-start | bytes 388
  7.2 7.7 %copy-start.7 = (bf16[128,3072]{1,0:T(8,128)(2,1)S(1)}, bf16[128,3072]{1,0:T(8,128)(2,1)}, u32[]{:S(2)}) copy-start(bf16[128,3072]{1,0:T(8,128)(2,1)} %param.12) | copy-start | bytes 2359300
  7.2 8.9 %copy-start.11 = (s32[16]{0:T(128)S(1)}, s32[16]{0:T(128)}, u32[]{:S(2)}) copy-start(s32[16]{0:T(128)} %param.15) | copy-start | bytes 196
  7.2 9.1 %copy-start.10 = (s32[32]{0:T(128)S(1)}, s32[32]{0:T(128)}, u32[]{:S(2)}) copy-start(s32[32]{0:T(128)} %param.17) | copy-start | bytes 388
  7.2 80.0 %all-gather.3.cloned.1.call-start = ((), (), s32[]{:S(2)}) async-start(), calls=%async_computation.4 | async-start | bytes 6684672 | tf_op jit(solution)/shard_map/all_gather | solution.py:114
  7.9 130.0 %all-gather.5.cloned.1.call-start = ((), (), s32[]{:S(2)}) async-start(), calls=%async_computation.5 | async-start | bytes 6684672 | tf_op jit(solution)/shard_map/all_gather | solution.py:123
  8.7 19.8 %copy-start.8 = (bf16[128,3072]{1,0:T(8,128)(2,1)S(1)}, bf16[128,3072]{1,0:T(8,128)(2,1)}, u32[]{:S(2)}) copy-start(bf16[128,3072]{1,0:T(8,128)(2,1)} %param.10) | copy-start | bytes 2359300
  11.1 13.8 %all-to-all-start.1 = ((bf16[128,2,1536]{0,2,1:T(8,128)(2,1)}), bf16[128,2,1536]{0,2,1:T(8,128)(2,1)S(1)}, u32[]{:S(2)}, u32[]{:S(2)}) async-start(bf16[128,2,1536]{0,2,1:T(8,128)(2,1)} %bitcast.6), calls=%async_computation.1 | async-start | bytes 1572864 | tf_op jit(solution)/shard_map/all_to_all | solution.py:44
  24.9 12.9 %all-to-all-start.2 = ((bf16[128,2,1536]{0,2,1:T(8,128)(2,1)}), bf16[128,2,1536]{0,2,1:T(8,128)(2,1)S(1)}, u32[]{:S(2)}, u32[]{:S(2)}) async-start(bf16[128,2,1536]{0,2,1:T(8,128)(2,1)} %bitcast.10), calls=%async_computation.2 | async-start | bytes 1572864 | tf_op jit(solution)/shard_map/all_to_all | solution.py:45
  37.8 22.1 %all-to-all-start = ((bf16[128,2,1536]{0,2,1:T(8,128)(2,1)}), bf16[128,2,1536]{0,2,1:T(8,128)(2,1)S(1)}, u32[]{:S(2)}, u32[]{:S(2)}) async-start(bf16[128,2,1536]{0,2,1:T(8,128)(2,1)} %bitcast.2), calls=%async_computation | async-start | bytes 1572864 | tf_op jit(solution)/shard_map/all_to_all | solution.py:43
  51.1 27.6 %collective-permute-start.1 = (bf16[256,1536]{1,0:T(8,128)(2,1)}, bf16[256,1536]{1,0:T(8,128)(2,1)}, u32[]{:S(2)}, u32[]{:S(2)}) collective-permute-start(bf16[256,1536]{1,0:T(8,128)(2,1)} %bitcast.12), channel_id=1, source_target_pairs={{0,2},{2,4},{4,6},{6,8},{8,10},{10,12},{12,14},{14,16},{16,18},{18... | collective-permute-start | bytes 2359304 | tf_op jit(solution)/shard_map/ppermute | solution.py:15
  57.8 23.2 %copy-start.5 = (bf16[256,16,96]{0,2,1:T(8,128)(2,1)}, bf16[256,16,96]{0,2,1:T(8,128)(2,1)S(1)}, u32[]{:S(2)}) copy-start(bf16[256,16,96]{0,2,1:T(8,128)(2,1)S(1)} %pad_maximum_fusion.1) | copy-start | bytes 2359300
  57.8 23.2 %collective-permute-start = (bf16[256,1536]{0,1:T(8,128)(2,1)S(1)}, bf16[256,1536]{0,1:T(8,128)(2,1)}, u32[]{:S(2)}, u32[]{:S(2)}) collective-permute-start(bf16[256,1536]{0,1:T(8,128)(2,1)S(1)} %bitcast.84), channel_id=1, source_target_pairs={{0,2},{2,4},{4,6},{6,8},{8,10},{10,12},{12,14},{14,16},{16,18},{18... | collective-permute-start | bytes 2359304 | tf_op jit(solution)/shard_map/ppermute | solution.py:15
  138.0 0.9 copy-start.2
  142.7 1.6 copy-start
  147.0 2.1 copy-start.1
  147.1 2.1 copy-start.12
  149.1 3.8 %copy-start.3 = (bf16[256,1536]{0,1:T(8,128)(2,1)S(1)}, bf16[256,1536]{0,1:T(8,128)(2,1)}, u32[]{:S(2)}) copy-start(bf16[256,1536]{0,1:T(8,128)(2,1)} %copy-done.2) | copy-start | bytes 2359300 | tf_op jit(solution)/shard_map/while
  151.7 1.2 copy-start.13
  152.9 0.9 copy-start.2
  157.6 1.6 copy-start
  162.0 2.1 copy-start.1
  162.0 2.1 copy-start.12
  164.1 3.8 %copy-start.3 = (bf16[256,1536]{0,1:T(8,128)(2,1)S(1)}, bf16[256,1536]{0,1:T(8,128)(2,1)}, u32[]{:S(2)}) copy-start(bf16[256,1536]{0,1:T(8,128)(2,1)} %copy-done.2) | copy-start | bytes 2359300 | tf_op jit(solution)/shard_map/while
  166.6 1.2 copy-start.13
  167.8 0.9 copy-start.2
  172.5 1.6 copy-start
  176.9 2.1 copy-start.1
  176.9 2.1 copy-start.12
  179.0 3.8 %copy-start.3 = (bf16[256,1536]{0,1:T(8,128)(2,1)S(1)}, bf16[256,1536]{0,1:T(8,128)(2,1)}, u32[]{:S(2)}) copy-start(bf16[256,1536]{0,1:T(8,128)(2,1)} %copy-done.2) | copy-start | bytes 2359300 | tf_op jit(solution)/shard_map/while
  181.6 1.2 copy-start.13
  182.7 0.9 copy-start.2
  187.5 1.6 copy-start
  191.8 2.1 copy-start.1
  191.8 2.1 copy-start.12
  193.9 3.8 %copy-start.3 = (bf16[256,1536]{0,1:T(8,128)(2,1)S(1)}, bf16[256,1536]{0,1:T(8,128)(2,1)}, u32[]{:S(2)}) copy-start(bf16[256,1536]{0,1:T(8,128)(2,1)} %copy-done.2) | copy-start | bytes 2359300 | tf_op jit(solution)/shard_map/while
  196.5 1.2 copy-start.13
  197.7 5.8 %copy-start.4 = (f32[16,256,512]{2,1,0:T(8,128)S(1)}, f32[16,256,512]{2,1,0:T(8,128)}, u32[]{:S(2)}) copy-start(f32[16,256,512]{2,1,0:T(8,128)} %get-tuple-element.173) | copy-start | bytes 25165828
  207.7 4.7 %copy-start.6 = (bf16[256,16,96]{0,2,1:T(8,128)(2,1)S(1)}, bf16[256,16,96]{0,2,1:T(8,128)(2,1)}, u32[]{:S(2)}) copy-start(bf16[256,16,96]{0,2,1:T(8,128)(2,1)} %copy-done.5) | copy-start | bytes 2359300
  208.9 14.2 %all-to-all-start.3 = ((bf16[2,128,1536]{1,2,0:T(8,128)(2,1)}), bf16[2,128,1536]{1,2,0:T(8,128)(2,1)S(1)}, u32[]{:S(2)}, u32[]{:S(2)}) async-start(bf16[2,128,1536]{1,2,0:T(8,128)(2,1)} %copy.72), calls=%async_computation.3 | async-start | bytes 1572864 | tf_op jit(solution)/shard_map/all_to_all | solution.py:143
Sparse Core Ops, SparseCore 0:
  10.3 62.2 all-gather.2
  74.9 62.9 all-gather.4
where the time goes:
time: 235 us; the launch traced here: 231 us
  waiting for transfers between devices  77.9 us (33%)
  local copies, waits for them, and re-layouts  66.6 us (28%)
  matrix products  30.2 us (13%)
  starting transfers between devices  21.7 us (9%)
  other arithmetic  19.8 us (8%)
  between operations  14.4 us (6%)
    all_gather x1, waiting for transfers between devices, local(): lax.all_gather(pool_values, 'seq', axis=0, tiled=True)  50.7 us
    dynamic_slice x12, local copies, waits for them, and re-layouts, local(): lax.scan(one_step, state, (keys_blocked, values_blocked, groups_blocked))  21.3 us
    dot_general x5, matrix products, attend(): jnp.einsum('qhd,khd->hqk', query_heads, key_heads, preferred_element_type...  15.8 us
    dot_general x5, matrix products, attend(): jnp.einsum('hqk,khd->hqd', weights_bf16, value_heads, preferred_element_t...  14.4 us
    reduce_sum x5, other arithmetic, attend(): new_total = total * factor + jnp.sum(weights, axis=-1)  13 us
    all_to_all x1, waiting for transfers between devices, local(): lax.all_to_all(context_heads, 'tp', split_axis=0, concat_axis=1, tiled=True)  9.5 us
    all_to_all x1, waiting for transfers between devices, local(): lax.all_to_all(keys, 'tp', split_axis=1, concat_axis=0, tiled=True)  8.32 us
    convert_element_type x2, local copies, waits for them, and re-layouts, local(): head_queries.astype(jnp.float32)  8.12 us
  transfers between devices with their start and end apart: 8, of which 4 were waited for; matrix products, arithmetic and copies ran while one was open for 19% of the time, Pallas kernels for 0%

commit v1 on v0

v1 whole, which is shorter than its diff:
```python
import functools

import jax
import jax.numpy as jnp
from jax import lax
from jax.experimental import pallas as pl
from jax.experimental.pallas import tpu as pltpu
from jax.sharding import PartitionSpec as P

HD = 96
ROT = 24
SLAB = 4
LOG2E = 1.4426950408889634
VMEM = pl.BlockSpec(memory_space=pltpu.VMEM)
SMEM = pl.BlockSpec(memory_space=pltpu.SMEM)
ANY = pl.BlockSpec(memory_space=pl.ANY)


def params(mib):
    return pltpu.CompilerParams(vmem_limit_bytes=mib << 20)


def shape(rows, lanes):
    return jax.ShapeDtypeStruct((rows, lanes), jnp.bfloat16)


def cost(flops, moved, exps=0):
    return pl.CostEstimate(flops=flops, bytes_accessed=moved, transcendentals=exps)


def starts_and_groups(rows, table):
    starts, ends, groups = table[0:1], table[1:2], table[2:3]
    start = jnp.max(jnp.where(ends <= rows, ends, 0.0), axis=1, keepdims=True)
    inside = (starts <= rows) & (rows < ends)
    group = jnp.sum(jnp.where(inside, groups, 0.0), axis=1, keepdims=True)
    return start, group


def lanes_at(ref, index, each, count, *lead):
    if each % 128 == 0:
        return ref[(*lead, slice(None), pl.ds(pl.multiple_of(index * each, each), each))]
    x = ref[(*lead, slice(None), slice(0, each))]
    for i in range(1, count):
        x = jnp.where(index == i, ref[(*lead, slice(None), slice(i * each, (i + 1) * each))], x)
    return x


def page_kernel(chunks, place, keys, values, *outs):
    lanes = keys.shape[-1] // SLAB
    half = lanes // chunks
    for n in range(SLAB):
        k = lanes_at(keys, place[1] ^ n, lanes, SLAB, 0)
        v = lanes_at(values, place[1] ^ n, lanes, SLAB, 0)
        for c in range(chunks):
            cut = slice(c * half, (c + 1) * half)
            pair = [k[:, cut], v[:, cut]]
            outs[c * SLAB + n][...] = jnp.concatenate(pair[::-1] if c else pair, axis=1)


def cut_page(place, keys, values, chunks):
    lanes = keys.shape[-1] // SLAB // chunks * 2
    outs = pl.pallas_call(
        functools.partial(page_kernel, chunks),
        out_shape=[shape(keys.shape[1], lanes)] * (SLAB * chunks),
        in_specs=[SMEM, VMEM, VMEM],
        out_specs=[VMEM] * (SLAB * chunks),
        compiler_params=params(16),
        cost_estimate=cost(0, 4 * keys.size),
    )(place, keys, values)
    return [outs[c * SLAB : (c + 1) * SLAB] for c in range(chunks)]


def rotate_kernel(tp, prefix, place, table, freq, queries, keys, values, *outs):
    rows, lanes = queries.shape[0], queries.shape[1] // tp
    width = freq.shape[1]
    token = place[2] + lax.broadcasted_iota(jnp.int32, (rows, 1), 0)
    token = token.astype(jnp.float32)
    start, _ = starts_and_groups(token, table[...])
    angle = (prefix + token - start) * freq[...]
    dim = lax.rem(lax.broadcasted_iota(jnp.int32, (rows, width), 1), HD)
    cosine, sine = jnp.cos(angle), jnp.sin(angle)
    keep = jnp.where(dim < ROT, cosine, 1.0)
    after = jnp.where(dim < ROT // 2, -sine, 0.0)
    before = jnp.where((dim >= ROT // 2) & (dim < ROT), sine, 0.0)
    for m in range(tp):
        base = (place[3] ^ m) * lanes
        for part in range(lanes // width):
            at = pl.ds(pl.multiple_of(base + part * width, width), width)
            to = pl.ds(part * width, width)
            for source, out in ((queries, outs[m]), (keys, outs[tp + m])):
                x = source[:, at].astype(jnp.float32)
                far = pltpu.roll(x, width - ROT // 2, 1)
                near = pltpu.roll(x, ROT // 2, 1)
                out[:, to] = (x * keep + far * after + near * before).astype(jnp.bfloat16)
            outs[2 * tp + m][:, to] = values[:, at]


def rotate_and_cut(place, table, freq, queries, keys, values, tp, prefix):
    rows, lanes = queries.shape[0], queries.shape[1] // tp
    outs = pl.pallas_call(
        functools.partial(rotate_kernel, tp, prefix),
        out_shape=[shape(rows, lanes)] * (3 * tp),
        in_specs=[SMEM] + [VMEM] * 5,
        out_specs=[VMEM] * (3 * tp),
        compiler_params=params(24),
        cost_estimate=cost(0, 12 * queries.size),
    )(place, table, freq, queries, keys, values)
    return outs[:tp], outs[tp : 2 * tp], outs[2 * tp :]


def query_kernel(tp, place, *refs):
    parts, outs = refs[:tp], refs[tp:]
    rows, lanes = parts[0].shape[0], outs[0].shape[1]
    for m in range(tp):
        to = pl.ds(pl.multiple_of((place[3] ^ m) * rows, rows), rows)
        for n in range(SLAB):
            outs[n][to, :] = lanes_at(parts[m], place[1] ^ n, lanes, SLAB)


def cut_queries(place, parts):
    tp = len(parts)
    rows, lanes = parts[0].shape
    return pl.pallas_call(
        functools.partial(query_kernel, tp),
        out_shape=[shape(rows * tp, lanes // SLAB)] * SLAB,
        in_specs=[SMEM] + [VMEM] * tp,
        out_specs=[VMEM] * SLAB,
        compiler_params=params(16),
        cost_estimate=cost(0, 4 * tp * parts[0].size),
    )(place, *parts)


def suffix_kernel(tp, chunks, place, *refs):
    keys, values = refs[:tp], refs[tp : 2 * tp]
    new_keys, new_values = refs[2 * tp : 2 * tp + 2]
    outs = refs[2 * tp + 2 :]
    rows, lanes = keys[0].shape[0], new_keys.shape[1] // SLAB
    for m in range(tp):
        to = pl.ds(pl.multiple_of((place[3] ^ m) * rows, rows), rows)
        new_keys[to, :] = keys[m][...]
        new_values[to, :] = values[m][...]
        for n in range(SLAB):
            k = lanes_at(keys[m], place[1] ^ n, lanes, SLAB)
            v = lanes_at(values[m], place[1] ^ n, lanes, SLAB)
            half = lanes // 2
            parts = [k, v[:, half:], v[:, :half]] if chunks == 2 else [k, v]
            outs[n][to, :] = jnp.concatenate(parts, axis=1)


def cut_suffix(place, keys, values, chunks):
    tp = len(keys)
    rows, lanes = keys[0].shape
    outs = pl.pallas_call(
        functools.partial(suffix_kernel, tp, chunks),
        out_shape=[shape(rows * tp, lanes)] * 2 + [shape(rows * tp, lanes // SLAB * 2)] * SLAB,
        in_specs=[SMEM] + [VMEM] * (2 * tp),
        out_specs=[VMEM] * (2 + SLAB),
        compiler_params=params(24),
        cost_estimate=cost(0, 12 * tp * keys[0].size),
    )(place, *keys, *values)
    return outs[0], outs[1], outs[2:]


def window(lane, count, lanes):
    return lane // 128 * 128, min(-(-(lane + count) // 128) * 128, lanes)


def attend_kernel(plan, place, pages, table, *refs):
    chunk, heads, lines, early_count, unit_count, page, block = plan
    q_parts, kv_parts = refs[:SLAB], refs[SLAB : 2 * SLAB]
    early = refs[2 * SLAB : 2 * SLAB + early_count]
    units = refs[2 * SLAB + early_count : 2 * SLAB + early_count + unit_count]
    refs = refs[2 * SLAB + early_count + unit_count :]
    outs, (q_all, kv_all, pool, seat, sems) = refs[:SLAB], refs[SLAB:]
    z, j = place[0], place[1]
    slots = lines * SLAB
    middle = (z > 0) & (z < lines - 1)
    copies = []

    def start(source, target, other=None, take_other=None):
        sem = sems.at[len(copies)]
        copy = pltpu.make_async_copy(source, target, sem)
        if other is None:
            copy.start()
        else:
            pl.when(jnp.logical_not(take_other))(copy.start)
            pl.when(take_other)(pltpu.make_async_copy(other, target, sem).start)
        copies.append(copy)

    def fill(i, carry):
        seat[pages[i]] = i
        return carry

    lax.fori_loop(0, slots, fill, 0)
    for n in range(SLAB):
        at = pl.multiple_of((j ^ n) * block, block)
        start(q_parts[n], q_all.at[pl.ds(at, block)])
        start(kv_parts[n], kv_all.at[pl.ds(at + block, block)])
    before = kv_all.at[pl.ds(0, block)]
    if early_count == 2:
        start(early[0], before, early[1], z == 2)
    else:
        start(early[0], before)
    if unit_count == 6:
        own, a1, b1, a2, b2, a3 = units
        third, fourth = jnp.where(z < 2, 2, 1), jnp.where(z < 2, 3, 0)
        sources = [(own, None, z, 0), (a1, None, z ^ 1, 0), (a2, b1, third, 0), (a3, b2, fourth, 0)]
    else:
        sources = [(units[0], None, line, line * SLAB * page) for line in range(lines)]
    for source, other, line, base in sources:
        for n in range(SLAB):
            rows = pl.ds(base + n * page, page)
            to = pl.multiple_of(seat[line * SLAB + (j ^ n)] * page, page)
            target = pool.at[pl.ds(to, page)]
            if other is None:
                start(source.at[rows], target)
            else:
                start(source.at[rows], target, other.at[rows], middle)
    for copy in copies:
        copy.wait()

    half = slots // 2 * page
    own_lanes = q_all.shape[1]
    width = heads * HD
    key_lane = chunk * width
    value_lane = (key_lane + width) % (2 * width)
    key_low, key_high = window(key_lane, width, 2 * own_lanes)
    low, high = window(value_lane, width, 2 * width)
    near_low = low + (own_lanes if 2 * width == own_lanes else 0)
    key_at, value_at = slice(key_low, key_high), slice(low, high)
    near_at = slice(near_low, near_low + high - low)
    factor = HD ** (-0.5) * LOG2E
    contract = (((1,), (1,)), ((), ()))
    first = z * (SLAB * block)

    def dot_t(x, y):
        return lax.dot_general(x, y, contract, preferred_element_type=jnp.float32)

    def dot(x, y):
        return jnp.dot(x, y, preferred_element_type=jnp.float32)

    def one_block(n, carry):
        b = j ^ n
        rows = pl.ds(pl.multiple_of(b * block, block), block)
        token = first + b * block + lax.broadcasted_iota(jnp.int32, (block, 1), 0)
        request_start, group = starts_and_groups(token.astype(jnp.float32), table[...])
        zero_group = group < 0.5
        key = first + (b - 1) * block + lax.broadcasted_iota(jnp.int32, (block, 2 * block), 1)
        near = (key >= request_start.astype(jnp.int32)) & (key <= token)
        near_rows = pl.ds(pl.multiple_of(b * block, block), 2 * block)
        query_high = min(key_high, own_lanes)
        queries = q_all[rows, key_low:query_high]
        lane = key_low + lax.broadcasted_iota(jnp.int32, queries.shape, 1)
        out_lane = low + lax.broadcasted_iota(jnp.int32, (block, high - low), 1)
        result = jnp.zeros((block, high - low), jnp.float32)
        for h in range(heads):
            begin = key_lane + h * HD
            query = jnp.where((lane >= begin) & (lane < begin + HD), queries, jnp.zeros_like(queries))
            if query_high < key_high:
                rest = jnp.zeros((block, key_high - query_high), query.dtype)
                query = jnp.concatenate([query, rest], axis=1)
            score = jnp.where(
                zero_group,
                dot_t(query, pool[0:half, key_at]),
                dot_t(query, pool[half : 2 * half, key_at]),
            )
            near_score = jnp.where(near, dot_t(query, kv_all[near_rows, key_at]), -1e30)
            top = jnp.maximum(
                jnp.max(score, axis=1, keepdims=True), jnp.max(near_score, axis=1, keepdims=True)
            )
            weight = jnp.exp2((score - top) * factor)
            near_weight = jnp.exp2((near_score - top) * factor)
            total = jnp.sum(weight, axis=1, keepdims=True) + jnp.sum(
                near_weight, axis=1, keepdims=True
            )
            narrow = weight.astype(jnp.bfloat16)
            nothing = jnp.zeros_like(narrow)
            mixed = (
                dot(jnp.where(zero_group, narrow, nothing), pool[0:half, value_at])
                + dot(jnp.where(zero_group, nothing, narrow), pool[half : 2 * half, value_at])
                + dot(near_weight.astype(jnp.bfloat16), kv_all[near_rows, near_at])
            )
            begin = value_lane + h * HD
            inside = (out_lane >= begin) & (out_lane < begin + HD)
            result = jnp.where(inside, mixed / total, result)
        result = result[:, value_lane - low : value_lane - low + width].astype(jnp.bfloat16)
        folded = jnp.concatenate([result[: block // 2], result[block // 2 :]], axis=1)
        for i in range(SLAB):

            @pl.when(n == i)
            def _():
                outs[i][...] = folded

        return carry

    lax.fori_loop(0, SLAB, one_block, 0)


def attend(place, pages, table, q_parts, kv_parts, early, units, chunk, chunks, lines, page):
    block, own_lanes = q_parts[0].shape
    heads = own_lanes // HD // chunks
    slots = lines * SLAB
    pool_lanes = 2 * heads * HD
    plan = (chunk, heads, lines, len(early), len(units), page, block)
    keys = slots * page + 2 * block
    copies = 2 * SLAB + 1 + slots
    return pl.pallas_call(
        functools.partial(attend_kernel, plan),
        out_shape=[shape(block // 2, pool_lanes)] * SLAB,
        in_specs=[SMEM, SMEM, VMEM] + [ANY] * (2 * SLAB + len(early) + len(units)),
        out_specs=[VMEM] * SLAB,
        scratch_shapes=[
            pltpu.VMEM((SLAB * block, own_lanes), jnp.bfloat16),
            pltpu.VMEM(((SLAB + 1) * block, 2 * own_lanes), jnp.bfloat16),
            pltpu.VMEM((slots * page, pool_lanes), jnp.bfloat16),
            pltpu.SMEM((slots,), jnp.int32),
            pltpu.SemaphoreType.DMA((copies,)),
        ],
        compiler_params=params(32),
        cost_estimate=cost(
            4 * SLAB * block * keys * heads * 256,
            2 * keys * pool_lanes,
            SLAB * block * heads * (keys // 2),
        ),
    )(place, pages, table, *q_parts, *kv_parts, *early, *units)


def back_kernel(tp, place, *refs):
    parts, outs = refs[:SLAB], refs[SLAB:]
    rows, lanes = parts[0].shape
    each = 2 * rows // tp
    for m in range(tp):
        first = (place[3] ^ m) * each
        upper = first >= rows
        at = pl.ds(pl.multiple_of(jnp.where(upper, first - rows, first), each), each)
        cuts = []
        for n in range(SLAB):
            x = parts[n][at, :]
            cuts.append(jnp.where(upper, x[:, lanes // 2 :], x[:, : lanes // 2]))
        outs[m][...] = jnp.concatenate(cuts, axis=1)


def cut_back(place, parts, tp):
    rows, lanes = parts[0].shape
    return pl.pallas_call(
        functools.partial(back_kernel, tp),
        out_shape=[shape(2 * rows // tp, lanes // 2 * SLAB)] * tp,
        in_specs=[SMEM] + [VMEM] * SLAB,
        out_specs=[VMEM] * tp,
        compiler_params=params(16),
        cost_estimate=cost(0, 4 * SLAB * rows * lanes),
    )(place, *parts)


def join_kernel(tp, chunks, place, *refs):
    out = refs[-1]
    lanes = out.shape[1] // tp
    each = lanes // SLAB
    cut = each // chunks
    for m in range(tp):
        for n in range(SLAB):
            base = (place[3] ^ m) * lanes + (place[1] ^ n) * each
            pieces = [refs[c * tp + m][:, n * cut : (n + 1) * cut] for c in range(chunks)]
            x = jnp.concatenate(pieces, axis=1) if chunks > 1 else pieces[0]
            if each % 128:
                for i in range(tp * SLAB):

                    @pl.when(base == i * each)
                    def _():
                        out[:, i * each : (i + 1) * each] = x
            else:
                out[:, pl.ds(pl.multiple_of(base, each), each)] = x


def join(place, parts, tp, chunks):
    rows, lanes = parts[0][0].shape
    return pl.pallas_call(
        functools.partial(join_kernel, tp, chunks),
        out_shape=shape(rows, lanes * tp * chunks),
        in_specs=[SMEM] + [VMEM] * (tp * chunks),
        out_specs=VMEM,
        compiler_params=params(16),
        cost_estimate=cost(0, 4 * rows * lanes * tp * chunks),
    )(place, *[x for chunk in parts for x in chunk])


def swap(parts, axis):
    size = lax.axis_size(axis)
    return [parts[0]] + [
        lax.ppermute(parts[m], axis, [(i, i ^ m) for i in range(size)])
        for m in range(1, len(parts))
    ]


def along(block, pairs):
    return lax.ppermute(
        block, "seq", [(a * SLAB + j, b * SLAB + j) for a, b in pairs for j in range(SLAB)]
    )


INNER = [(1, 2), (2, 1)]
OUTER = [(0, 1), (1, 0), (2, 3), (3, 2)]
OUTWARD = [(1, 0), (2, 3)]


def gather(unit, lines):
    if lines == 4:
        a1 = along(unit, OUTER)
        b1 = along(unit, INNER)
        b2 = along(a1, INNER)
        a2 = along(b1, OUTWARD)
        a3 = along(b2, OUTWARD)
        return [unit, a1, b1, a2, b2, a3]
    groups = [[line * SLAB + j for line in range(lines)] for j in range(SLAB)]
    return [lax.all_gather(unit, "seq", axis=0, axis_index_groups=groups, tiled=True)]


def local(queries, keys, values, pool_keys, pool_values, page_table, lengths, group_of):
    seq, tp = lax.axis_size("seq"), lax.axis_size("tp")
    lines = seq // SLAB
    rows = queries.shape[0]
    page = pool_keys.shape[1]
    own_heads = pool_keys.shape[2] // SLAB // HD
    chunks = 2 if own_heads % 2 == 0 else 1
    index, y = lax.axis_index("seq"), lax.axis_index("tp")
    j = index % SLAB
    place = jnp.stack([index // SLAB, j, (index * tp + y) * rows, y]).astype(jnp.int32)
    ends = jnp.cumsum(lengths)
    table = jnp.stack([ends - lengths, ends, group_of]).astype(jnp.float32)
    width = pool_keys.shape[2] // SLAB
    if width % 128:
        width = pool_keys.shape[2]
    dims = (jnp.arange(width) % HD) % (ROT // 2)
    freq = (10000.0 ** (-(dims.astype(jnp.float32) * 2.0 / ROT)))[None]
    prefix = seq // 2 * page

    pieces = cut_page(place, pool_keys, pool_values, chunks)
    q_cut, k_cut, v_cut = rotate_and_cut(place, table, freq, queries, keys, values, tp, prefix)
    units = [
        gather(jnp.concatenate(swap(pieces[c], "seq"), axis=0), lines) for c in range(chunks)
    ]
    q_parts = swap(cut_queries(place, swap(q_cut, "tp")), "seq")
    new_keys, new_values, kv_cut = cut_suffix(place, swap(k_cut, "tp"), swap(v_cut, "tp"), chunks)
    kv_parts = swap(kv_cut, "seq")
    last = lax.select_n(jnp.broadcast_to(j ^ (SLAB - 1), ()), *kv_parts)
    if lines == 4:
        early = [along(last, [(0, 1), (2, 3)]), along(last, [(1, 2)])]
    else:
        early = [along(last, [(i, i + 1) for i in range(lines - 1)])]
    backs = []
    for c in range(chunks):
        outs = attend(
            place, page_table, table, q_parts, kv_parts, early, units[c], c, chunks, lines, page
        )
        backs.append(swap(cut_back(place, swap(outs, "seq"), tp), "tp"))
    return join(place, backs, tp, chunks), new_keys, new_values


def solution(mesh):
    return jax.shard_map(
        local,
        mesh=mesh,
        in_specs=(
            P(("seq", "tp"), None),
            P(("seq", "tp"), None),
            P(("seq", "tp"), None),
            P("seq", None, "tp"),
            P("seq", None, "tp"),
            P(),
            P(),
            P(),
        ),
        out_specs=(P(("seq", "tp"), None), P("seq", "tp"), P("seq", "tp")),
        check_vma=False,
    )
```

time: 235 us -> 144 us (0.61); the launches traced: 231 us -> 143 us
  local copies, waits for them, and re-layouts: 66.6 us -> 6.6 us
  Pallas kernels: 0 us -> 42.4 us
  matrix products: 30.2 us -> 0 us
  waiting for transfers between devices: 77.9 us -> 53.7 us
  other arithmetic: 19.8 us -> 0.37 us
  starting transfers between devices: 21.7 us -> 39.4 us
  between operations: 14.4 us -> 0.96 us
    ppermute x2 -> x35, waiting for transfers between devices: 0.01 us -> 53.7 us  [the longest x23 36.1 us: swap(): lax.ppermute(parts[m], axis, [(i, i ^ m) for i in range(size)])]
    all_gather x2 -> x0, waiting for transfers between devices: 50.7 us -> none  [the longest x1 50.7 us: local(): lax.all_gather(pool_values, 'seq', axis=0, tiled=True)]
    pallas_call x0 -> x9, Pallas kernels: none -> 42.4 us  [the longest x2 32.1 us: attend(): pl.pallas_call(functools.partial(attend_kernel, plan), out_shape=[shape(b...]
    ppermute x2 -> x35, starting transfers between devices: 7.48 us -> 39.4 us  [the longest x23 26.3 us: swap(): lax.ppermute(parts[m], axis, [(i, i ^ m) for i in range(size)])]
    dot_general x10 -> x0, matrix products: 30.2 us -> none  [the longest x5 15.8 us: attend(): jnp.einsum('qhd,khd->hqk', query_heads, key_heads, preferred_element_type...]
    all_to_all x4 -> x0, waiting for transfers between devices: 25.8 us -> none  [the longest x1 9.5 us: local(): lax.all_to_all(context_heads, 'tp', split_axis=0, concat_axis=1, tiled=True)]
    dynamic_slice x12 -> x0, local copies, waits for them, and re-layouts: 21.3 us -> none  [local(): lax.scan(one_step, state, (keys_blocked, values_blocked, groups_blocked))]
    convert_element_type x6 -> x0, local copies, waits for them, and re-layouts: 16.3 us -> none  [the longest x2 8.12 us: local(): head_queries.astype(jnp.float32)]
  transfers between devices with their start and end apart: 8 -> 35, of which waited for: 4 -> 14; matrix products, arithmetic and copies ran while one was open for 19% -> 0% of each run, Pallas kernels for 0% -> 26%
where the time goes in v1:
time: 144 us; the launch traced here: 143 us
  waiting for transfers between devices  53.7 us (37%)
  Pallas kernels  42.4 us (29%)
  starting transfers between devices  39.4 us (27%)
  local copies, waits for them, and re-layouts  6.6 us (5%)
    ppermute x23, waiting for transfers between devices, swap(): lax.ppermute(parts[m], axis, [(i, i ^ m) for i in range(size)])  36.1 us
    pallas_call x2, Pallas kernels, attend(): pl.pallas_call(functools.partial(attend_kernel, plan), out_shape=[shape(b...  32.1 us
    ppermute x23, starting transfers between devices, swap(): lax.ppermute(parts[m], axis, [(i, i ^ m) for i in range(size)])  26.3 us
    ppermute x12, waiting for transfers between devices, along(): lax.ppermute(block, 'seq', [(a * SLAB + j, b * SLAB + j) for a, b in pair...  17.7 us
    ppermute x12, starting transfers between devices, along(): lax.ppermute(block, 'seq', [(a * SLAB + j, b * SLAB + j) for a, b in pair...  13.1 us
    unnamed x30, local copies, waits for them, and re-layouts  6.47 us
    pallas_call x1, Pallas kernels, rotate_and_cut(): pl.pallas_call(functools.partial(rotate_kernel, tp, prefix), out_shape=[s...  2.96 us
  transfers between devices with their start and end apart: 35, of which 14 were waited for; matrix products, arithmetic and copies ran while one was open for 0% of the time, Pallas kernels for 26%

profile of v1, /device:TPU:25, one launch (start us, length us, event | category | flops | bytes accessed | tf_op | source)
XLA Modules:
  0.0 143.4 jit_solution(2688178838568671443)
XLA Ops:
  2.4 1.1 copy-done
  3.5 1.1 copy-done.1
  4.7 1.1 copy-done.2
  5.8 3.0 %shard_map.103 = (bf16[128,1536]{1,0:T(8,128)(2,1)S(1)}, bf16[128,1536]{1,0:T(8,128)(2,1)S(1)}, bf16[128,1536]{1,0:T(8,128)(2,1)S(1)}, bf16[128,1536]{1,0:T(8,12...) custom-call(s32[4]{0:T(128)S(1)} %pad_add_fusion.place, f32[3,32]{1,0:T(4,128)S(1)} %add_convert_fusion.table, ...), custom_call_target="tpu_custom_call" | custom-call | bytes 4718592 | tf_op jit(solution)/shard_map/pallas_call | solution.py:100
  8.8 1.3 collective-permute-start
  10.3 1.2 collective-permute-start.5
  12.3 1.6 %collective-permute-start.11 = (bf16[128,384]{1,0:T(8,128)(2,1)S(1)}, bf16[128,384]{1,0:T(8,128)(2,1)S(1)}, u32[]{:S(2)}, u32[]{:S(2)}) collective-permute-start(bf16[128,384]{1,0:T(8,128)(2,1)S(1)} %get-tuple-element.54), channel_id=1, source_target_pairs={{0,2},{2,0},{4,6},{6,4},{8,10},{10,8},{12,14},{14,12},{16,18},{18,... | collective-permute-start | bytes 294920 | tf_op jit(solution)/shard_map/ppermute | solution.py:390
  13.8 1.2 collective-permute-start.12
  15.1 1.1 collective-permute-start.13
  16.3 2.0 %collective-permute-done.12 = bf16[128,384]{1,0:T(8,128)(2,1)S(1)} collective-permute-done((bf16[128,384]{1,0:T(8,128)(2,1)S(1)}, bf16[128,384]{1,0:T(8,128)(2,1)S(1)}, u32[]{:S(2)}, u32[]{:S(2)}) %collective-permute-start.12) | collective-permute-done | bytes 98336 | tf_op jit(solution)/shard_map/ppermute | solution.py:390
  18.2 1.3 collective-permute-start.23
  19.5 1.2 collective-permute-done.13
  20.8 1.2 collective-permute-start.24
  22.3 3.0 %collective-permute-done.24 = bf16[128,384]{1,0:T(8,128)(2,1)S(1)} collective-permute-done((bf16[128,384]{1,0:T(8,128)(2,1)S(1)}, bf16[128,384]{1,0:T(8,128)(2,1)S(1)}, u32[]{:S(2)}, u32[]{:S(2)}) %collective-permute-start.24) | collective-permute-done | bytes 98336 | tf_op jit(solution)/shard_map/ppermute | solution.py:390
  25.3 1.8 %collective-permute-start.25 = (bf16[128,384]{1,0:T(8,128)(2,1)S(1)}, bf16[128,384]{1,0:T(8,128)(2,1)S(1)}, u32[]{:S(2)}, u32[]{:S(2)}) collective-permute-start(bf16[128,384]{1,0:T(8,128)(2,1)S(1)} %get-tuple-element.66), channel_id=1, source_target_pairs={{0,6},{2,4},{4,2},{6,0},{8,14},{10,12},{12,10},{14,8},{16,22},{18,... | collective-permute-start | bytes 294920 | tf_op jit(solution)/shard_map/ppermute | solution.py:390
  27.1 3.6 %collective-permute-done.25 = bf16[128,384]{1,0:T(8,128)(2,1)S(1)} collective-permute-done((bf16[128,384]{1,0:T(8,128)(2,1)S(1)}, bf16[128,384]{1,0:T(8,128)(2,1)S(1)}, u32[]{:S(2)}, u32[]{:S(2)}) %collective-permute-start.25) | collective-permute-done | bytes 98336 | tf_op jit(solution)/shard_map/ppermute | solution.py:390
  31.4 1.6 %collective-permute-start.26 = (bf16[512,384]{1,0:T(8,128)(2,1)S(1)}, bf16[512,384]{1,0:T(8,128)(2,1)S(1)}, u32[]{:S(2)}, u32[]{:S(2)}) collective-permute-start(bf16[512,384]{1,0:T(8,128)(2,1)S(1)} %constant_dynamic-update-slice_fusion.4.refs_10_), channel_id=1, source_target_pairs={{0,8},{2,10},{4,12},{6,14},{8,0},{10,2},{12,4},{14,6},{16,24},{18,... | collective-permute-start | bytes 1179656 | tf_op jit(solution)/shard_map/ppermute | solution.py:396
  33.0 2.6 %collective-permute-done.5.refs_3_ = bf16[128,1536]{1,0:T(8,128)(2,1)S(1)} collective-permute-done((bf16[128,1536]{1,0:T(8,128)(2,1)S(1)}, bf16[128,1536]{1,0:T(8,128)(2,1)S(1)}, u32[]{:S(2)}, u32[]{:S(2)}) %collective-permute-start.5) | collective-permute-done | bytes 393248 | tf_op jit(solution)/shard_map/ppermute | solution.py:390
  35.7 2.3 %shard_map.105 = (bf16[256,1536]{1,0:T(8,128)(2,1)}, bf16[256,1536]{1,0:T(8,128)(2,1)}, bf16[256,768]{1,0:T(8,128)(2,1)S(1)}, bf16[256,768]{1,0:T(8,128)(2,1)}, ...) custom-call(s32[4]{0:T(128)S(1)} %pad_add_fusion.place, bf16[128,1536]{1,0:T(8,128)(2,1)S(1)} %get-tuple-element.45.refs_0_, ...), custom_call_target="tpu_custom_call" | custom-call | bytes 4718592 | tf_op jit(solution)/shard_map/pallas_call | solution.py:153
  38.0 1.6 %collective-permute-start.6 = (bf16[256,768]{1,0:T(8,128)(2,1)}, bf16[256,768]{1,0:T(8,128)(2,1)S(1)}, u32[]{:S(2)}, u32[]{:S(2)}) collective-permute-start(bf16[256,768]{1,0:T(8,128)(2,1)} %get-tuple-element.50), channel_id=1, source_target_pairs={{0,2},{2,0},{4,6},{6,4},{8,10},{10,8},{12,14},{14,12},{16,18},{18,... | collective-permute-start | bytes 1179656 | tf_op jit(solution)/shard_map/ppermute | solution.py:390
  39.6 1.2 collective-permute-start.7
  41.3 1.4 collective-permute-start.27
  43.4 1.4 collective-permute-start.17
  46.0 4.5 %collective-permute-done.7.refs_6_ = bf16[256,768]{1,0:T(8,128)(2,1)S(1)} collective-permute-done((bf16[256,768]{1,0:T(8,128)(2,1)}, bf16[256,768]{1,0:T(8,128)(2,1)S(1)}, u32[]{:S(2)}, u32[]{:S(2)}) %collective-permute-start.7) | collective-permute-done | bytes 393248 | tf_op jit(solution)/shard_map/ppermute | solution.py:390
  50.5 1.2 collective-permute-start.2
  51.7 7.8 %collective-permute-done.8.refs_7_ = bf16[256,768]{1,0:T(8,128)(2,1)S(1)} collective-permute-done((bf16[256,768]{1,0:T(8,128)(2,1)}, bf16[256,768]{1,0:T(8,128)(2,1)S(1)}, u32[]{:S(2)}, u32[]{:S(2)}) %collective-permute-start.8) | collective-permute-done | bytes 393248 | tf_op jit(solution)/shard_map/ppermute | solution.py:390
  60.5 0.9 copy-done.8
  61.4 1.3 collective-permute-start.16
  63.4 1.3 collective-permute-start.9
  64.7 3.1 %collective-permute-done.3.refs_3_ = bf16[256,384]{1,0:T(8,128)(2,1)S(1)} collective-permute-done((bf16[256,384]{1,0:T(8,128)(2,1)S(1)}, bf16[256,384]{1,0:T(8,128)(2,1)S(1)}, u32[]{:S(2)}, u32[]{:S(2)}) %collective-permute-start.3) | collective-permute-done | bytes 196640 | tf_op jit(solution)/shard_map/ppermute | solution.py:390
  68.5 1.3 collective-permute-start.18
  69.8 3.4 %collective-permute-done.16.refs_13_ = bf16[512,384]{1,0:T(8,128)(2,1)S(1)} collective-permute-done((bf16[512,384]{1,0:T(8,128)(2,1)S(1)}, bf16[512,384]{1,0:T(8,128)(2,1)S(1)}, u32[]{:S(2)}, u32[]{:S(2)}) %collective-permute-start.16) | collective-permute-done | bytes 393248 | tf_op jit(solution)/shard_map/ppermute | solution.py:396
  73.2 1.3 collective-permute-start.28
  74.5 1.3 collective-permute-start.30
  75.8 5.8 %collective-permute-done.9.refs_8_ = bf16[256,768]{1,0:T(8,128)(2,1)S(1)} collective-permute-done((bf16[256,768]{1,0:T(8,128)(2,1)S(1)}, bf16[256,768]{1,0:T(8,128)(2,1)S(1)}, u32[]{:S(2)}, u32[]{:S(2)}) %collective-permute-start.9) | collective-permute-done | bytes 393248 | tf_op jit(solution)/shard_map/ppermute | solution.py:396
  81.6 8.4 %collective-permute-done.18.refs_15_ = bf16[512,384]{1,0:T(8,128)(2,1)S(1)} collective-permute-done((bf16[512,384]{1,0:T(8,128)(2,1)}, bf16[512,384]{1,0:T(8,128)(2,1)S(1)}, u32[]{:S(2)}, u32[]{:S(2)}) %collective-permute-start.18) | collective-permute-done | bytes 393248 | tf_op jit(solution)/shard_map/ppermute | solution.py:396
  90.0 15.9 %shard_map.107 = (bf16[128,384]{1,0:T(8,128)(2,1)S(1)}, bf16[128,384]{1,0:T(8,128)(2,1)S(1)}, bf16[128,384]{1,0:T(8,128)(2,1)S(1)}, bf16[128,384]{1,0:T(8,128)(2,1)S(1)}) custom-call(s32[4]{0:T(128)S(1)} %pad_add_fusion.place, s32[16]{0:T(128)S(1)} %copy-done.9, f32[3,32]{1,0:T(4,128)S(1)} %add_convert_fusion.table, ...), custom_call_target="tpu_custom_call" | custom-call | flops 5368709120 | bytes 1966080 | tf_op jit(solution)/shard_map/pallas_call | solution.py:307
  105.9 2.9 %collective-permute-start.19 = (bf16[128,384]{1,0:T(8,128)(2,1)S(1)}, bf16[128,384]{1,0:T(8,128)(2,1)S(1)}, u32[]{:S(2)}, u32[]{:S(2)}) collective-permute-start(bf16[128,384]{1,0:T(8,128)(2,1)S(1)} %get-tuple-element.58), channel_id=1, source_target_pairs={{0,2},{2,0},{4,6},{6,4},{8,10},{10,8},{12,14},{14,12},{16,18},{18,... | collective-permute-start | bytes 294920 | tf_op jit(solution)/shard_map/ppermute | solution.py:390
  109.0 1.5 %collective-permute-start.21 = (bf16[128,384]{1,0:T(8,128)(2,1)S(1)}, bf16[128,384]{1,0:T(8,128)(2,1)S(1)}, u32[]{:S(2)}, u32[]{:S(2)}) collective-permute-start(bf16[128,384]{1,0:T(8,128)(2,1)S(1)} %get-tuple-element.60), channel_id=1, source_target_pairs={{0,6},{2,4},{4,2},{6,0},{8,14},{10,12},{12,10},{14,8},{16,22},{18,... | collective-permute-start | bytes 294920 | tf_op jit(solution)/shard_map/ppermute | solution.py:390
  110.5 16.2 %shard_map.109 = (bf16[128,384]{1,0:T(8,128)(2,1)S(1)}, bf16[128,384]{1,0:T(8,128)(2,1)S(1)}, bf16[128,384]{1,0:T(8,128)(2,1)S(1)}, bf16[128,384]{1,0:T(8,128)(2,1)S(1)}) custom-call(s32[4]{0:T(128)S(1)} %pad_add_fusion.place, s32[16]{0:T(128)S(1)} %copy-done.9, f32[3,32]{1,0:T(4,128)S(1)} %add_convert_fusion.table, ...), custom_call_target="tpu_custom_call" | custom-call | flops 5368709120 | bytes 1966080 | tf_op jit(solution)/shard_map/pallas_call | solution.py:307
  127.2 1.7 %collective-permute-start.33 = (bf16[128,384]{1,0:T(8,128)(2,1)S(1)}, bf16[128,384]{1,0:T(8,128)(2,1)S(1)}, u32[]{:S(2)}, u32[]{:S(2)}) collective-permute-start(bf16[128,384]{1,0:T(8,128)(2,1)S(1)} %get-tuple-element.70), channel_id=1, source_target_pairs={{0,6},{2,4},{4,2},{6,0},{8,14},{10,12},{12,10},{14,8},{16,22},{18,... | collective-permute-start | bytes 294920 | tf_op jit(solution)/shard_map/ppermute | solution.py:390
  128.9 1.0 shard_map.108
  129.9 1.3 collective-permute-start.22
  131.3 2.6 %collective-permute-done.33.refs_3_ = bf16[128,384]{1,0:T(8,128)(2,1)S(1)} collective-permute-done((bf16[128,384]{1,0:T(8,128)(2,1)S(1)}, bf16[128,384]{1,0:T(8,128)(2,1)S(1)}, u32[]{:S(2)}, u32[]{:S(2)}) %collective-permute-start.33) | collective-permute-done | bytes 98336 | tf_op jit(solution)/shard_map/ppermute | solution.py:390
  133.9 1.0 shard_map.110
  134.9 1.3 collective-permute-start.34
  136.6 5.2 %collective-permute-done.34.refs_3_ = bf16[128,768]{1,0:T(8,128)(2,1)S(1)} collective-permute-done((bf16[128,768]{1,0:T(8,128)(2,1)S(1)}, bf16[128,768]{1,0:T(8,128)(2,1)S(1)}, u32[]{:S(2)}, u32[]{:S(2)}) %collective-permute-start.34) | collective-permute-done | bytes 196640 | tf_op jit(solution)/shard_map/ppermute | solution.py:390
  141.8 1.6 %shard_map.111 = bf16[128,3072]{1,0:T(8,128)(2,1)} custom-call(s32[4]{0:T(128)S(1)} %pad_add_fusion.place, bf16[128,768]{1,0:T(8,128)(2,1)S(1)} %get-tuple-element.61.refs_0_, bf16[128,768]{1,0:T(8,128)(2,1)S(1)} %collective-permute-done.22.refs_1_, bf16[128,768]{1,0:T(8,128)(2,1)S(1)} %get-tuple-element.71.refs_2_, ...), custom_call_target="tpu_custom_call" | custom-call | bytes 1572864 | tf_op jit(solution)/shard_map/pallas_call | solution.py:377
  (71 shorter events, 9.6 us)
Async XLA Ops:
  0.7 0.7 copy-start.10
  1.6 0.7 copy-start.11
  2.4 1.1 copy-start
  3.5 1.1 copy-start.1
  4.7 1.1 copy-start.2
  5.8 5.7 %copy-start.3 = (bf16[1,128,1536]{2,1,0:T(8,128)(2,1)S(1)}, bf16[1,128,1536]{2,1,0:T(8,128)(2,1)}, u32[]{:S(2)}) copy-start(bf16[1,128,1536]{2,1,0:T(8,128)(2,1)} %keys.3) | copy-start | bytes 1179652
  5.8 5.7 %copy-start.4 = (bf16[1,128,1536]{2,1,0:T(8,128)(2,1)S(1)}, bf16[1,128,1536]{2,1,0:T(8,128)(2,1)}, u32[]{:S(2)}) copy-start(bf16[1,128,1536]{2,1,0:T(8,128)(2,1)} %values.3) | copy-start | bytes 1179652
  8.8 30.8 %collective-permute-start = (bf16[128,1536]{1,0:T(8,128)(2,1)S(1)}, bf16[128,1536]{1,0:T(8,128)(2,1)S(1)}, u32[]{:S(2)}, u32[]{:S(2)}) collective-permute-start(bf16[128,1536]{1,0:T(8,128)(2,1)S(1)} %get-tuple-element.40), channel_id=1, source_target_pairs={{0,1},{1,0},{2,3},{3,2},{4,5},{5,4},{6,7},{7,6},{8,9},{9,8},{10,11... | collective-permute-start | bytes 1179656 | tf_op jit(solution)/shard_map/ppermute | solution.py:390
  10.1 21.3 %collective-permute-start.4 = (bf16[128,1536]{1,0:T(8,128)(2,1)S(1)}, bf16[128,1536]{1,0:T(8,128)(2,1)S(1)}, u32[]{:S(2)}, u32[]{:S(2)}) collective-permute-start(bf16[128,1536]{1,0:T(8,128)(2,1)S(1)} %get-tuple-element.46), channel_id=1, source_target_pairs={{0,1},{1,0},{2,3},{3,2},{4,5},{5,4},{6,7},{7,6},{8,9},{9,8},{10,11... | collective-permute-start | bytes 1179656 | tf_op jit(solution)/shard_map/ppermute | solution.py:390
  10.3 25.4 %collective-permute-start.5 = (bf16[128,1536]{1,0:T(8,128)(2,1)S(1)}, bf16[128,1536]{1,0:T(8,128)(2,1)S(1)}, u32[]{:S(2)}, u32[]{:S(2)}) collective-permute-start(bf16[128,1536]{1,0:T(8,128)(2,1)S(1)} %get-tuple-element.48), channel_id=1, source_target_pairs={{0,1},{1,0},{2,3},{3,2},{4,5},{5,4},{6,7},{7,6},{8,9},{9,8},{10,11... | collective-permute-start | bytes 1179656 | tf_op jit(solution)/shard_map/ppermute | solution.py:390
  12.3 2.8 %collective-permute-start.11 = (bf16[128,384]{1,0:T(8,128)(2,1)S(1)}, bf16[128,384]{1,0:T(8,128)(2,1)S(1)}, u32[]{:S(2)}, u32[]{:S(2)}) collective-permute-start(bf16[128,384]{1,0:T(8,128)(2,1)S(1)} %get-tuple-element.54), channel_id=1, source_target_pairs={{0,2},{2,0},{4,6},{6,4},{8,10},{10,8},{12,14},{14,12},{16,18},{18,... | collective-permute-start | bytes 294920 | tf_op jit(solution)/shard_map/ppermute | solution.py:390
  13.8 4.4 %collective-permute-start.12 = (bf16[128,384]{1,0:T(8,128)(2,1)S(1)}, bf16[128,384]{1,0:T(8,128)(2,1)S(1)}, u32[]{:S(2)}, u32[]{:S(2)}) collective-permute-start(bf16[128,384]{1,0:T(8,128)(2,1)S(1)} %get-tuple-element.55), channel_id=1, source_target_pairs={{0,4},{2,6},{4,0},{6,2},{8,12},{10,14},{12,8},{14,10},{16,20},{18,... | collective-permute-start | bytes 294920 | tf_op jit(solution)/shard_map/ppermute | solution.py:390
  15.1 5.7 %collective-permute-start.13 = (bf16[128,384]{1,0:T(8,128)(2,1)S(1)}, bf16[128,384]{1,0:T(8,128)(2,1)S(1)}, u32[]{:S(2)}, u32[]{:S(2)}) collective-permute-start(bf16[128,384]{1,0:T(8,128)(2,1)S(1)} %get-tuple-element.56), channel_id=1, source_target_pairs={{0,6},{2,4},{4,2},{6,0},{8,14},{10,12},{12,10},{14,8},{16,22},{18,... | collective-permute-start | bytes 294920 | tf_op jit(solution)/shard_map/ppermute | solution.py:390
  18.2 3.8 %collective-permute-start.23 = (bf16[128,384]{1,0:T(8,128)(2,1)S(1)}, bf16[128,384]{1,0:T(8,128)(2,1)S(1)}, u32[]{:S(2)}, u32[]{:S(2)}) collective-permute-start(bf16[128,384]{1,0:T(8,128)(2,1)S(1)} %get-tuple-element.64), channel_id=1, source_target_pairs={{0,2},{2,0},{4,6},{6,4},{8,10},{10,8},{12,14},{14,12},{16,18},{18,... | collective-permute-start | bytes 294920 | tf_op jit(solution)/shard_map/ppermute | solution.py:390
  20.8 4.5 %collective-permute-start.24 = (bf16[128,384]{1,0:T(8,128)(2,1)S(1)}, bf16[128,384]{1,0:T(8,128)(2,1)S(1)}, u32[]{:S(2)}, u32[]{:S(2)}) collective-permute-start(bf16[128,384]{1,0:T(8,128)(2,1)S(1)} %get-tuple-element.65), channel_id=1, source_target_pairs={{0,4},{2,6},{4,0},{6,2},{8,12},{10,14},{12,8},{14,10},{16,20},{18,... | collective-permute-start | bytes 294920 | tf_op jit(solution)/shard_map/ppermute | solution.py:390
  22.0 18.8 %collective-permute-start.14 = (bf16[512,384]{1,0:T(8,128)(2,1)S(1)}, bf16[512,384]{1,0:T(8,128)(2,1)S(1)}, u32[]{:S(2)}, u32[]{:S(2)}) collective-permute-start(bf16[512,384]{1,0:T(8,128)(2,1)S(1)} %constant_dynamic-update-slice_fusion.refs_10_), channel_id=1, source_target_pairs={{0,8},{2,10},{4,12},{6,14},{8,0},{10,2},{12,4},{14,6},{16,24},{18,... | collective-permute-start | bytes 1179656 | tf_op jit(solution)/shard_map/ppermute | solution.py:396
  25.3 5.4 %collective-permute-start.25 = (bf16[128,384]{1,0:T(8,128)(2,1)S(1)}, bf16[128,384]{1,0:T(8,128)(2,1)S(1)}, u32[]{:S(2)}, u32[]{:S(2)}) collective-permute-start(bf16[128,384]{1,0:T(8,128)(2,1)S(1)} %get-tuple-element.66), channel_id=1, source_target_pairs={{0,6},{2,4},{4,2},{6,0},{8,14},{10,12},{12,10},{14,8},{16,22},{18,... | collective-permute-start | bytes 294920 | tf_op jit(solution)/shard_map/ppermute | solution.py:390
  30.7 10.6 %collective-permute-start.15 = (bf16[512,384]{1,0:T(8,128)(2,1)S(1)}, bf16[512,384]{1,0:T(8,128)(2,1)S(1)}, u32[]{:S(2)}, u32[]{:S(2)}) collective-permute-start(bf16[512,384]{1,0:T(8,128)(2,1)S(1)} %constant_dynamic-update-slice_fusion.refs_10_), channel_id=1, source_target_pairs={{8,16},{10,18},{12,20},{14,22},{16,8},{18,10},{20,12},{22,14},{9,1... | collective-permute-start | bytes 1179656 | tf_op jit(solution)/shard_map/ppermute | solution.py:396
  31.4 11.3 %collective-permute-start.26 = (bf16[512,384]{1,0:T(8,128)(2,1)S(1)}, bf16[512,384]{1,0:T(8,128)(2,1)S(1)}, u32[]{:S(2)}, u32[]{:S(2)}) collective-permute-start(bf16[512,384]{1,0:T(8,128)(2,1)S(1)} %constant_dynamic-update-slice_fusion.4.refs_10_), channel_id=1, source_target_pairs={{0,8},{2,10},{4,12},{6,14},{8,0},{10,2},{12,4},{14,6},{16,24},{18,... | collective-permute-start | bytes 1179656 | tf_op jit(solution)/shard_map/ppermute | solution.py:396
  38.0 7.5 %collective-permute-start.6 = (bf16[256,768]{1,0:T(8,128)(2,1)}, bf16[256,768]{1,0:T(8,128)(2,1)S(1)}, u32[]{:S(2)}, u32[]{:S(2)}) collective-permute-start(bf16[256,768]{1,0:T(8,128)(2,1)} %get-tuple-element.50), channel_id=1, source_target_pairs={{0,2},{2,0},{4,6},{6,4},{8,10},{10,8},{12,14},{14,12},{16,18},{18,... | collective-permute-start | bytes 1179656 | tf_op jit(solution)/shard_map/ppermute | solution.py:390
  39.6 10.9 %collective-permute-start.7 = (bf16[256,768]{1,0:T(8,128)(2,1)}, bf16[256,768]{1,0:T(8,128)(2,1)S(1)}, u32[]{:S(2)}, u32[]{:S(2)}) collective-permute-start(bf16[256,768]{1,0:T(8,128)(2,1)} %get-tuple-element.51), channel_id=1, source_target_pairs={{0,4},{2,6},{4,0},{6,2},{8,12},{10,14},{12,8},{14,10},{16,20},{18,... | collective-permute-start | bytes 1179656 | tf_op jit(solution)/shard_map/ppermute | solution.py:390
  40.8 18.7 %collective-permute-start.8 = (bf16[256,768]{1,0:T(8,128)(2,1)}, bf16[256,768]{1,0:T(8,128)(2,1)S(1)}, u32[]{:S(2)}, u32[]{:S(2)}) collective-permute-start(bf16[256,768]{1,0:T(8,128)(2,1)} %get-tuple-element.52), channel_id=1, source_target_pairs={{0,6},{2,4},{4,2},{6,0},{8,14},{10,12},{12,10},{14,8},{16,22},{18,... | collective-permute-start | bytes 1179656 | tf_op jit(solution)/shard_map/ppermute | solution.py:390
  41.3 1.4 copy-start.7
  41.3 19.2 %collective-permute-start.27 = (bf16[512,384]{1,0:T(8,128)(2,1)S(1)}, bf16[512,384]{1,0:T(8,128)(2,1)}, u32[]{:S(2)}, u32[]{:S(2)}) collective-permute-start(bf16[512,384]{1,0:T(8,128)(2,1)S(1)} %constant_dynamic-update-slice_fusion.4.refs_10_), channel_id=1, source_target_pairs={{8,16},{10,18},{12,20},{14,22},{16,8},{18,10},{20,12},{22,14},{9,1... | collective-permute-start | bytes 1179656 | tf_op jit(solution)/shard_map/ppermute | solution.py:396
  42.7 0.8 copy-start.5
  43.4 25.0 %collective-permute-start.17 = (bf16[512,384]{1,0:T(8,128)(2,1)S(1)}, bf16[512,384]{1,0:T(8,128)(2,1)}, u32[]{:S(2)}, u32[]{:S(2)}) collective-permute-start(bf16[512,384]{1,0:T(8,128)(2,1)S(1)} %collective-permute-done.14.refs_11_), channel_id=1, source_target_pairs={{8,16},{10,18},{12,20},{14,22},{16,8},{18,10},{20,12},{22,14},{9,1... | collective-permute-start | bytes 1179656 | tf_op jit(solution)/shard_map/ppermute | solution.py:396
  45.5 17.2 %collective-permute-start.1 = (bf16[256,384]{1,0:T(8,128)(2,1)S(1)}, bf16[256,384]{1,0:T(8,128)(2,1)S(1)}, u32[]{:S(2)}, u32[]{:S(2)}) collective-permute-start(bf16[256,384]{1,0:T(8,128)(2,1)S(1)} %get-tuple-element.42), channel_id=1, source_target_pairs={{0,2},{2,0},{4,6},{6,4},{8,10},{10,8},{12,14},{14,12},{16,18},{18,... | collective-permute-start | bytes 589832 | tf_op jit(solution)/shard_map/ppermute | solution.py:390
  50.5 12.9 %collective-permute-start.2 = (bf16[256,384]{1,0:T(8,128)(2,1)S(1)}, bf16[256,384]{1,0:T(8,128)(2,1)S(1)}, u32[]{:S(2)}, u32[]{:S(2)}) collective-permute-start(bf16[256,384]{1,0:T(8,128)(2,1)S(1)} %get-tuple-element.43), channel_id=1, source_target_pairs={{0,4},{2,6},{4,0},{6,2},{8,12},{10,14},{12,8},{14,10},{16,20},{18,... | collective-permute-start | bytes 589832 | tf_op jit(solution)/shard_map/ppermute | solution.py:390
  59.5 8.3 %collective-permute-start.3 = (bf16[256,384]{1,0:T(8,128)(2,1)S(1)}, bf16[256,384]{1,0:T(8,128)(2,1)S(1)}, u32[]{:S(2)}, u32[]{:S(2)}) collective-permute-start(bf16[256,384]{1,0:T(8,128)(2,1)S(1)} %get-tuple-element.44), channel_id=1, source_target_pairs={{0,6},{2,4},{4,2},{6,0},{8,14},{10,12},{12,10},{14,8},{16,22},{18,... | collective-permute-start | bytes 589832 | tf_op jit(solution)/shard_map/ppermute | solution.py:390
  60.4 1.0 copy-start.8
  60.4 2.3 %copy-start.6 = (bf16[512,384]{1,0:T(8,128)(2,1)S(1)}, bf16[512,384]{1,0:T(8,128)(2,1)}, u32[]{:S(2)}) copy-start(bf16[512,384]{1,0:T(8,128)(2,1)} %copy-done.5) | copy-start | bytes 1179652
  60.4 29.6 %copy-start.9 = (s32[16]{0:T(128)S(1)}, s32[16]{0:T(128)}, u32[]{:S(2)}) copy-start(s32[16]{0:T(128)} %pages.3) | copy-start | bytes 196
  61.4 11.8 %collective-permute-start.16 = (bf16[512,384]{1,0:T(8,128)(2,1)S(1)}, bf16[512,384]{1,0:T(8,128)(2,1)S(1)}, u32[]{:S(2)}, u32[]{:S(2)}) collective-permute-start(bf16[512,384]{1,0:T(8,128)(2,1)S(1)} %copy-done.8), channel_id=1, source_target_pairs={{8,0},{10,2},{12,4},{14,6},{16,24},{18,26},{20,28},{22,30},{9,1},{... | collective-permute-start | bytes 1179656 | tf_op jit(solution)/shard_map/ppermute | solution.py:396
  62.7 11.8 %collective-permute-start.29 = (bf16[512,384]{1,0:T(8,128)(2,1)S(1)}, bf16[512,384]{1,0:T(8,128)(2,1)S(1)}, u32[]{:S(2)}, u32[]{:S(2)}) collective-permute-start(bf16[512,384]{1,0:T(8,128)(2,1)S(1)} %copy-done.6), channel_id=1, source_target_pairs={{8,16},{10,18},{12,20},{14,22},{16,8},{18,10},{20,12},{22,14},{9,1... | collective-permute-start | bytes 1179656 | tf_op jit(solution)/shard_map/ppermute | solution.py:396
  63.4 18.2 %collective-permute-start.9 = (bf16[256,768]{1,0:T(8,128)(2,1)S(1)}, bf16[256,768]{1,0:T(8,128)(2,1)S(1)}, u32[]{:S(2)}, u32[]{:S(2)}) collective-permute-start(bf16[256,768]{1,0:T(8,128)(2,1)S(1)} %select_select_fusion), channel_id=1, source_target_pairs={{0,8},{2,10},{4,12},{6,14},{16,24},{18,26},{20,28},{22,30},{1,9},{... | collective-permute-start | bytes 1179656 | tf_op jit(solution)/shard_map/ppermute | solution.py:396
  67.8 13.8 %collective-permute-start.10 = (bf16[256,768]{1,0:T(8,128)(2,1)S(1)}, bf16[256,768]{1,0:T(8,128)(2,1)S(1)}, u32[]{:S(2)}, u32[]{:S(2)}) collective-permute-start(bf16[256,768]{1,0:T(8,128)(2,1)S(1)} %select_select_fusion), channel_id=1, source_target_pairs={{8,16},{10,18},{12,20},{14,22},{9,17},{11,19},{13,21},{15,23}} | collective-permute-start | bytes 1179656 | tf_op jit(solution)/shard_map/ppermute | solution.py:396
  68.5 21.6 %collective-permute-start.18 = (bf16[512,384]{1,0:T(8,128)(2,1)}, bf16[512,384]{1,0:T(8,128)(2,1)S(1)}, u32[]{:S(2)}, u32[]{:S(2)}) collective-permute-start(bf16[512,384]{1,0:T(8,128)(2,1)} %collective-permute-done.17.refs_14_), channel_id=1, source_target_pairs={{8,0},{10,2},{12,4},{14,6},{16,24},{18,26},{20,28},{22,30},{9,1},{... | collective-permute-start | bytes 1179656 | tf_op jit(solution)/shard_map/ppermute | solution.py:396
  73.2 37.3 %collective-permute-start.28 = (bf16[512,384]{1,0:T(8,128)(2,1)}, bf16[512,384]{1,0:T(8,128)(2,1)S(1)}, u32[]{:S(2)}, u32[]{:S(2)}) collective-permute-start(bf16[512,384]{1,0:T(8,128)(2,1)} %collective-permute-done.27.refs_12_), channel_id=1, source_target_pairs={{8,0},{10,2},{12,4},{14,6},{16,24},{18,26},{20,28},{22,30},{9,1},{... | collective-permute-start | bytes 1179656 | tf_op jit(solution)/shard_map/ppermute | solution.py:396
  74.5 36.0 %collective-permute-start.30 = (bf16[512,384]{1,0:T(8,128)(2,1)S(1)}, bf16[512,384]{1,0:T(8,128)(2,1)S(1)}, u32[]{:S(2)}, u32[]{:S(2)}) collective-permute-start(bf16[512,384]{1,0:T(8,128)(2,1)S(1)} %collective-permute-done.29.refs_14_), channel_id=1, source_target_pairs={{8,0},{10,2},{12,4},{14,6},{16,24},{18,26},{20,28},{22,30},{9,1},{... | collective-permute-start | bytes 1179656 | tf_op jit(solution)/shard_map/ppermute | solution.py:396
  105.9 21.3 %collective-permute-start.19 = (bf16[128,384]{1,0:T(8,128)(2,1)S(1)}, bf16[128,384]{1,0:T(8,128)(2,1)S(1)}, u32[]{:S(2)}, u32[]{:S(2)}) collective-permute-start(bf16[128,384]{1,0:T(8,128)(2,1)S(1)} %get-tuple-element.58), channel_id=1, source_target_pairs={{0,2},{2,0},{4,6},{6,4},{8,10},{10,8},{12,14},{14,12},{16,18},{18,... | collective-permute-start | bytes 294920 | tf_op jit(solution)/shard_map/ppermute | solution.py:390
  108.8 20.1 %collective-permute-start.20 = (bf16[128,384]{1,0:T(8,128)(2,1)S(1)}, bf16[128,384]{1,0:T(8,128)(2,1)S(1)}, u32[]{:S(2)}, u32[]{:S(2)}) collective-permute-start(bf16[128,384]{1,0:T(8,128)(2,1)S(1)} %get-tuple-element.59), channel_id=1, source_target_pairs={{0,4},{2,6},{4,0},{6,2},{8,12},{10,14},{12,8},{14,10},{16,20},{18,... | collective-permute-start | bytes 294920 | tf_op jit(solution)/shard_map/ppermute | solution.py:390
  109.0 19.9 %collective-permute-start.21 = (bf16[128,384]{1,0:T(8,128)(2,1)S(1)}, bf16[128,384]{1,0:T(8,128)(2,1)S(1)}, u32[]{:S(2)}, u32[]{:S(2)}) collective-permute-start(bf16[128,384]{1,0:T(8,128)(2,1)S(1)} %get-tuple-element.60), channel_id=1, source_target_pairs={{0,6},{2,4},{4,2},{6,0},{8,14},{10,12},{12,10},{14,8},{16,22},{18,... | collective-permute-start | bytes 294920 | tf_op jit(solution)/shard_map/ppermute | solution.py:390
  126.7 4.5 %collective-permute-start.31 = (bf16[128,384]{1,0:T(8,128)(2,1)S(1)}, bf16[128,384]{1,0:T(8,128)(2,1)S(1)}, u32[]{:S(2)}, u32[]{:S(2)}) collective-permute-start(bf16[128,384]{1,0:T(8,128)(2,1)S(1)} %get-tuple-element.68), channel_id=1, source_target_pairs={{0,2},{2,0},{4,6},{6,4},{8,10},{10,8},{12,14},{14,12},{16,18},{18,... | collective-permute-start | bytes 294920 | tf_op jit(solution)/shard_map/ppermute | solution.py:390
  126.9 4.3 %collective-permute-start.32 = (bf16[128,384]{1,0:T(8,128)(2,1)S(1)}, bf16[128,384]{1,0:T(8,128)(2,1)S(1)}, u32[]{:S(2)}, u32[]{:S(2)}) collective-permute-start(bf16[128,384]{1,0:T(8,128)(2,1)S(1)} %get-tuple-element.69), channel_id=1, source_target_pairs={{0,4},{2,6},{4,0},{6,2},{8,12},{10,14},{12,8},{14,10},{16,20},{18,... | collective-permute-start | bytes 294920 | tf_op jit(solution)/shard_map/ppermute | solution.py:390
  127.2 6.7 %collective-permute-start.33 = (bf16[128,384]{1,0:T(8,128)(2,1)S(1)}, bf16[128,384]{1,0:T(8,128)(2,1)S(1)}, u32[]{:S(2)}, u32[]{:S(2)}) collective-permute-start(bf16[128,384]{1,0:T(8,128)(2,1)S(1)} %get-tuple-element.70), channel_id=1, source_target_pairs={{0,6},{2,4},{4,2},{6,0},{8,14},{10,12},{12,10},{14,8},{16,22},{18,... | collective-permute-start | bytes 294920 | tf_op jit(solution)/shard_map/ppermute | solution.py:390
  129.9 6.6 %collective-permute-start.22 = (bf16[128,768]{1,0:T(8,128)(2,1)S(1)}, bf16[128,768]{1,0:T(8,128)(2,1)S(1)}, u32[]{:S(2)}, u32[]{:S(2)}) collective-permute-start(bf16[128,768]{1,0:T(8,128)(2,1)S(1)} %get-tuple-element.62), channel_id=1, source_target_pairs={{0,1},{1,0},{2,3},{3,2},{4,5},{5,4},{6,7},{7,6},{8,9},{9,8},{10,11... | collective-permute-start | bytes 589832 | tf_op jit(solution)/shard_map/ppermute | solution.py:390
  134.9 6.9 %collective-permute-start.34 = (bf16[128,768]{1,0:T(8,128)(2,1)S(1)}, bf16[128,768]{1,0:T(8,128)(2,1)S(1)}, u32[]{:S(2)}, u32[]{:S(2)}) collective-permute-start(bf16[128,768]{1,0:T(8,128)(2,1)S(1)} %get-tuple-element.72), channel_id=1, source_target_pairs={{0,1},{1,0},{2,3},{3,2},{4,5},{5,4},{6,7},{7,6},{8,9},{9,8},{10,11... | collective-permute-start | bytes 589832 | tf_op jit(solution)/shard_map/ppermute | solution.py:390

commit v2 on v1

v2 whole, which is shorter than its diff:
```python
import functools

import jax
import jax.numpy as jnp
from jax import lax
from jax.experimental import pallas as pl
from jax.experimental.pallas import tpu as pltpu
from jax.sharding import PartitionSpec as P

HD = 96
ROT = 24
SLAB = 4
LOG2E = 1.4426950408889634
VMEM = pl.BlockSpec(memory_space=pltpu.VMEM)
SMEM = pl.BlockSpec(memory_space=pltpu.SMEM)


def params(mib):
    return pltpu.CompilerParams(vmem_limit_bytes=mib << 20)


def shape(rows, lanes):
    return jax.ShapeDtypeStruct((rows, lanes), jnp.bfloat16)


def cost(flops, moved, exps=0):
    return pl.CostEstimate(flops=1, bytes_accessed=1, transcendentals=0)


def starts_and_groups(rows, table):
    starts, ends, groups = table[0:1], table[1:2], table[2:3]
    start = jnp.max(jnp.where(ends <= rows, ends, 0.0), axis=1, keepdims=True)
    inside = (starts <= rows) & (rows < ends)
    group = jnp.sum(jnp.where(inside, groups, 0.0), axis=1, keepdims=True)
    return start, group


def lanes_at(ref, index, each, count, *lead):
    if each % 128 == 0:
        return ref[(*lead, slice(None), pl.ds(pl.multiple_of(index * each, each), each))]
    x = ref[(*lead, slice(None), slice(0, each))]
    for i in range(1, count):
        x = jnp.where(index == i, ref[(*lead, slice(None), slice(i * each, (i + 1) * each))], x)
    return x


def page_kernel(chunks, place, keys, values, *outs):
    lanes = keys.shape[-1] // SLAB
    half = lanes // chunks
    for n in range(SLAB):
        k = lanes_at(keys, place[1] ^ n, lanes, SLAB, 0)
        v = lanes_at(values, place[1] ^ n, lanes, SLAB, 0)
        for c in range(chunks):
            cut = slice(c * half, (c + 1) * half)
            pair = [k[:, cut], v[:, cut]]
            outs[c * SLAB + n][...] = jnp.concatenate(pair[::-1] if c else pair, axis=1)


def cut_page(place, keys, values, chunks):
    lanes = keys.shape[-1] // SLAB // chunks * 2
    outs = pl.pallas_call(
        functools.partial(page_kernel, chunks),
        out_shape=[shape(keys.shape[1], lanes)] * (SLAB * chunks),
        in_specs=[SMEM, VMEM, VMEM],
        out_specs=[VMEM] * (SLAB * chunks),
        compiler_params=params(16),
        cost_estimate=cost(0, 4 * keys.size),
    )(place, keys, values)
    return [outs[c * SLAB : (c + 1) * SLAB] for c in range(chunks)]


def rotate_kernel(tp, chunks, prefix, place, table, freq, queries, keys, values, *outs):
    rows, lanes = queries.shape[0], queries.shape[1] // tp
    width = freq.shape[1]
    token = place[2] + lax.broadcasted_iota(jnp.int32, (rows, 1), 0)
    token = token.astype(jnp.float32)
    start, _ = starts_and_groups(token, table[...])
    angle = (prefix + token - start) * freq[...]
    dim = lax.rem(lax.broadcasted_iota(jnp.int32, (rows, width), 1), HD)
    cosine, sine = jnp.cos(angle), jnp.sin(angle)
    keep = jnp.where(dim < ROT, cosine, 1.0)
    after = jnp.where(dim < ROT // 2, -sine, 0.0)
    before = jnp.where((dim >= ROT // 2) & (dim < ROT), sine, 0.0)
    cut = width // chunks

    def turned(x):
        x = x.astype(jnp.float32)
        far = pltpu.roll(x, width - ROT // 2, 1)
        near = pltpu.roll(x, ROT // 2, 1)
        return (x * keep + far * after + near * before).astype(jnp.bfloat16)

    for m in range(tp):
        base = (place[3] ^ m) * lanes
        for part in range(lanes // width):
            at = pl.ds(pl.multiple_of(base + part * width, width), width)
            q, k, v = turned(queries[:, at]), turned(keys[:, at]), values[:, at]
            quarters = lanes // width == 1 and SLAB or 1
            for i in range(quarters):
                for c in range(chunks):
                    size = cut // quarters
                    of = slice(c * cut + i * size, c * cut + (i + 1) * size)
                    to = slice((part + i) * 2 * size, (part + i + 1) * 2 * size)
                    pair = [k[:, of], v[:, of]]
                    out = outs[c * tp + m]
                    out[:rows, to] = jnp.concatenate(pair[::-1] if c else pair, axis=1)
                    out[rows:, to] = jnp.concatenate([q[: rows // 2, of], q[rows // 2 :, of]], axis=1)


def rotate_and_cut(place, table, freq, queries, keys, values, tp, chunks, prefix):
    rows, lanes = queries.shape[0], queries.shape[1] // tp
    outs = pl.pallas_call(
        functools.partial(rotate_kernel, tp, chunks, prefix),
        out_shape=[shape(rows * 3 // 2, 2 * lanes // chunks)] * (chunks * tp),
        in_specs=[SMEM] + [VMEM] * 5,
        out_specs=[VMEM] * (chunks * tp),
        compiler_params=params(24),
        cost_estimate=cost(0, 12 * queries.size),
    )(place, table, freq, queries, keys, values)
    return [outs[c * tp : (c + 1) * tp] for c in range(chunks)]


def quarter_kernel(tp, place, *refs):
    parts, outs = refs[:tp], refs[tp:]
    rows, each = parts[0].shape[0] * 2 // 3, outs[0].shape[1]
    for n in range(SLAB):
        for m in range(tp):
            x = lanes_at(parts[m], place[1] ^ n, each, SLAB)
            to = pl.multiple_of((place[3] ^ m) * rows, rows)
            outs[n][pl.ds(to, rows), :] = x[:rows]
            to = pl.multiple_of(tp * rows + (place[3] ^ m) * (rows // 2), rows // 2)
            outs[n][pl.ds(to, rows // 2), :] = x[rows:]


def cut_quarters(place, parts):
    tp = len(parts)
    rows, lanes = parts[0].shape
    return pl.pallas_call(
        functools.partial(quarter_kernel, tp),
        out_shape=[shape(rows * tp, lanes // SLAB)] * SLAB,
        in_specs=[SMEM] + [VMEM] * tp,
        out_specs=[VMEM] * SLAB,
        compiler_params=params(24),
        cost_estimate=cost(0, 4 * tp * parts[0].size),
    )(place, *parts)


def output_kernel(tp, chunks, place, *refs):
    parts, outs = refs[: chunks * tp], refs[chunks * tp :]
    rows, lanes = outs[0].shape[0] // tp, outs[0].shape[1]
    each = lanes // chunks // SLAB
    for m in range(tp):
        to = pl.ds(pl.multiple_of((place[3] ^ m) * rows, rows), rows)
        for section, out in enumerate(outs):
            pieces = []
            for i in range(SLAB):
                for c in range(chunks):
                    at = 2 * i * each + (each if section != c else 0)
                    pieces.append(parts[c * tp + m][:rows, at : at + each])
            out[to, :] = jnp.concatenate(pieces, axis=1)


def join_outputs(place, parts, lanes):
    chunks, tp = len(parts), len(parts[0])
    rows = parts[0][0].shape[0] * 2 // 3
    return pl.pallas_call(
        functools.partial(output_kernel, tp, chunks),
        out_shape=[shape(rows * tp, lanes)] * 2,
        in_specs=[SMEM] + [VMEM] * (tp * chunks),
        out_specs=[VMEM] * 2,
        compiler_params=params(24),
        cost_estimate=cost(0, 8 * rows * tp * lanes),
    )(place, *[x for chunk in parts for x in chunk])


def stack_kernel(*refs):
    rows = refs[0].shape[0]
    for n, ref in enumerate(refs[:-1]):
        refs[-1][n * rows : (n + 1) * rows, :] = ref[...]


def stacked(parts):
    rows, lanes = parts[0].shape
    return pl.pallas_call(
        stack_kernel,
        out_shape=shape(rows * len(parts), lanes),
        in_specs=[VMEM] * len(parts),
        out_specs=VMEM,
        compiler_params=params(16),
        cost_estimate=cost(0, 4 * len(parts) * parts[0].size),
    )(*parts)


def last_kernel(place, *refs):
    out = refs[-1]
    for n in range(SLAB):

        @pl.when((place[1] ^ n) == SLAB - 1)
        def _():
            out[...] = refs[n][: out.shape[0], :]


def last_of(place, parts, block):
    return pl.pallas_call(
        last_kernel,
        out_shape=shape(block, parts[0].shape[1]),
        in_specs=[SMEM] + [VMEM] * SLAB,
        out_specs=VMEM,
        compiler_params=params(16),
        cost_estimate=cost(0, 4 * block * parts[0].shape[1]),
    )(place, *parts)


def window(lane, count, lanes):
    return lane // 128 * 128, min(-(-(lane + count) // 128) * 128, lanes)


def set_in(x, offset, lanes):
    rows, count = x.shape
    parts = [x]
    if offset:
        parts.insert(0, jnp.zeros((rows, offset), x.dtype))
    if lanes > offset + count:
        parts.append(jnp.zeros((rows, lanes - offset - count), x.dtype))
    return jnp.concatenate(parts, axis=1) if len(parts) > 1 else x


def attend_kernel(plan, place, pages, table, *refs):
    chunk, heads, lines, early_count, unit_count, page, block, rows = plan
    parts = refs[:SLAB]
    early = refs[SLAB : SLAB + early_count]
    units = refs[SLAB + early_count : SLAB + early_count + unit_count]
    refs = refs[SLAB + early_count + unit_count :]
    outs, (near_keys, near_values, pool, seat) = refs[:SLAB], refs[SLAB:]
    z, j = place[0], place[1]
    slots = lines * SLAB
    middle = (z > 0) & (z < lines - 1)

    half = slots // 2 * page
    width = heads * HD
    key_lane = width if chunk else 0
    value_lane = width - key_lane
    key_low, key_high = window(key_lane, width, 2 * width)
    low, high = window(value_lane, width, 2 * width)
    key_at, value_at = slice(key_low, key_high), slice(low, high)
    factor = HD ** (-0.5) * LOG2E
    contract = (((1,), (1,)), ((), ()))
    first = z * (SLAB * block)

    def dot_t(x, y):
        return lax.dot_general(x, y, contract, preferred_element_type=jnp.float32)

    def dot(x, y):
        return jnp.dot(x, y, preferred_element_type=jnp.float32)

    def fill(i, carry):
        seat[pages[i]] = i
        return carry

    lax.fori_loop(0, slots, fill, 0)

    def set_near(source, at):
        near_keys[pl.ds(at, block), :] = source[:block, key_at]
        near_values[pl.ds(at, block), :] = source[:block, value_at]

    def set_pool(source, line, base):
        for n in range(SLAB):
            to = pl.multiple_of(seat[line * SLAB + (j ^ n)] * page, page)
            pool[pl.ds(to, page), :] = source[base + n * page : base + (n + 1) * page, :]

    for n in range(SLAB):
        set_near(parts[n], pl.multiple_of(((j ^ n) + 1) * block, block))
    if early_count == 2:
        pl.when(z == 2)(lambda: set_near(early[1], 0))
        pl.when(z != 2)(lambda: set_near(early[0], 0))
    else:
        set_near(early[0], 0)
    if unit_count == 6:
        own, a1, b1, a2, b2, a3 = units
        set_pool(own, z, 0)
        set_pool(a1, z ^ 1, 0)
        third, fourth = jnp.where(z < 2, 2, 1), jnp.where(z < 2, 3, 0)

        @pl.when(middle)
        def _():
            set_pool(b1, third, 0)
            set_pool(b2, fourth, 0)

        @pl.when(jnp.logical_not(middle))
        def _():
            set_pool(a2, third, 0)
            set_pool(a3, fourth, 0)
    else:
        for line in range(lines):
            set_pool(units[0], line, line * SLAB * page)

    for n in range(SLAB):
        b = j ^ n
        token = first + b * block + lax.broadcasted_iota(jnp.int32, (block, 1), 0)
        request_start, group = starts_and_groups(token.astype(jnp.float32), table[...])
        zero_group = group < 0.5
        key = first + (b - 1) * block + lax.broadcasted_iota(jnp.int32, (block, 2 * block), 1)
        near = (key >= request_start.astype(jnp.int32)) & (key <= token)
        near_rows = pl.ds(pl.multiple_of(b * block, block), 2 * block)
        folded = parts[n][block:, :]
        halves = []
        for at in range(0, block // 2, rows // 2):
            some = folded[at : at + rows // 2]
            halves += [some[:, :width], some[:, width:]]
        queries = jnp.concatenate(halves, axis=0)
        queries = set_in(queries, key_lane - key_low, key_high - key_low)
        lane = key_low + lax.broadcasted_iota(jnp.int32, queries.shape, 1)
        out_lane = low + lax.broadcasted_iota(jnp.int32, (block, high - low), 1)
        result = jnp.zeros((block, high - low), jnp.float32)
        for h in range(heads):
            begin = key_lane + h * HD
            query = jnp.where((lane >= begin) & (lane < begin + HD), queries, jnp.zeros_like(queries))
            score = jnp.where(
                zero_group,
                dot_t(query, pool[0:half, key_at]),
                dot_t(query, pool[half : 2 * half, key_at]),
            )
            near_score = jnp.where(near, dot_t(query, near_keys[near_rows, :]), -1e30)
            top = jnp.maximum(
                jnp.max(score, axis=1, keepdims=True), jnp.max(near_score, axis=1, keepdims=True)
            )
            weight = jnp.exp2((score - top) * factor)
            near_weight = jnp.exp2((near_score - top) * factor)
            total = jnp.sum(weight, axis=1, keepdims=True) + jnp.sum(
                near_weight, axis=1, keepdims=True
            )
            narrow = weight.astype(jnp.bfloat16)
            nothing = jnp.zeros_like(narrow)
            mixed = (
                dot(jnp.where(zero_group, narrow, nothing), pool[0:half, value_at])
                + dot(jnp.where(zero_group, nothing, narrow), pool[half : 2 * half, value_at])
                + dot(near_weight.astype(jnp.bfloat16), near_values[near_rows, :])
            )
            begin = value_lane + h * HD
            inside = (out_lane >= begin) & (out_lane < begin + HD)
            result = jnp.where(inside, mixed / total, result)
        result = result[:, value_lane - low : value_lane - low + width].astype(jnp.bfloat16)
        folded = jnp.concatenate([result[: block // 2], result[block // 2 :]], axis=1)
        outs[n][...] = folded


def attend(place, pages, table, parts, early, units, chunk, lines, page, rows):
    block, width = parts[0].shape[0] * 2 // 3, parts[0].shape[1] // 2
    heads = width // HD
    slots = lines * SLAB
    key_low, key_high = window(width if chunk else 0, width, 2 * width)
    low, high = window(0 if chunk else width, width, 2 * width)
    plan = (chunk, heads, lines, len(early), len(units), page, block, rows)
    keys = slots * page + 2 * block
    return pl.pallas_call(
        functools.partial(attend_kernel, plan),
        out_shape=[shape(block // 2, 2 * width)] * SLAB,
        in_specs=[SMEM, SMEM, VMEM] + [VMEM] * (SLAB + len(early) + len(units)),
        out_specs=[VMEM] * SLAB,
        scratch_shapes=[
            pltpu.VMEM(((SLAB + 1) * block, key_high - key_low), jnp.bfloat16),
            pltpu.VMEM(((SLAB + 1) * block, high - low), jnp.bfloat16),
            pltpu.VMEM((slots * page, 2 * width), jnp.bfloat16),
            pltpu.SMEM((slots,), jnp.int32),
        ],
        compiler_params=params(32),
        cost_estimate=cost(
            4 * SLAB * block * keys * heads * 256,
            4 * keys * width,
            SLAB * block * heads * (keys // 2),
        ),
    )(place, pages, table, *parts, *early, *units)


def back_kernel(tp, place, *refs):
    parts, outs = refs[:SLAB], refs[SLAB:]
    rows, lanes = parts[0].shape
    each = 2 * rows // tp
    for m in range(tp):
        first = (place[3] ^ m) * each
        upper = first >= rows
        at = pl.ds(pl.multiple_of(jnp.where(upper, first - rows, first), each), each)
        cuts = []
        for n in range(SLAB):
            x = parts[n][at, :]
            cuts.append(jnp.where(upper, x[:, lanes // 2 :], x[:, : lanes // 2]))
        outs[m][...] = jnp.concatenate(cuts, axis=1)


def cut_back(place, parts, tp):
    rows, lanes = parts[0].shape
    return pl.pallas_call(
        functools.partial(back_kernel, tp),
        out_shape=[shape(2 * rows // tp, lanes // 2 * SLAB)] * tp,
        in_specs=[SMEM] + [VMEM] * SLAB,
        out_specs=[VMEM] * tp,
        compiler_params=params(16),
        cost_estimate=cost(0, 4 * SLAB * rows * lanes),
    )(place, *parts)


def join_kernel(tp, chunks, place, *refs):
    out = refs[-1]
    lanes = out.shape[1] // tp
    each = lanes // SLAB
    cut = each // chunks
    for m in range(tp):
        for n in range(SLAB):
            base = (place[3] ^ m) * lanes + (place[1] ^ n) * each
            pieces = [refs[c * tp + m][:, n * cut : (n + 1) * cut] for c in range(chunks)]
            x = jnp.concatenate(pieces, axis=1) if chunks > 1 else pieces[0]
            if each % 128:
                for i in range(tp * SLAB):

                    @pl.when(base == i * each)
                    def _():
                        out[:, i * each : (i + 1) * each] = x
            else:
                out[:, pl.ds(pl.multiple_of(base, each), each)] = x


def join(place, parts, tp, chunks):
    rows, lanes = parts[0][0].shape
    return pl.pallas_call(
        functools.partial(join_kernel, tp, chunks),
        out_shape=shape(rows, lanes * tp * chunks),
        in_specs=[SMEM] + [VMEM] * (tp * chunks),
        out_specs=VMEM,
        compiler_params=params(16),
        cost_estimate=cost(0, 4 * rows * lanes * tp * chunks),
    )(place, *[x for chunk in parts for x in chunk])


def swap(parts, axis):
    size = lax.axis_size(axis)
    return [parts[0]] + [
        lax.ppermute(parts[m], axis, [(i, i ^ m) for i in range(size)])
        for m in range(1, len(parts))
    ]


def along(block, pairs):
    return lax.ppermute(
        block, "seq", [(a * SLAB + j, b * SLAB + j) for a, b in pairs for j in range(SLAB)]
    )


INNER = [(1, 2), (2, 1)]
OUTER = [(0, 1), (1, 0), (2, 3), (3, 2)]
OUTWARD = [(1, 0), (2, 3)]


def gather(unit, lines):
    if lines == 4:
        a1 = along(unit, OUTER)
        b1 = along(unit, INNER)
        b2 = along(a1, INNER)
        a2 = along(b1, OUTWARD)
        a3 = along(b2, OUTWARD)
        return [unit, a1, b1, a2, b2, a3]
    groups = [[line * SLAB + j for line in range(lines)] for j in range(SLAB)]
    return [lax.all_gather(unit, "seq", axis=0, axis_index_groups=groups, tiled=True)]


def local(queries, keys, values, pool_keys, pool_values, page_table, lengths, group_of):
    seq, tp = lax.axis_size("seq"), lax.axis_size("tp")
    lines = seq // SLAB
    rows = queries.shape[0]
    page = pool_keys.shape[1]
    own_heads = pool_keys.shape[2] // SLAB // HD
    chunks = 2 if own_heads % 2 == 0 else 1
    index, y = lax.axis_index("seq"), lax.axis_index("tp")
    j = index % SLAB
    place = jnp.stack([index // SLAB, j, (index * tp + y) * rows, y]).astype(jnp.int32)
    ends = jnp.cumsum(lengths)
    table = jnp.stack([ends - lengths, ends, group_of]).astype(jnp.float32)
    width = pool_keys.shape[2] // SLAB
    if width % 128:
        width = pool_keys.shape[2]
    dims = (jnp.arange(width) % HD) % (ROT // 2)
    freq = (10000.0 ** (-(dims.astype(jnp.float32) * 2.0 / ROT)))[None]
    prefix = seq // 2 * page

    after = lax.optimization_barrier
    after = lax.optimization_barrier
    after = lax.optimization_barrier
    pieces = cut_page(place, pool_keys, pool_values, chunks)
    units, tokens = [], None
    for c in range(chunks):
        if c:
            pieces[c], units[0] = after((pieces[c], units[0]))
        swapped = swap(pieces[c], "seq")
        if not c:
            swapped[1], turn_table = after((swapped[1], table))
            tokens = rotate_and_cut(
                place, turn_table, freq, queries, keys, values, tp, chunks, prefix
            )
            swapped, tokens = after((swapped, tokens))
        units.append(stacked(swapped))
    gathered = [gather(unit, lines) for unit in units]
    cuts = []
    for c in range(chunks):
        if c:
            tokens[c], tokens[c - 1] = after((tokens[c], tokens[c - 1]))
        tokens[c] = swap(tokens[c], "tp")
        cuts.append(cut_quarters(place, tokens[c]))
    new_keys, new_values = join_outputs(place, tokens, pool_keys.shape[2])
    backs = []
    for c in range(chunks):
        parts = swap(cuts[c], "seq")
        block = parts[0].shape[0] * 2 // 3
        last = last_of(place, parts, block)
        if c + 1 < chunks:
            last, cuts[c + 1] = after((last, cuts[c + 1]))
        if lines == 4:
            early = [along(last, [(0, 1), (2, 3)]), along(last, [(1, 2)])]
        else:
            early = [along(last, [(i, i + 1) for i in range(lines - 1)])]
        if c:
            backs[-1], parts = after((backs[-1], parts))
        outs = attend(place, page_table, table, parts, early, gathered[c], c, lines, page, rows)
        backs.append(cut_back(place, swap(outs, "seq"), tp))
    backs = [swap(back, "tp") for back in backs]
    return join(place, backs, tp, chunks), new_keys, new_values


def solution(mesh):
    return jax.shard_map(
        local,
        mesh=mesh,
        in_specs=(
            P(("seq", "tp"), None),
            P(("seq", "tp"), None),
            P(("seq", "tp"), None),
            P("seq", None, "tp"),
            P("seq", None, "tp"),
            P(),
            P(),
            P(),
        ),
        out_specs=(P(("seq", "tp"), None), P("seq", "tp"), P("seq", "tp")),
        check_vma=False,
    )
```

time: 144 us -> 117 us (0.81); the launches traced: 143 us -> 114 us
  waiting for transfers between devices: 53.7 us -> 38.5 us
  Pallas kernels: 42.4 us -> 29.4 us
    pallas_call x2, Pallas kernels: 32.1 us -> 17.2 us  [attend(): pl.pallas_call(functools.partial(attend_kernel, plan), out_shape=[shape(b...]
    ppermute x12 -> x14, waiting for transfers between devices: 17.7 us -> 8.98 us  [along(): lax.ppermute(block, 'seq', [(a * SLAB + j, b * SLAB + j) for a, b in pair...]
    ppermute x23 -> x22, waiting for transfers between devices: 36.1 us -> 29.6 us  [swap(): lax.ppermute(parts[m], axis, [(i, i ^ m) for i in range(size)])]
    pallas_call x3 -> x8, Pallas kernels: 5.91 us -> 7.79 us  [the longest x1 3.16 us: rotate_and_cut(): pl.pallas_call(functools.partial(rotate_kernel, tp, chunks, prefix), out_...]
    unnamed x30 -> x16, local copies, waits for them, and re-layouts: 6.47 us -> 5.15 us
    ppermute x23 -> x22, starting transfers between devices: 26.3 us -> 26.6 us  [swap(): lax.ppermute(parts[m], axis, [(i, i ^ m) for i in range(size)])]
    ppermute x12 -> x14, starting transfers between devices: 13.1 us -> 13.4 us  [along(): lax.ppermute(block, 'seq', [(a * SLAB + j, b * SLAB + j) for a, b in pair...]
  transfers between devices with their start and end apart: 35 -> 36, of which waited for: 14 -> 15; matrix products, arithmetic and copies ran while one was open for 0% -> 0% of each run, Pallas kernels for 26% -> 16%
where the time goes in v2:
time: 117 us; the launch traced here: 114 us
  starting transfers between devices  40 us (34%)
  waiting for transfers between devices  38.5 us (33%)
  Pallas kernels  29.4 us (25%)
  local copies, waits for them, and re-layouts  5.23 us (4%)
    ppermute x22, waiting for transfers between devices, swap(): lax.ppermute(parts[m], axis, [(i, i ^ m) for i in range(size)])  29.6 us
    ppermute x22, starting transfers between devices, swap(): lax.ppermute(parts[m], axis, [(i, i ^ m) for i in range(size)])  26.6 us
    pallas_call x2, Pallas kernels, attend(): pl.pallas_call(functools.partial(attend_kernel, plan), out_shape=[shape(b...  17.2 us
    ppermute x14, starting transfers between devices, along(): lax.ppermute(block, 'seq', [(a * SLAB + j, b * SLAB + j) for a, b in pair...  13.4 us
    ppermute x14, waiting for transfers between devices, along(): lax.ppermute(block, 'seq', [(a * SLAB + j, b * SLAB + j) for a, b in pair...  8.98 us
    unnamed x16, local copies, waits for them, and re-layouts  5.15 us
    pallas_call x1, Pallas kernels, rotate_and_cut(): pl.pallas_call(functools.partial(rotate_kernel, tp, chunks, prefix), out_...  3.16 us
  transfers between devices with their start and end apart: 36, of which 15 were waited for; matrix products, arithmetic and copies ran while one was open for 0% of the time, Pallas kernels for 16%

profile of v2, /device:TPU:25, one launch (start us, length us, event | category | flops | bytes accessed | tf_op | source)
XLA Modules:
  0.0 114.5 jit_solution(15230005337018666458)
XLA Ops:
  0.7 1.1 copy-done.3
  1.8 1.0 copy-done.4
  2.8 0.7 shard_map.103
  3.5 0.7 collective-permute-start
  4.3 1.2 %collective-permute-start.1 = (bf16[128,384]{1,0:T(8,128)(2,1)S(1)}, bf16[128,384]{1,0:T(8,128)(2,1)S(1)}, u32[]{:S(2)}, u32[]{:S(2)}) collective-permute-start(bf16[128,384]{1,0:T(8,128)(2,1)S(1)} %get-tuple-element.70), channel_id=1, source_target_pairs={{0,4},{2,6},{4,0},{6,2},{8,12},{10,14},{12,8},{14,10},{16,20},{18,... | collective-permute-start | bytes 294920 | tf_op jit(solution)/shard_map/ppermute | solution.py:436
  7.1 1.1 copy-done.1
  8.3 1.1 copy-done.2
  9.4 3.2 %shard_map.104 = (bf16[192,1536]{1,0:T(8,128)(2,1)S(1)}, bf16[192,1536]{1,0:T(8,128)(2,1)S(1)}, bf16[192,1536]{1,0:T(8,128)(2,1)S(1)}, bf16[192,1536]{1,0:T(8,128)(2,1)S(1)}) custom-call(s32[4]{0:T(128)S(1)} %pad_add_fusion.place, f32[3,32]{1,0:T(4,128)S(1)} %add_convert_fusion.table, f32[1,384]{1,0:T(1,128)S(1)} %fusion.4.freq, ...), custom_call_target="tpu_custom_call" | custom-call | flops 1 | bytes 1 | tf_op jit(solution)/shard_map/pallas_call | solution.py:111
  12.6 1.3 %collective-permute-start.3 = (bf16[192,1536]{1,0:T(8,128)(2,1)S(1)}, bf16[192,1536]{1,0:T(8,128)(2,1)S(1)}, u32[]{:S(2)}, u32[]{:S(2)}) collective-permute-start(bf16[192,1536]{1,0:T(8,128)(2,1)S(1)} %get-tuple-element.78), channel_id=1, source_target_pairs={{0,1},{1,0},{2,3},{3,2},{4,5},{5,4},{6,7},{7,6},{8,9},{9,8},{10,11... | collective-permute-start | bytes 1769480 | tf_op jit(solution)/shard_map/ppermute | solution.py:436
  14.2 0.9 collective-permute-start.24
  15.1 0.9 collective-permute-start.25
  15.9 0.8 collective-permute-start.26
  17.4 2.1 %collective-permute-done.25.refs_2_ = bf16[128,384]{1,0:T(8,128)(2,1)S(1)} collective-permute-done((bf16[128,384]{1,0:T(8,128)(2,1)S(1)}, bf16[128,384]{1,0:T(8,128)(2,1)S(1)}, u32[]{:S(2)}, u32[]{:S(2)}) %collective-permute-start.25) | collective-permute-done | bytes 98336 | tf_op jit(solution)/shard_map/ppermute | solution.py:436
  19.5 2.5 %collective-permute-done.26.refs_3_ = bf16[128,384]{1,0:T(8,128)(2,1)S(1)} collective-permute-done((bf16[128,384]{1,0:T(8,128)(2,1)S(1)}, bf16[128,384]{1,0:T(8,128)(2,1)S(1)}, u32[]{:S(2)}, u32[]{:S(2)}) %collective-permute-start.26) | collective-permute-done | bytes 98336 | tf_op jit(solution)/shard_map/ppermute | solution.py:436
  22.0 1.4 %collective-permute-start.27 = (bf16[512,384]{1,0:T(8,128)(2,1)S(1)}, bf16[512,384]{1,0:T(8,128)(2,1)S(1)}, u32[]{:S(2)}, u32[]{:S(2)}) collective-permute-start(bf16[512,384]{1,0:T(8,128)(2,1)S(1)} %shard_map.112.refs_6_), channel_id=1, source_target_pairs={{0,8},{2,10},{4,12},{6,14},{8,0},{10,2},{12,4},{14,6},{16,24},{18,... | collective-permute-start | bytes 1179656 | tf_op jit(solution)/shard_map/ppermute | solution.py:442
  24.7 2.5 %collective-permute-done.3.refs_1_ = bf16[192,1536]{1,0:T(8,128)(2,1)S(1)} collective-permute-done((bf16[192,1536]{1,0:T(8,128)(2,1)S(1)}, bf16[192,1536]{1,0:T(8,128)(2,1)S(1)}, u32[]{:S(2)}, u32[]{:S(2)}) %collective-permute-start.3) | collective-permute-done | bytes 589856 | tf_op jit(solution)/shard_map/ppermute | solution.py:436
  27.9 1.2 %collective-permute-start.4 = (bf16[384,384]{1,0:T(8,128)(2,1)S(1)}, bf16[384,384]{1,0:T(8,128)(2,1)S(1)}, u32[]{:S(2)}, u32[]{:S(2)}) collective-permute-start(bf16[384,384]{1,0:T(8,128)(2,1)S(1)} %get-tuple-element.80), channel_id=1, source_target_pairs={{0,2},{2,0},{4,6},{6,4},{8,10},{10,8},{12,14},{14,12},{16,18},{18,... | collective-permute-start | bytes 884744 | tf_op jit(solution)/shard_map/ppermute | solution.py:436
  29.1 1.3 %collective-permute-start.7 = (bf16[192,1536]{1,0:T(8,128)(2,1)S(1)}, bf16[192,1536]{1,0:T(8,128)(2,1)S(1)}, u32[]{:S(2)}, u32[]{:S(2)}) collective-permute-start(bf16[192,1536]{1,0:T(8,128)(2,1)S(1)} %get-tuple-element.86), channel_id=1, source_target_pairs={{0,1},{1,0},{2,3},{3,2},{4,5},{5,4},{6,7},{7,6},{8,9},{9,8},{10,11... | collective-permute-start | bytes 1769480 | tf_op jit(solution)/shard_map/ppermute | solution.py:436
  30.4 1.0 collective-permute-start.5
  31.4 1.9 %collective-permute-done.27.refs_7_ = bf16[512,384]{1,0:T(8,128)(2,1)S(1)} collective-permute-done((bf16[512,384]{1,0:T(8,128)(2,1)S(1)}, bf16[512,384]{1,0:T(8,128)(2,1)S(1)}, u32[]{:S(2)}, u32[]{:S(2)}) %collective-permute-start.27) | collective-permute-done | bytes 393248 | tf_op jit(solution)/shard_map/ppermute | solution.py:442
  33.3 1.6 %collective-permute-start.6 = (bf16[384,384]{1,0:T(8,128)(2,1)S(1)}, bf16[384,384]{1,0:T(8,128)(2,1)S(1)}, u32[]{:S(2)}, u32[]{:S(2)}) collective-permute-start(bf16[384,384]{1,0:T(8,128)(2,1)S(1)} %get-tuple-element.82), channel_id=1, source_target_pairs={{0,6},{2,4},{4,2},{6,0},{8,14},{10,12},{12,10},{14,8},{16,22},{18,... | collective-permute-start | bytes 884744 | tf_op jit(solution)/shard_map/ppermute | solution.py:436
  35.6 1.3 %collective-permute-start.12 = (bf16[512,384]{1,0:T(8,128)(2,1)S(1)}, bf16[512,384]{1,0:T(8,128)(2,1)S(1)}, u32[]{:S(2)}, u32[]{:S(2)}) collective-permute-start(bf16[512,384]{1,0:T(8,128)(2,1)S(1)} %collective-permute-done.11.refs_8_), channel_id=1, source_target_pairs={{8,0},{10,2},{12,4},{14,6},{16,24},{18,26},{20,28},{22,30},{9,1},{... | collective-permute-start | bytes 1179656 | tf_op jit(solution)/shard_map/ppermute | solution.py:442
  36.9 1.7 %collective-permute-done.5.refs_2_ = bf16[384,384]{1,0:T(8,128)(2,1)S(1)} collective-permute-done((bf16[384,384]{1,0:T(8,128)(2,1)S(1)}, bf16[384,384]{1,0:T(8,128)(2,1)S(1)}, u32[]{:S(2)}, u32[]{:S(2)}) %collective-permute-start.5) | collective-permute-done | bytes 294944 | tf_op jit(solution)/shard_map/ppermute | solution.py:436
  39.3 6.4 %collective-permute-done.6.refs_3_ = bf16[384,384]{1,0:T(8,128)(2,1)S(1)} collective-permute-done((bf16[384,384]{1,0:T(8,128)(2,1)S(1)}, bf16[384,384]{1,0:T(8,128)(2,1)S(1)}, u32[]{:S(2)}, u32[]{:S(2)}) %collective-permute-start.6) | collective-permute-done | bytes 294944 | tf_op jit(solution)/shard_map/ppermute | solution.py:436
  45.7 1.3 %collective-permute-start.14 = (bf16[512,384]{1,0:T(8,128)(2,1)S(1)}, bf16[512,384]{1,0:T(8,128)(2,1)S(1)}, u32[]{:S(2)}, u32[]{:S(2)}) collective-permute-start(bf16[512,384]{1,0:T(8,128)(2,1)S(1)} %collective-permute-done.13.refs_10_), channel_id=1, source_target_pairs={{8,0},{10,2},{12,4},{14,6},{16,24},{18,26},{20,28},{22,30},{9,1},{... | collective-permute-start | bytes 1179656 | tf_op jit(solution)/shard_map/ppermute | solution.py:442
  48.3 1.3 %collective-permute-start.8 = (bf16[256,384]{1,0:T(8,128)(2,1)S(1)}, bf16[256,384]{1,0:T(8,128)(2,1)S(1)}, u32[]{:S(2)}, u32[]{:S(2)}) collective-permute-start(bf16[256,384]{1,0:T(8,128)(2,1)S(1)} %shard_map.106), channel_id=1, source_target_pairs={{0,8},{2,10},{4,12},{6,14},{16,24},{18,26},{20,28},{22,30},{1,9},{... | collective-permute-start | bytes 589832 | tf_op jit(solution)/shard_map/ppermute | solution.py:442
  50.8 2.8 %collective-permute-start.18 = (bf16[384,384]{1,0:T(8,128)(2,1)S(1)}, bf16[384,384]{1,0:T(8,128)(2,1)S(1)}, u32[]{:S(2)}, u32[]{:S(2)}) collective-permute-start(bf16[384,384]{1,0:T(8,128)(2,1)S(1)} %get-tuple-element.108), channel_id=1, source_target_pairs={{0,2},{2,0},{4,6},{6,4},{8,10},{10,8},{12,14},{14,12},{16,18},{18,... | collective-permute-start | bytes 884744 | tf_op jit(solution)/shard_map/ppermute | solution.py:436
  54.2 5.0 %collective-permute-done.14.refs_11_ = bf16[512,384]{1,0:T(8,128)(2,1)S(1)} collective-permute-done((bf16[512,384]{1,0:T(8,128)(2,1)S(1)}, bf16[512,384]{1,0:T(8,128)(2,1)S(1)}, u32[]{:S(2)}, u32[]{:S(2)}) %collective-permute-start.14) | collective-permute-done | bytes 393248 | tf_op jit(solution)/shard_map/ppermute | solution.py:442
  59.2 3.3 %collective-permute-start.20 = (bf16[384,384]{1,0:T(8,128)(2,1)S(1)}, bf16[384,384]{1,0:T(8,128)(2,1)S(1)}, u32[]{:S(2)}, u32[]{:S(2)}) collective-permute-start(bf16[384,384]{1,0:T(8,128)(2,1)S(1)} %get-tuple-element.110), channel_id=1, source_target_pairs={{0,6},{2,4},{4,2},{6,0},{8,14},{10,12},{12,10},{14,8},{16,22},{18,... | collective-permute-start | bytes 884744 | tf_op jit(solution)/shard_map/ppermute | solution.py:436
  62.5 0.9 collective-permute-done.8.refs_4_
  63.4 1.3 %collective-permute-start.29 = (bf16[512,384]{1,0:T(8,128)(2,1)S(1)}, bf16[512,384]{1,0:T(8,128)(2,1)S(1)}, u32[]{:S(2)}, u32[]{:S(2)}) collective-permute-start(bf16[512,384]{1,0:T(8,128)(2,1)S(1)} %collective-permute-done.28.refs_8_), channel_id=1, source_target_pairs={{8,0},{10,2},{12,4},{14,6},{16,24},{18,26},{20,28},{22,30},{9,1},{... | collective-permute-start | bytes 1179656 | tf_op jit(solution)/shard_map/ppermute | solution.py:442
  64.7 1.3 %collective-permute-start.31 = (bf16[512,384]{1,0:T(8,128)(2,1)S(1)}, bf16[512,384]{1,0:T(8,128)(2,1)S(1)}, u32[]{:S(2)}, u32[]{:S(2)}) collective-permute-start(bf16[512,384]{1,0:T(8,128)(2,1)S(1)} %collective-permute-done.30.refs_10_), channel_id=1, source_target_pairs={{8,0},{10,2},{12,4},{14,6},{16,24},{18,26},{20,28},{22,30},{9,1},{... | collective-permute-start | bytes 1179656 | tf_op jit(solution)/shard_map/ppermute | solution.py:442
  66.0 8.6 %shard_map.109 = (bf16[128,384]{1,0:T(8,128)(2,1)S(1)}, bf16[128,384]{1,0:T(8,128)(2,1)S(1)}, bf16[128,384]{1,0:T(8,128)(2,1)S(1)}, bf16[128,384]{1,0:T(8,128)(2,1)S(1)}) custom-call(s32[4]{0:T(128)S(1)} %pad_add_fusion.place, s32[16]{0:T(128)S(1)} %copy-done.5, f32[3,32]{1,0:T(4,128)S(1)} %add_convert_fusion.table, ...), custom_call_target="tpu_custom_call" | custom-call | flops 1 | bytes 1 | tf_op jit(solution)/shard_map/pallas_call | solution.py:354
  74.6 1.7 %collective-permute-start.15 = (bf16[128,384]{1,0:T(8,128)(2,1)S(1)}, bf16[128,384]{1,0:T(8,128)(2,1)S(1)}, u32[]{:S(2)}, u32[]{:S(2)}) collective-permute-start(bf16[128,384]{1,0:T(8,128)(2,1)S(1)} %get-tuple-element.102), channel_id=1, source_target_pairs={{0,2},{2,0},{4,6},{6,4},{8,10},{10,8},{12,14},{14,12},{16,18},{18,... | collective-permute-start | bytes 294920 | tf_op jit(solution)/shard_map/ppermute | solution.py:436
  77.5 1.3 %collective-permute-start.22 = (bf16[256,384]{1,0:T(8,128)(2,1)S(1)}, bf16[256,384]{1,0:T(8,128)(2,1)S(1)}, u32[]{:S(2)}, u32[]{:S(2)}) collective-permute-start(bf16[256,384]{1,0:T(8,128)(2,1)S(1)} %shard_map.111), channel_id=1, source_target_pairs={{0,8},{2,10},{4,12},{6,14},{16,24},{18,26},{20,28},{22,30},{1,9},{... | collective-permute-start | bytes 589832 | tf_op jit(solution)/shard_map/ppermute | solution.py:442
  79.5 1.1 collective-permute-done.16.refs_2_
  80.7 1.4 %collective-permute-start.17 = (bf16[128,384]{1,0:T(8,128)(2,1)S(1)}, bf16[128,384]{1,0:T(8,128)(2,1)S(1)}, u32[]{:S(2)}, u32[]{:S(2)}) collective-permute-start(bf16[128,384]{1,0:T(8,128)(2,1)S(1)} %get-tuple-element.104), channel_id=1, source_target_pairs={{0,6},{2,4},{4,2},{6,0},{8,14},{10,12},{12,10},{14,8},{16,22},{18,... | collective-permute-start | bytes 294920 | tf_op jit(solution)/shard_map/ppermute | solution.py:436
  82.0 3.8 %collective-permute-done.17.refs_3_ = bf16[128,384]{1,0:T(8,128)(2,1)S(1)} collective-permute-done((bf16[128,384]{1,0:T(8,128)(2,1)S(1)}, bf16[128,384]{1,0:T(8,128)(2,1)S(1)}, u32[]{:S(2)}, u32[]{:S(2)}) %collective-permute-start.17) | collective-permute-done | bytes 98336 | tf_op jit(solution)/shard_map/ppermute | solution.py:436
  85.9 1.0 shard_map.110
  87.0 8.7 %shard_map.113 = (bf16[128,384]{1,0:T(8,128)(2,1)S(1)}, bf16[128,384]{1,0:T(8,128)(2,1)S(1)}, bf16[128,384]{1,0:T(8,128)(2,1)S(1)}, bf16[128,384]{1,0:T(8,128)(2,1)S(1)}) custom-call(s32[4]{0:T(128)S(1)} %pad_add_fusion.place, s32[16]{0:T(128)S(1)} %copy-done.5, f32[3,32]{1,0:T(4,128)S(1)} %add_convert_fusion.table, ...), custom_call_target="tpu_custom_call" | custom-call | flops 1 | bytes 1 | tf_op jit(solution)/shard_map/pallas_call | solution.py:354
  95.6 2.6 %collective-permute-start.32 = (bf16[128,384]{1,0:T(8,128)(2,1)S(1)}, bf16[128,384]{1,0:T(8,128)(2,1)S(1)}, u32[]{:S(2)}, u32[]{:S(2)}) collective-permute-start(bf16[128,384]{1,0:T(8,128)(2,1)S(1)} %get-tuple-element.122), channel_id=1, source_target_pairs={{0,2},{2,0},{4,6},{6,4},{8,10},{10,8},{12,14},{14,12},{16,18},{18,... | collective-permute-start | bytes 294920 | tf_op jit(solution)/shard_map/ppermute | solution.py:436
  98.9 1.1 collective-permute-start.34
  100.2 2.4 %collective-permute-done.33.refs_2_ = bf16[128,384]{1,0:T(8,128)(2,1)S(1)} collective-permute-done((bf16[128,384]{1,0:T(8,128)(2,1)S(1)}, bf16[128,384]{1,0:T(8,128)(2,1)S(1)}, u32[]{:S(2)}, u32[]{:S(2)}) %collective-permute-start.33) | collective-permute-done | bytes 98336 | tf_op jit(solution)/shard_map/ppermute | solution.py:436
  102.6 2.6 %collective-permute-done.34.refs_3_ = bf16[128,384]{1,0:T(8,128)(2,1)S(1)} collective-permute-done((bf16[128,384]{1,0:T(8,128)(2,1)S(1)}, bf16[128,384]{1,0:T(8,128)(2,1)S(1)}, u32[]{:S(2)}, u32[]{:S(2)}) %collective-permute-start.34) | collective-permute-done | bytes 98336 | tf_op jit(solution)/shard_map/ppermute | solution.py:436
  105.2 1.0 shard_map.114
  106.5 2.1 %shard_map.116 = (bf16[256,1536]{1,0:T(8,128)(2,1)}, bf16[256,1536]{1,0:T(8,128)(2,1)}) custom-call(s32[4]{0:T(128)S(1)} %pad_add_fusion.place, bf16[192,1536]{1,0:T(8,128)(2,1)S(1)} %get-tuple-element.127.refs_0_, bf16[192,1536]{1,0:T(8,128)(2,1)S(1)} %collective-permute-done.3.refs_1_, bf16[192,1536]{1,0:T(8,128)(2,1)S(1)} %get-tuple-element.85.refs_0_.refs_2_, ...), custom_call_target="tpu_custom_call" | custom-call | flops 1 | bytes 1 | tf_op jit(solution)/shard_map/pallas_call | solution.py:165
  108.6 4.3 %collective-permute-done.35.refs_3_ = bf16[128,768]{1,0:T(8,128)(2,1)S(1)} collective-permute-done((bf16[128,768]{1,0:T(8,128)(2,1)S(1)}, bf16[128,768]{1,0:T(8,128)(2,1)S(1)}, u32[]{:S(2)}, u32[]{:S(2)}) %collective-permute-start.35) | collective-permute-done | bytes 196640 | tf_op jit(solution)/shard_map/ppermute | solution.py:436
  112.9 1.6 %shard_map.115 = bf16[128,3072]{1,0:T(8,128)(2,1)} custom-call(s32[4]{0:T(128)S(1)} %pad_add_fusion.place, bf16[128,768]{1,0:T(8,128)(2,1)S(1)} %get-tuple-element.111.refs_0_, bf16[128,768]{1,0:T(8,128)(2,1)S(1)} %collective-permute-done.21.refs_1_, bf16[128,768]{1,0:T(8,128)(2,1)S(1)} %get-tuple-element.125.refs_2_, ...), custom_call_target="tpu_custom_call" | custom-call | flops 1 | bytes 1 | tf_op jit(solution)/shard_map/pallas_call | solution.py:423
  (61 shorter events, 12.2 us)
Async XLA Ops:
  0.6 6.5 %copy-start = (bf16[128,3072]{1,0:T(8,128)(2,1)S(1)}, bf16[128,3072]{1,0:T(8,128)(2,1)}, u32[]{:S(2)}) copy-start(bf16[128,3072]{1,0:T(8,128)(2,1)} %queries.1) | copy-start | bytes 2359300
  0.7 1.1 copy-start.3
  1.8 1.0 copy-start.4
  3.5 3.6 %collective-permute-start = (bf16[128,384]{1,0:T(8,128)(2,1)S(1)}, bf16[128,384]{1,0:T(8,128)(2,1)S(1)}, u32[]{:S(2)}, u32[]{:S(2)}) collective-permute-start(bf16[128,384]{1,0:T(8,128)(2,1)S(1)} %get-tuple-element.68), channel_id=1, source_target_pairs={{0,2},{2,0},{4,6},{6,4},{8,10},{10,8},{12,14},{14,12},{16,18},{18,... | collective-permute-start | bytes 294920 | tf_op jit(solution)/shard_map/ppermute | solution.py:436
  4.3 8.3 %collective-permute-start.1 = (bf16[128,384]{1,0:T(8,128)(2,1)S(1)}, bf16[128,384]{1,0:T(8,128)(2,1)S(1)}, u32[]{:S(2)}, u32[]{:S(2)}) collective-permute-start(bf16[128,384]{1,0:T(8,128)(2,1)S(1)} %get-tuple-element.70), channel_id=1, source_target_pairs={{0,4},{2,6},{4,0},{6,2},{8,12},{10,14},{12,8},{14,10},{16,20},{18,... | collective-permute-start | bytes 294920 | tf_op jit(solution)/shard_map/ppermute | solution.py:436
  5.5 0.7 copy-start.6
  5.5 7.1 %collective-permute-start.2 = (bf16[128,384]{1,0:T(8,128)(2,1)S(1)}, bf16[128,384]{1,0:T(8,128)(2,1)S(1)}, u32[]{:S(2)}, u32[]{:S(2)}) collective-permute-start(bf16[128,384]{1,0:T(8,128)(2,1)S(1)} %get-tuple-element.71), channel_id=1, source_target_pairs={{0,6},{2,4},{4,2},{6,0},{8,14},{10,12},{12,10},{14,8},{16,22},{18,... | collective-permute-start | bytes 294920 | tf_op jit(solution)/shard_map/ppermute | solution.py:436
  6.4 0.7 copy-start.7
  7.1 1.1 copy-start.1
  8.3 1.1 copy-start.2
  12.6 14.6 %collective-permute-start.3 = (bf16[192,1536]{1,0:T(8,128)(2,1)S(1)}, bf16[192,1536]{1,0:T(8,128)(2,1)S(1)}, u32[]{:S(2)}, u32[]{:S(2)}) collective-permute-start(bf16[192,1536]{1,0:T(8,128)(2,1)S(1)} %get-tuple-element.78), channel_id=1, source_target_pairs={{0,1},{1,0},{2,3},{3,2},{4,5},{5,4},{6,7},{7,6},{8,9},{9,8},{10,11... | collective-permute-start | bytes 1769480 | tf_op jit(solution)/shard_map/ppermute | solution.py:436
  13.9 10.1 %collective-permute-start.10 = (bf16[512,384]{1,0:T(8,128)(2,1)S(1)}, bf16[512,384]{1,0:T(8,128)(2,1)S(1)}, u32[]{:S(2)}, u32[]{:S(2)}) collective-permute-start(bf16[512,384]{1,0:T(8,128)(2,1)S(1)} %shard_map.108.refs_6_), channel_id=1, source_target_pairs={{0,8},{2,10},{4,12},{6,14},{8,0},{10,2},{12,4},{14,6},{16,24},{18,... | collective-permute-start | bytes 1179656 | tf_op jit(solution)/shard_map/ppermute | solution.py:442
  14.2 2.5 %collective-permute-start.24 = (bf16[128,384]{1,0:T(8,128)(2,1)S(1)}, bf16[128,384]{1,0:T(8,128)(2,1)S(1)}, u32[]{:S(2)}, u32[]{:S(2)}) collective-permute-start(bf16[128,384]{1,0:T(8,128)(2,1)S(1)} %get-tuple-element.118), channel_id=1, source_target_pairs={{0,2},{2,0},{4,6},{6,4},{8,10},{10,8},{12,14},{14,12},{16,18},{18,... | collective-permute-start | bytes 294920 | tf_op jit(solution)/shard_map/ppermute | solution.py:436
  15.1 4.4 %collective-permute-start.25 = (bf16[128,384]{1,0:T(8,128)(2,1)S(1)}, bf16[128,384]{1,0:T(8,128)(2,1)S(1)}, u32[]{:S(2)}, u32[]{:S(2)}) collective-permute-start(bf16[128,384]{1,0:T(8,128)(2,1)S(1)} %get-tuple-element.119), channel_id=1, source_target_pairs={{0,4},{2,6},{4,0},{6,2},{8,12},{10,14},{12,8},{14,10},{16,20},{18,... | collective-permute-start | bytes 294920 | tf_op jit(solution)/shard_map/ppermute | solution.py:436
  15.9 6.1 %collective-permute-start.26 = (bf16[128,384]{1,0:T(8,128)(2,1)S(1)}, bf16[128,384]{1,0:T(8,128)(2,1)S(1)}, u32[]{:S(2)}, u32[]{:S(2)}) collective-permute-start(bf16[128,384]{1,0:T(8,128)(2,1)S(1)} %get-tuple-element.120), channel_id=1, source_target_pairs={{0,6},{2,4},{4,2},{6,0},{8,14},{10,12},{12,10},{14,8},{16,22},{18,... | collective-permute-start | bytes 294920 | tf_op jit(solution)/shard_map/ppermute | solution.py:436
  16.7 13.7 %collective-permute-start.11 = (bf16[512,384]{1,0:T(8,128)(2,1)S(1)}, bf16[512,384]{1,0:T(8,128)(2,1)S(1)}, u32[]{:S(2)}, u32[]{:S(2)}) collective-permute-start(bf16[512,384]{1,0:T(8,128)(2,1)S(1)} %shard_map.108.refs_6_), channel_id=1, source_target_pairs={{8,16},{10,18},{12,20},{14,22},{16,8},{18,10},{20,12},{22,14},{9,1... | collective-permute-start | bytes 1179656 | tf_op jit(solution)/shard_map/ppermute | solution.py:442
  22.0 11.3 %collective-permute-start.27 = (bf16[512,384]{1,0:T(8,128)(2,1)S(1)}, bf16[512,384]{1,0:T(8,128)(2,1)S(1)}, u32[]{:S(2)}, u32[]{:S(2)}) collective-permute-start(bf16[512,384]{1,0:T(8,128)(2,1)S(1)} %shard_map.112.refs_6_), channel_id=1, source_target_pairs={{0,8},{2,10},{4,12},{6,14},{8,0},{10,2},{12,4},{14,6},{16,24},{18,... | collective-permute-start | bytes 1179656 | tf_op jit(solution)/shard_map/ppermute | solution.py:442
  24.0 10.9 %collective-permute-start.13 = (bf16[512,384]{1,0:T(8,128)(2,1)S(1)}, bf16[512,384]{1,0:T(8,128)(2,1)S(1)}, u32[]{:S(2)}, u32[]{:S(2)}) collective-permute-start(bf16[512,384]{1,0:T(8,128)(2,1)S(1)} %collective-permute-done.10.refs_7_), channel_id=1, source_target_pairs={{8,16},{10,18},{12,20},{14,22},{16,8},{18,10},{20,12},{22,14},{9,1... | collective-permute-start | bytes 1179656 | tf_op jit(solution)/shard_map/ppermute | solution.py:442
  27.9 7.7 %collective-permute-start.4 = (bf16[384,384]{1,0:T(8,128)(2,1)S(1)}, bf16[384,384]{1,0:T(8,128)(2,1)S(1)}, u32[]{:S(2)}, u32[]{:S(2)}) collective-permute-start(bf16[384,384]{1,0:T(8,128)(2,1)S(1)} %get-tuple-element.80), channel_id=1, source_target_pairs={{0,2},{2,0},{4,6},{6,4},{8,10},{10,8},{12,14},{14,12},{16,18},{18,... | collective-permute-start | bytes 884744 | tf_op jit(solution)/shard_map/ppermute | solution.py:436
  29.1 18.5 %collective-permute-start.7 = (bf16[192,1536]{1,0:T(8,128)(2,1)S(1)}, bf16[192,1536]{1,0:T(8,128)(2,1)S(1)}, u32[]{:S(2)}, u32[]{:S(2)}) collective-permute-start(bf16[192,1536]{1,0:T(8,128)(2,1)S(1)} %get-tuple-element.86), channel_id=1, source_target_pairs={{0,1},{1,0},{2,3},{3,2},{4,5},{5,4},{6,7},{7,6},{8,9},{9,8},{10,11... | collective-permute-start | bytes 1769480 | tf_op jit(solution)/shard_map/ppermute | solution.py:436
  30.4 8.2 %collective-permute-start.5 = (bf16[384,384]{1,0:T(8,128)(2,1)S(1)}, bf16[384,384]{1,0:T(8,128)(2,1)S(1)}, u32[]{:S(2)}, u32[]{:S(2)}) collective-permute-start(bf16[384,384]{1,0:T(8,128)(2,1)S(1)} %get-tuple-element.81), channel_id=1, source_target_pairs={{0,4},{2,6},{4,0},{6,2},{8,12},{10,14},{12,8},{14,10},{16,20},{18,... | collective-permute-start | bytes 884744 | tf_op jit(solution)/shard_map/ppermute | solution.py:436
  33.3 12.4 %collective-permute-start.6 = (bf16[384,384]{1,0:T(8,128)(2,1)S(1)}, bf16[384,384]{1,0:T(8,128)(2,1)S(1)}, u32[]{:S(2)}, u32[]{:S(2)}) collective-permute-start(bf16[384,384]{1,0:T(8,128)(2,1)S(1)} %get-tuple-element.82), channel_id=1, source_target_pairs={{0,6},{2,4},{4,2},{6,0},{8,14},{10,12},{12,10},{14,8},{16,22},{18,... | collective-permute-start | bytes 884744 | tf_op jit(solution)/shard_map/ppermute | solution.py:436
  34.9 14.7 %collective-permute-start.28 = (bf16[512,384]{1,0:T(8,128)(2,1)S(1)}, bf16[512,384]{1,0:T(8,128)(2,1)S(1)}, u32[]{:S(2)}, u32[]{:S(2)}) collective-permute-start(bf16[512,384]{1,0:T(8,128)(2,1)S(1)} %shard_map.112.refs_6_), channel_id=1, source_target_pairs={{8,16},{10,18},{12,20},{14,22},{16,8},{18,10},{20,12},{22,14},{9,1... | collective-permute-start | bytes 1179656 | tf_op jit(solution)/shard_map/ppermute | solution.py:442
  35.6 15.2 %collective-permute-start.12 = (bf16[512,384]{1,0:T(8,128)(2,1)S(1)}, bf16[512,384]{1,0:T(8,128)(2,1)S(1)}, u32[]{:S(2)}, u32[]{:S(2)}) collective-permute-start(bf16[512,384]{1,0:T(8,128)(2,1)S(1)} %collective-permute-done.11.refs_8_), channel_id=1, source_target_pairs={{8,0},{10,2},{12,4},{14,6},{16,24},{18,26},{20,28},{22,30},{9,1},{... | collective-permute-start | bytes 1179656 | tf_op jit(solution)/shard_map/ppermute | solution.py:442
  38.6 15.0 %collective-permute-start.30 = (bf16[512,384]{1,0:T(8,128)(2,1)S(1)}, bf16[512,384]{1,0:T(8,128)(2,1)S(1)}, u32[]{:S(2)}, u32[]{:S(2)}) collective-permute-start(bf16[512,384]{1,0:T(8,128)(2,1)S(1)} %collective-permute-done.27.refs_7_), channel_id=1, source_target_pairs={{8,16},{10,18},{12,20},{14,22},{16,8},{18,10},{20,12},{22,14},{9,1... | collective-permute-start | bytes 1179656 | tf_op jit(solution)/shard_map/ppermute | solution.py:442
  45.7 13.5 %collective-permute-start.14 = (bf16[512,384]{1,0:T(8,128)(2,1)S(1)}, bf16[512,384]{1,0:T(8,128)(2,1)S(1)}, u32[]{:S(2)}, u32[]{:S(2)}) collective-permute-start(bf16[512,384]{1,0:T(8,128)(2,1)S(1)} %collective-permute-done.13.refs_10_), channel_id=1, source_target_pairs={{8,0},{10,2},{12,4},{14,6},{16,24},{18,26},{20,28},{22,30},{9,1},{... | collective-permute-start | bytes 1179656 | tf_op jit(solution)/shard_map/ppermute | solution.py:442
  48.3 17.8 %copy-start.5 = (s32[16]{0:T(128)S(1)}, s32[16]{0:T(128)}, u32[]{:S(2)}) copy-start(s32[16]{0:T(128)} %pages.3) | copy-start | bytes 196
  48.3 15.1 %collective-permute-start.8 = (bf16[256,384]{1,0:T(8,128)(2,1)S(1)}, bf16[256,384]{1,0:T(8,128)(2,1)S(1)}, u32[]{:S(2)}, u32[]{:S(2)}) collective-permute-start(bf16[256,384]{1,0:T(8,128)(2,1)S(1)} %shard_map.106), channel_id=1, source_target_pairs={{0,8},{2,10},{4,12},{6,14},{16,24},{18,26},{20,28},{22,30},{1,9},{... | collective-permute-start | bytes 589832 | tf_op jit(solution)/shard_map/ppermute | solution.py:442
  49.6 15.1 %collective-permute-start.9 = (bf16[256,384]{1,0:T(8,128)(2,1)S(1)}, bf16[256,384]{1,0:T(8,128)(2,1)S(1)}, u32[]{:S(2)}, u32[]{:S(2)}) collective-permute-start(bf16[256,384]{1,0:T(8,128)(2,1)S(1)} %shard_map.106), channel_id=1, source_target_pairs={{8,16},{10,18},{12,20},{14,22},{9,17},{11,19},{13,21},{15,23}} | collective-permute-start | bytes 589832 | tf_op jit(solution)/shard_map/ppermute | solution.py:442
  50.8 23.8 %collective-permute-start.18 = (bf16[384,384]{1,0:T(8,128)(2,1)S(1)}, bf16[384,384]{1,0:T(8,128)(2,1)S(1)}, u32[]{:S(2)}, u32[]{:S(2)}) collective-permute-start(bf16[384,384]{1,0:T(8,128)(2,1)S(1)} %get-tuple-element.108), channel_id=1, source_target_pairs={{0,2},{2,0},{4,6},{6,4},{8,10},{10,8},{12,14},{14,12},{16,18},{18,... | collective-permute-start | bytes 884744 | tf_op jit(solution)/shard_map/ppermute | solution.py:436
  53.6 22.7 %collective-permute-start.19 = (bf16[384,384]{1,0:T(8,128)(2,1)S(1)}, bf16[384,384]{1,0:T(8,128)(2,1)S(1)}, u32[]{:S(2)}, u32[]{:S(2)}) collective-permute-start(bf16[384,384]{1,0:T(8,128)(2,1)S(1)} %get-tuple-element.109), channel_id=1, source_target_pairs={{0,4},{2,6},{4,0},{6,2},{8,12},{10,14},{12,8},{14,10},{16,20},{18,... | collective-permute-start | bytes 884744 | tf_op jit(solution)/shard_map/ppermute | solution.py:436
  59.2 17.7 %collective-permute-start.20 = (bf16[384,384]{1,0:T(8,128)(2,1)S(1)}, bf16[384,384]{1,0:T(8,128)(2,1)S(1)}, u32[]{:S(2)}, u32[]{:S(2)}) collective-permute-start(bf16[384,384]{1,0:T(8,128)(2,1)S(1)} %get-tuple-element.110), channel_id=1, source_target_pairs={{0,6},{2,4},{4,2},{6,0},{8,14},{10,12},{12,10},{14,8},{16,22},{18,... | collective-permute-start | bytes 884744 | tf_op jit(solution)/shard_map/ppermute | solution.py:436
  63.4 23.5 %collective-permute-start.29 = (bf16[512,384]{1,0:T(8,128)(2,1)S(1)}, bf16[512,384]{1,0:T(8,128)(2,1)S(1)}, u32[]{:S(2)}, u32[]{:S(2)}) collective-permute-start(bf16[512,384]{1,0:T(8,128)(2,1)S(1)} %collective-permute-done.28.refs_8_), channel_id=1, source_target_pairs={{8,0},{10,2},{12,4},{14,6},{16,24},{18,26},{20,28},{22,30},{9,1},{... | collective-permute-start | bytes 1179656 | tf_op jit(solution)/shard_map/ppermute | solution.py:442
  64.7 22.2 %collective-permute-start.31 = (bf16[512,384]{1,0:T(8,128)(2,1)S(1)}, bf16[512,384]{1,0:T(8,128)(2,1)S(1)}, u32[]{:S(2)}, u32[]{:S(2)}) collective-permute-start(bf16[512,384]{1,0:T(8,128)(2,1)S(1)} %collective-permute-done.30.refs_10_), channel_id=1, source_target_pairs={{8,0},{10,2},{12,4},{14,6},{16,24},{18,26},{20,28},{22,30},{9,1},{... | collective-permute-start | bytes 1179656 | tf_op jit(solution)/shard_map/ppermute | solution.py:442
  74.6 4.2 %collective-permute-start.15 = (bf16[128,384]{1,0:T(8,128)(2,1)S(1)}, bf16[128,384]{1,0:T(8,128)(2,1)S(1)}, u32[]{:S(2)}, u32[]{:S(2)}) collective-permute-start(bf16[128,384]{1,0:T(8,128)(2,1)S(1)} %get-tuple-element.102), channel_id=1, source_target_pairs={{0,2},{2,0},{4,6},{6,4},{8,10},{10,8},{12,14},{14,12},{16,18},{18,... | collective-permute-start | bytes 294920 | tf_op jit(solution)/shard_map/ppermute | solution.py:436
  76.3 4.4 %collective-permute-start.16 = (bf16[128,384]{1,0:T(8,128)(2,1)S(1)}, bf16[128,384]{1,0:T(8,128)(2,1)S(1)}, u32[]{:S(2)}, u32[]{:S(2)}) collective-permute-start(bf16[128,384]{1,0:T(8,128)(2,1)S(1)} %get-tuple-element.103), channel_id=1, source_target_pairs={{0,4},{2,6},{4,0},{6,2},{8,12},{10,14},{12,8},{14,10},{16,20},{18,... | collective-permute-start | bytes 294920 | tf_op jit(solution)/shard_map/ppermute | solution.py:436
  77.5 9.4 %collective-permute-start.22 = (bf16[256,384]{1,0:T(8,128)(2,1)S(1)}, bf16[256,384]{1,0:T(8,128)(2,1)S(1)}, u32[]{:S(2)}, u32[]{:S(2)}) collective-permute-start(bf16[256,384]{1,0:T(8,128)(2,1)S(1)} %shard_map.111), channel_id=1, source_target_pairs={{0,8},{2,10},{4,12},{6,14},{16,24},{18,26},{20,28},{22,30},{1,9},{... | collective-permute-start | bytes 589832 | tf_op jit(solution)/shard_map/ppermute | solution.py:442
  78.9 8.1 %collective-permute-start.23 = (bf16[256,384]{1,0:T(8,128)(2,1)S(1)}, bf16[256,384]{1,0:T(8,128)(2,1)S(1)}, u32[]{:S(2)}, u32[]{:S(2)}) collective-permute-start(bf16[256,384]{1,0:T(8,128)(2,1)S(1)} %shard_map.111), channel_id=1, source_target_pairs={{8,16},{10,18},{12,20},{14,22},{9,17},{11,19},{13,21},{15,23}} | collective-permute-start | bytes 589832 | tf_op jit(solution)/shard_map/ppermute | solution.py:442
  80.7 5.2 %collective-permute-start.17 = (bf16[128,384]{1,0:T(8,128)(2,1)S(1)}, bf16[128,384]{1,0:T(8,128)(2,1)S(1)}, u32[]{:S(2)}, u32[]{:S(2)}) collective-permute-start(bf16[128,384]{1,0:T(8,128)(2,1)S(1)} %get-tuple-element.104), channel_id=1, source_target_pairs={{0,6},{2,4},{4,2},{6,0},{8,14},{10,12},{12,10},{14,8},{16,22},{18,... | collective-permute-start | bytes 294920 | tf_op jit(solution)/shard_map/ppermute | solution.py:436
  95.6 4.5 %collective-permute-start.32 = (bf16[128,384]{1,0:T(8,128)(2,1)S(1)}, bf16[128,384]{1,0:T(8,128)(2,1)S(1)}, u32[]{:S(2)}, u32[]{:S(2)}) collective-permute-start(bf16[128,384]{1,0:T(8,128)(2,1)S(1)} %get-tuple-element.122), channel_id=1, source_target_pairs={{0,2},{2,0},{4,6},{6,4},{8,10},{10,8},{12,14},{14,12},{16,18},{18,... | collective-permute-start | bytes 294920 | tf_op jit(solution)/shard_map/ppermute | solution.py:436
  98.2 4.4 %collective-permute-start.33 = (bf16[128,384]{1,0:T(8,128)(2,1)S(1)}, bf16[128,384]{1,0:T(8,128)(2,1)S(1)}, u32[]{:S(2)}, u32[]{:S(2)}) collective-permute-start(bf16[128,384]{1,0:T(8,128)(2,1)S(1)} %get-tuple-element.123), channel_id=1, source_target_pairs={{0,4},{2,6},{4,0},{6,2},{8,12},{10,14},{12,8},{14,10},{16,20},{18,... | collective-permute-start | bytes 294920 | tf_op jit(solution)/shard_map/ppermute | solution.py:436
  98.9 6.3 %collective-permute-start.34 = (bf16[128,384]{1,0:T(8,128)(2,1)S(1)}, bf16[128,384]{1,0:T(8,128)(2,1)S(1)}, u32[]{:S(2)}, u32[]{:S(2)}) collective-permute-start(bf16[128,384]{1,0:T(8,128)(2,1)S(1)} %get-tuple-element.124), channel_id=1, source_target_pairs={{0,6},{2,4},{4,2},{6,0},{8,14},{10,12},{12,10},{14,8},{16,22},{18,... | collective-permute-start | bytes 294920 | tf_op jit(solution)/shard_map/ppermute | solution.py:436
  99.9 8.6 %collective-permute-start.21 = (bf16[128,768]{1,0:T(8,128)(2,1)S(1)}, bf16[128,768]{1,0:T(8,128)(2,1)S(1)}, u32[]{:S(2)}, u32[]{:S(2)}) collective-permute-start(bf16[128,768]{1,0:T(8,128)(2,1)S(1)} %get-tuple-element.112), channel_id=1, source_target_pairs={{0,1},{1,0},{2,3},{3,2},{4,5},{5,4},{6,7},{7,6},{8,9},{9,8},{10,11... | collective-permute-start | bytes 589832 | tf_op jit(solution)/shard_map/ppermute | solution.py:436
  106.2 6.7 %collective-permute-start.35 = (bf16[128,768]{1,0:T(8,128)(2,1)S(1)}, bf16[128,768]{1,0:T(8,128)(2,1)S(1)}, u32[]{:S(2)}, u32[]{:S(2)}) collective-permute-start(bf16[128,768]{1,0:T(8,128)(2,1)S(1)} %get-tuple-element.126), channel_id=1, source_target_pairs={{0,1},{1,0},{2,3},{3,2},{4,5},{5,4},{6,7},{7,6},{8,9},{9,8},{10,11... | collective-permute-start | bytes 589832 | tf_op jit(solution)/shard_map/ppermute | solution.py:436

commit v3 on v2

--- a/solution.py
+++ b/solution.py
@@ -12,6 +12,7 @@
 SLAB = 4
 LOG2E = 1.4426950408889634
 VMEM = pl.BlockSpec(memory_space=pltpu.VMEM)
+ANY = pl.BlockSpec(memory_space=pl.ANY)
 SMEM = pl.BlockSpec(memory_space=pltpu.SMEM)
 
 
@@ -44,7 +45,18 @@
     return x
 
 
-def page_kernel(chunks, place, keys, values, *outs):
+def loaded(pairs, sems):
+    copies = []
+    for i, (source, target) in enumerate(pairs):
+        copies.append(pltpu.make_async_copy(source, target, sems.at[i]))
+        copies[-1].start()
+    return copies
+
+
+def page_kernel(chunks, place, keys_in, values_in, *refs):
+    outs, (keys, values, sems) = refs[:-3], refs[-3:]
+    for copy in loaded([(keys_in, keys), (values_in, values)], sems):
+        copy.wait()
     lanes = keys.shape[-1] // SLAB
     half = lanes // chunks
     for n in range(SLAB):
@@ -61,16 +73,24 @@
     outs = pl.pallas_call(
         functools.partial(page_kernel, chunks),
         out_shape=[shape(keys.shape[1], lanes)] * (SLAB * chunks),
-        in_specs=[SMEM, VMEM, VMEM],
+        in_specs=[SMEM, ANY, ANY],
         out_specs=[VMEM] * (SLAB * chunks),
-        compiler_params=params(16),
+        scratch_shapes=[pltpu.VMEM(keys.shape, keys.dtype)] * 2 + [pltpu.SemaphoreType.DMA((2,))],
+        compiler_params=params(52),
         cost_estimate=cost(0, 4 * keys.size),
     )(place, keys, values)
     return [outs[c * SLAB : (c + 1) * SLAB] for c in range(chunks)]
 
 
-def rotate_kernel(tp, chunks, prefix, place, table, freq, queries, keys, values, *outs):
+def rotate_kernel(tp, chunks, prefix, place, table, freq, queries_in, keys_in, values_in, *refs):
+    outs, (queries, keys, values, sems) = refs[:-4], refs[-4:]
     rows, lanes = queries.shape[0], queries.shape[1] // tp
+    inputs = ((queries_in, queries), (keys_in, keys), (values_in, values))
+    copies = []
+    for m in range(tp):
+        at = pl.ds(pl.multiple_of((place[3] ^ m) * lanes, lanes), lanes)
+        pairs = [(source.at[:, at], target.at[:, at]) for source, target in inputs]
+        copies.append(loaded(pairs, sems.at[m]))
     width = freq.shape[1]
     token = place[2] + lax.broadcasted_iota(jnp.int32, (rows, 1), 0)
     token = token.astype(jnp.float32)
@@ -91,6 +111,8 @@
 
     for m in range(tp):
         base = (place[3] ^ m) * lanes
+        for copy in copies[m]:
+            copy.wait()
         for part in range(lanes // width):
             at = pl.ds(pl.multiple_of(base + part * width, width), width)
             q, k, v = turned(queries[:, at]), turned(keys[:, at]), values[:, at]
@@ -111,9 +133,11 @@
     outs = pl.pallas_call(
         functools.partial(rotate_kernel, tp, chunks, prefix),
         out_shape=[shape(rows * 3 // 2, 2 * lanes // chunks)] * (chunks * tp),
-        in_specs=[SMEM] + [VMEM] * 5,
+        in_specs=[SMEM, VMEM, VMEM, ANY, ANY, ANY],
         out_specs=[VMEM] * (chunks * tp),
-        compiler_params=params(24),
+        scratch_shapes=[pltpu.VMEM(queries.shape, queries.dtype)] * 3
+        + [pltpu.SemaphoreType.DMA((tp, 3))],
+        compiler_params=params(52),
         cost_estimate=cost(0, 12 * queries.size),
     )(place, table, freq, queries, keys, values)
     return [outs[c * tp : (c + 1) * tp] for c in range(chunks)]
@@ -225,12 +249,12 @@
 
 
 def attend_kernel(plan, place, pages, table, *refs):
-    chunk, heads, lines, early_count, unit_count, page, block, rows = plan
+    chunk, heads, lines, early_count, unit_count, page, block, rows, served = plan
     parts = refs[:SLAB]
     early = refs[SLAB : SLAB + early_count]
     units = refs[SLAB + early_count : SLAB + early_count + unit_count]
     refs = refs[SLAB + early_count + unit_count :]
-    outs, (near_keys, near_values, pool, seat) = refs[:SLAB], refs[SLAB:]
+    outs, (near_keys, near_values, pool, seat) = refs[:-4], refs[-4:]
     z, j = place[0], place[1]
     slots = lines * SLAB
     middle = (z > 0) & (z < lines - 1)
@@ -293,7 +317,7 @@
         for line in range(lines):
             set_pool(units[0], line, line * SLAB * page)
 
-    for n in range(SLAB):
+    for out, n in zip(outs, served):
         b = j ^ n
         token = first + b * block + lax.broadcasted_iota(jnp.int32, (block, 1), 0)
         request_start, group = starts_and_groups(token.astype(jnp.float32), table[...])
@@ -340,22 +364,22 @@
             result = jnp.where(inside, mixed / total, result)
         result = result[:, value_lane - low : value_lane - low + width].astype(jnp.bfloat16)
         folded = jnp.concatenate([result[: block // 2], result[block // 2 :]], axis=1)
-        outs[n][...] = folded
-
-
-def attend(place, pages, table, parts, early, units, chunk, lines, page, rows):
+        out[...] = folded
+
+
+def attend(place, pages, table, parts, early, units, chunk, lines, page, rows, served):
     block, width = parts[0].shape[0] * 2 // 3, parts[0].shape[1] // 2
     heads = width // HD
     slots = lines * SLAB
     key_low, key_high = window(width if chunk else 0, width, 2 * width)
     low, high = window(0 if chunk else width, width, 2 * width)
-    plan = (chunk, heads, lines, len(early), len(units), page, block, rows)
+    plan = (chunk, heads, lines, len(early), len(units), page, block, rows, served)
     keys = slots * page + 2 * block
     return pl.pallas_call(
         functools.partial(attend_kernel, plan),
-        out_shape=[shape(block // 2, 2 * width)] * SLAB,
+        out_shape=[shape(block // 2, 2 * width)] * len(served),
         in_specs=[SMEM, SMEM, VMEM] + [VMEM] * (SLAB + len(early) + len(units)),
-        out_specs=[VMEM] * SLAB,
+        out_specs=[VMEM] * len(served),
         scratch_shapes=[
             pltpu.VMEM(((SLAB + 1) * block, key_high - key_low), jnp.bfloat16),
             pltpu.VMEM(((SLAB + 1) * block, high - low), jnp.bfloat16),
@@ -517,7 +541,13 @@
             early = [along(last, [(i, i + 1) for i in range(lines - 1)])]
         if c:
             backs[-1], parts = after((backs[-1], parts))
-        outs = attend(place, page_table, table, parts, early, gathered[c], c, lines, page, rows)
+        outs = []
+        for served in ((2, 3, 1, 0),):
+            outs += attend(
+                place, page_table, table, parts, early, gathered[c], c, lines, page, rows, served
+            )
+        outs = outs[::-1]
+        outs[2], outs[3] = outs[3], outs[2]
         backs.append(cut_back(place, swap(outs, "seq"), tp))
     backs = [swap(back, "tp") for back in backs]
     return join(place, backs, tp, chunks), new_keys, new_values

time: 117 us -> 116 us (level)
  local copies, waits for them, and re-layouts: 5.23 us -> 2.91 us
  Pallas kernels: 29.4 us -> 31.2 us
    unnamed x16 -> x12, local copies, waits for them, and re-layouts: 5.15 us -> 2.83 us
    pallas_call x1, Pallas kernels: 3.16 us -> 4.52 us  [rotate_and_cut(): pl.pallas_call(functools.partial(rotate_kernel, tp, chunks, prefix), out_...]
  transfers between devices with their start and end apart: 36 -> 36, of which waited for: 15 -> 15; matrix products, arithmetic and copies ran while one was open for 0% -> 0% of each run, Pallas kernels for 16% -> 17%
where the time goes in v3:
time: 116 us; the launch traced here: 114 us
  starting transfers between devices  40 us (34%)
  waiting for transfers between devices  38.5 us (33%)
  Pallas kernels  31.2 us (27%)
  local copies, waits for them, and re-layouts  2.91 us (3%)
    ppermute x22, waiting for transfers between devices, swap(): lax.ppermute(parts[m], axis, [(i, i ^ m) for i in range(size)])  29.6 us
    ppermute x22, starting transfers between devices, swap(): lax.ppermute(parts[m], axis, [(i, i ^ m) for i in range(size)])  26.7 us
    pallas_call x2, Pallas kernels, attend(): pl.pallas_call(functools.partial(attend_kernel, plan), out_shape=[shape(b...  17.2 us
    ppermute x14, starting transfers between devices, along(): lax.ppermute(block, 'seq', [(a * SLAB + j, b * SLAB + j) for a, b in pair...  13.4 us
    ppermute x14, waiting for transfers between devices, along(): lax.ppermute(block, 'seq', [(a * SLAB + j, b * SLAB + j) for a, b in pair...  8.95 us
    pallas_call x1, Pallas kernels, rotate_and_cut(): pl.pallas_call(functools.partial(rotate_kernel, tp, chunks, prefix), out_...  4.52 us
    unnamed x12, local copies, waits for them, and re-layouts  2.83 us
  transfers between devices with their start and end apart: 36, of which 15 were waited for; matrix products, arithmetic and copies ran while one was open for 0% of the time, Pallas kernels for 17%

profile of v3, /device:TPU:25, one launch (start us, length us, event | category | flops | bytes accessed | tf_op | source)
XLA Modules:
  0.0 113.9 jit_solution(8469908893604341750)
XLA Ops:
  0.7 1.0 copy-done
  1.7 1.0 copy-done.1
  2.7 1.1 shard_map.103
  3.9 0.7 collective-permute-start
  4.6 1.2 %collective-permute-start.1 = (bf16[128,384]{1,0:T(8,128)(2,1)S(1)}, bf16[128,384]{1,0:T(8,128)(2,1)S(1)}, u32[]{:S(2)}, u32[]{:S(2)}) collective-permute-start(bf16[128,384]{1,0:T(8,128)(2,1)S(1)} %get-tuple-element.70), channel_id=1, source_target_pairs={{0,4},{2,6},{4,0},{6,2},{8,12},{10,14},{12,8},{14,10},{16,20},{18,... | collective-permute-start | bytes 294920 | tf_op jit(solution)/shard_map/ppermute | solution.py:460
  7.5 4.5 %shard_map.104 = (bf16[192,1536]{1,0:T(8,128)(2,1)S(1)}, bf16[192,1536]{1,0:T(8,128)(2,1)S(1)}, bf16[192,1536]{1,0:T(8,128)(2,1)S(1)}, bf16[192,1536]{1,0:T(8,128)(2,1)}) custom-call(s32[4]{0:T(128)S(1)} %pad_add_fusion.place, f32[3,32]{1,0:T(4,128)S(1)} %add_convert_fusion.table, f32[1,384]{1,0:T(1,128)S(1)} %fusion.4.freq, bf16[128,3072]{1,0:T(8,128)(2,1)} %queries_in.1, ...), custom_call_target="tpu_custom_call" | custom-call | flops 1 | bytes 1 | tf_op jit(solution)/shard_map/pallas_call | solution.py:133
  12.0 1.3 %collective-permute-start.3 = (bf16[192,1536]{1,0:T(8,128)(2,1)S(1)}, bf16[192,1536]{1,0:T(8,128)(2,1)S(1)}, u32[]{:S(2)}, u32[]{:S(2)}) collective-permute-start(bf16[192,1536]{1,0:T(8,128)(2,1)S(1)} %get-tuple-element.78), channel_id=1, source_target_pairs={{0,1},{1,0},{2,3},{3,2},{4,5},{5,4},{6,7},{7,6},{8,9},{9,8},{10,11... | collective-permute-start | bytes 1769480 | tf_op jit(solution)/shard_map/ppermute | solution.py:460
  13.6 0.9 collective-permute-start.24
  14.5 0.9 collective-permute-start.25
  15.4 0.8 collective-permute-start.26
  16.1 0.7 collective-permute-start.11
  16.8 2.1 %collective-permute-done.25.refs_2_ = bf16[128,384]{1,0:T(8,128)(2,1)S(1)} collective-permute-done((bf16[128,384]{1,0:T(8,128)(2,1)S(1)}, bf16[128,384]{1,0:T(8,128)(2,1)S(1)}, u32[]{:S(2)}, u32[]{:S(2)}) %collective-permute-start.25) | collective-permute-done | bytes 98336 | tf_op jit(solution)/shard_map/ppermute | solution.py:460
  18.9 2.5 %collective-permute-done.26.refs_3_ = bf16[128,384]{1,0:T(8,128)(2,1)S(1)} collective-permute-done((bf16[128,384]{1,0:T(8,128)(2,1)S(1)}, bf16[128,384]{1,0:T(8,128)(2,1)S(1)}, u32[]{:S(2)}, u32[]{:S(2)}) %collective-permute-start.26) | collective-permute-done | bytes 98336 | tf_op jit(solution)/shard_map/ppermute | solution.py:460
  21.5 1.4 %collective-permute-start.27 = (bf16[512,384]{1,0:T(8,128)(2,1)S(1)}, bf16[512,384]{1,0:T(8,128)(2,1)S(1)}, u32[]{:S(2)}, u32[]{:S(2)}) collective-permute-start(bf16[512,384]{1,0:T(8,128)(2,1)S(1)} %shard_map.112.refs_6_), channel_id=1, source_target_pairs={{0,8},{2,10},{4,12},{6,14},{8,0},{10,2},{12,4},{14,6},{16,24},{18,... | collective-permute-start | bytes 1179656 | tf_op jit(solution)/shard_map/ppermute | solution.py:466
  24.1 2.5 %collective-permute-done.3.refs_1_ = bf16[192,1536]{1,0:T(8,128)(2,1)S(1)} collective-permute-done((bf16[192,1536]{1,0:T(8,128)(2,1)S(1)}, bf16[192,1536]{1,0:T(8,128)(2,1)S(1)}, u32[]{:S(2)}, u32[]{:S(2)}) %collective-permute-start.3) | collective-permute-done | bytes 589856 | tf_op jit(solution)/shard_map/ppermute | solution.py:460
  27.3 1.2 %collective-permute-start.4 = (bf16[384,384]{1,0:T(8,128)(2,1)S(1)}, bf16[384,384]{1,0:T(8,128)(2,1)S(1)}, u32[]{:S(2)}, u32[]{:S(2)}) collective-permute-start(bf16[384,384]{1,0:T(8,128)(2,1)S(1)} %get-tuple-element.80), channel_id=1, source_target_pairs={{0,2},{2,0},{4,6},{6,4},{8,10},{10,8},{12,14},{14,12},{16,18},{18,... | collective-permute-start | bytes 884744 | tf_op jit(solution)/shard_map/ppermute | solution.py:460
  28.6 1.3 %collective-permute-start.7 = (bf16[192,1536]{1,0:T(8,128)(2,1)S(1)}, bf16[192,1536]{1,0:T(8,128)(2,1)S(1)}, u32[]{:S(2)}, u32[]{:S(2)}) collective-permute-start(bf16[192,1536]{1,0:T(8,128)(2,1)S(1)} %copy-done.5), channel_id=1, source_target_pairs={{0,1},{1,0},{2,3},{3,2},{4,5},{5,4},{6,7},{7,6},{8,9},{9,8},{10,11... | collective-permute-start | bytes 1769480 | tf_op jit(solution)/shard_map/ppermute | solution.py:460
  29.8 1.0 collective-permute-start.5
  30.9 1.9 %collective-permute-done.27.refs_7_ = bf16[512,384]{1,0:T(8,128)(2,1)S(1)} collective-permute-done((bf16[512,384]{1,0:T(8,128)(2,1)S(1)}, bf16[512,384]{1,0:T(8,128)(2,1)S(1)}, u32[]{:S(2)}, u32[]{:S(2)}) %collective-permute-start.27) | collective-permute-done | bytes 393248 | tf_op jit(solution)/shard_map/ppermute | solution.py:466
  32.7 1.6 %collective-permute-start.6 = (bf16[384,384]{1,0:T(8,128)(2,1)S(1)}, bf16[384,384]{1,0:T(8,128)(2,1)S(1)}, u32[]{:S(2)}, u32[]{:S(2)}) collective-permute-start(bf16[384,384]{1,0:T(8,128)(2,1)S(1)} %get-tuple-element.82), channel_id=1, source_target_pairs={{0,6},{2,4},{4,2},{6,0},{8,14},{10,12},{12,10},{14,8},{16,22},{18,... | collective-permute-start | bytes 884744 | tf_op jit(solution)/shard_map/ppermute | solution.py:460
  34.3 0.7 collective-permute-start.28
  35.0 1.3 %collective-permute-start.12 = (bf16[512,384]{1,0:T(8,128)(2,1)S(1)}, bf16[512,384]{1,0:T(8,128)(2,1)S(1)}, u32[]{:S(2)}, u32[]{:S(2)}) collective-permute-start(bf16[512,384]{1,0:T(8,128)(2,1)S(1)} %collective-permute-done.11.refs_8_), channel_id=1, source_target_pairs={{8,0},{10,2},{12,4},{14,6},{16,24},{18,26},{20,28},{22,30},{9,1},{... | collective-permute-start | bytes 1179656 | tf_op jit(solution)/shard_map/ppermute | solution.py:466
  36.3 1.7 %collective-permute-done.5.refs_2_ = bf16[384,384]{1,0:T(8,128)(2,1)S(1)} collective-permute-done((bf16[384,384]{1,0:T(8,128)(2,1)S(1)}, bf16[384,384]{1,0:T(8,128)(2,1)S(1)}, u32[]{:S(2)}, u32[]{:S(2)}) %collective-permute-start.5) | collective-permute-done | bytes 294944 | tf_op jit(solution)/shard_map/ppermute | solution.py:460
  38.7 6.4 %collective-permute-done.6.refs_3_ = bf16[384,384]{1,0:T(8,128)(2,1)S(1)} collective-permute-done((bf16[384,384]{1,0:T(8,128)(2,1)S(1)}, bf16[384,384]{1,0:T(8,128)(2,1)S(1)}, u32[]{:S(2)}, u32[]{:S(2)}) %collective-permute-start.6) | collective-permute-done | bytes 294944 | tf_op jit(solution)/shard_map/ppermute | solution.py:460
  45.2 1.3 %collective-permute-start.14 = (bf16[512,384]{1,0:T(8,128)(2,1)S(1)}, bf16[512,384]{1,0:T(8,128)(2,1)S(1)}, u32[]{:S(2)}, u32[]{:S(2)}) collective-permute-start(bf16[512,384]{1,0:T(8,128)(2,1)S(1)} %collective-permute-done.13.refs_10_), channel_id=1, source_target_pairs={{8,0},{10,2},{12,4},{14,6},{16,24},{18,26},{20,28},{22,30},{9,1},{... | collective-permute-start | bytes 1179656 | tf_op jit(solution)/shard_map/ppermute | solution.py:466
  47.7 1.3 %collective-permute-start.8 = (bf16[256,384]{1,0:T(8,128)(2,1)S(1)}, bf16[256,384]{1,0:T(8,128)(2,1)S(1)}, u32[]{:S(2)}, u32[]{:S(2)}) collective-permute-start(bf16[256,384]{1,0:T(8,128)(2,1)S(1)} %shard_map.106), channel_id=1, source_target_pairs={{0,8},{2,10},{4,12},{6,14},{16,24},{18,26},{20,28},{22,30},{1,9},{... | collective-permute-start | bytes 589832 | tf_op jit(solution)/shard_map/ppermute | solution.py:466
  50.2 2.8 %collective-permute-start.18 = (bf16[384,384]{1,0:T(8,128)(2,1)S(1)}, bf16[384,384]{1,0:T(8,128)(2,1)S(1)}, u32[]{:S(2)}, u32[]{:S(2)}) collective-permute-start(bf16[384,384]{1,0:T(8,128)(2,1)S(1)} %get-tuple-element.108), channel_id=1, source_target_pairs={{0,2},{2,0},{4,6},{6,4},{8,10},{10,8},{12,14},{14,12},{16,18},{18,... | collective-permute-start | bytes 884744 | tf_op jit(solution)/shard_map/ppermute | solution.py:460
  53.7 5.0 %collective-permute-done.14.refs_11_ = bf16[512,384]{1,0:T(8,128)(2,1)S(1)} collective-permute-done((bf16[512,384]{1,0:T(8,128)(2,1)S(1)}, bf16[512,384]{1,0:T(8,128)(2,1)S(1)}, u32[]{:S(2)}, u32[]{:S(2)}) %collective-permute-start.14) | collective-permute-done | bytes 393248 | tf_op jit(solution)/shard_map/ppermute | solution.py:466
  58.7 3.3 %collective-permute-start.20 = (bf16[384,384]{1,0:T(8,128)(2,1)S(1)}, bf16[384,384]{1,0:T(8,128)(2,1)S(1)}, u32[]{:S(2)}, u32[]{:S(2)}) collective-permute-start(bf16[384,384]{1,0:T(8,128)(2,1)S(1)} %get-tuple-element.110), channel_id=1, source_target_pairs={{0,6},{2,4},{4,2},{6,0},{8,14},{10,12},{12,10},{14,8},{16,22},{18,... | collective-permute-start | bytes 884744 | tf_op jit(solution)/shard_map/ppermute | solution.py:460
  62.0 0.9 collective-permute-done.8.refs_4_
  62.9 1.3 %collective-permute-start.29 = (bf16[512,384]{1,0:T(8,128)(2,1)S(1)}, bf16[512,384]{1,0:T(8,128)(2,1)S(1)}, u32[]{:S(2)}, u32[]{:S(2)}) collective-permute-start(bf16[512,384]{1,0:T(8,128)(2,1)S(1)} %collective-permute-done.28.refs_8_), channel_id=1, source_target_pairs={{8,0},{10,2},{12,4},{14,6},{16,24},{18,26},{20,28},{22,30},{9,1},{... | collective-permute-start | bytes 1179656 | tf_op jit(solution)/shard_map/ppermute | solution.py:466
  64.2 1.3 %collective-permute-start.31 = (bf16[512,384]{1,0:T(8,128)(2,1)S(1)}, bf16[512,384]{1,0:T(8,128)(2,1)S(1)}, u32[]{:S(2)}, u32[]{:S(2)}) collective-permute-start(bf16[512,384]{1,0:T(8,128)(2,1)S(1)} %collective-permute-done.30.refs_10_), channel_id=1, source_target_pairs={{8,0},{10,2},{12,4},{14,6},{16,24},{18,26},{20,28},{22,30},{9,1},{... | collective-permute-start | bytes 1179656 | tf_op jit(solution)/shard_map/ppermute | solution.py:466
  65.5 8.6 %shard_map.109 = (bf16[128,384]{1,0:T(8,128)(2,1)S(1)}, bf16[128,384]{1,0:T(8,128)(2,1)S(1)}, bf16[128,384]{1,0:T(8,128)(2,1)S(1)}, bf16[128,384]{1,0:T(8,128)(2,1)S(1)}) custom-call(s32[4]{0:T(128)S(1)} %pad_add_fusion.place, s32[16]{0:T(128)S(1)} %copy-done.2, f32[3,32]{1,0:T(4,128)S(1)} %add_convert_fusion.table, ...), custom_call_target="tpu_custom_call" | custom-call | flops 1 | bytes 1 | tf_op jit(solution)/shard_map/pallas_call | solution.py:378
  74.1 1.7 %collective-permute-start.15 = (bf16[128,384]{1,0:T(8,128)(2,1)S(1)}, bf16[128,384]{1,0:T(8,128)(2,1)S(1)}, u32[]{:S(2)}, u32[]{:S(2)}) collective-permute-start(bf16[128,384]{1,0:T(8,128)(2,1)S(1)} %get-tuple-element.102), channel_id=1, source_target_pairs={{0,2},{2,0},{4,6},{6,4},{8,10},{10,8},{12,14},{14,12},{16,18},{18,... | collective-permute-start | bytes 294920 | tf_op jit(solution)/shard_map/ppermute | solution.py:460
  77.0 1.3 %collective-permute-start.22 = (bf16[256,384]{1,0:T(8,128)(2,1)S(1)}, bf16[256,384]{1,0:T(8,128)(2,1)S(1)}, u32[]{:S(2)}, u32[]{:S(2)}) collective-permute-start(bf16[256,384]{1,0:T(8,128)(2,1)S(1)} %shard_map.111), channel_id=1, source_target_pairs={{0,8},{2,10},{4,12},{6,14},{16,24},{18,26},{20,28},{22,30},{1,9},{... | collective-permute-start | bytes 589832 | tf_op jit(solution)/shard_map/ppermute | solution.py:466
  79.0 1.1 collective-permute-done.16.refs_2_
  80.1 1.4 %collective-permute-start.17 = (bf16[128,384]{1,0:T(8,128)(2,1)S(1)}, bf16[128,384]{1,0:T(8,128)(2,1)S(1)}, u32[]{:S(2)}, u32[]{:S(2)}) collective-permute-start(bf16[128,384]{1,0:T(8,128)(2,1)S(1)} %get-tuple-element.104), channel_id=1, source_target_pairs={{0,6},{2,4},{4,2},{6,0},{8,14},{10,12},{12,10},{14,8},{16,22},{18,... | collective-permute-start | bytes 294920 | tf_op jit(solution)/shard_map/ppermute | solution.py:460
  81.5 3.8 %collective-permute-done.17.refs_3_ = bf16[128,384]{1,0:T(8,128)(2,1)S(1)} collective-permute-done((bf16[128,384]{1,0:T(8,128)(2,1)S(1)}, bf16[128,384]{1,0:T(8,128)(2,1)S(1)}, u32[]{:S(2)}, u32[]{:S(2)}) %collective-permute-start.17) | collective-permute-done | bytes 98336 | tf_op jit(solution)/shard_map/ppermute | solution.py:460
  85.3 1.0 shard_map.110
  86.4 8.7 %shard_map.113 = (bf16[128,384]{1,0:T(8,128)(2,1)S(1)}, bf16[128,384]{1,0:T(8,128)(2,1)S(1)}, bf16[128,384]{1,0:T(8,128)(2,1)S(1)}, bf16[128,384]{1,0:T(8,128)(2,1)S(1)}) custom-call(s32[4]{0:T(128)S(1)} %pad_add_fusion.place, s32[16]{0:T(128)S(1)} %copy-done.2, f32[3,32]{1,0:T(4,128)S(1)} %add_convert_fusion.table, ...), custom_call_target="tpu_custom_call" | custom-call | flops 1 | bytes 1 | tf_op jit(solution)/shard_map/pallas_call | solution.py:378
  95.1 2.6 %collective-permute-start.32 = (bf16[128,384]{1,0:T(8,128)(2,1)S(1)}, bf16[128,384]{1,0:T(8,128)(2,1)S(1)}, u32[]{:S(2)}, u32[]{:S(2)}) collective-permute-start(bf16[128,384]{1,0:T(8,128)(2,1)S(1)} %get-tuple-element.122), channel_id=1, source_target_pairs={{0,2},{2,0},{4,6},{6,4},{8,10},{10,8},{12,14},{14,12},{16,18},{18,... | collective-permute-start | bytes 294920 | tf_op jit(solution)/shard_map/ppermute | solution.py:460
  98.3 1.1 collective-permute-start.34
  99.6 2.4 %collective-permute-done.33.refs_2_ = bf16[128,384]{1,0:T(8,128)(2,1)S(1)} collective-permute-done((bf16[128,384]{1,0:T(8,128)(2,1)S(1)}, bf16[128,384]{1,0:T(8,128)(2,1)S(1)}, u32[]{:S(2)}, u32[]{:S(2)}) %collective-permute-start.33) | collective-permute-done | bytes 98336 | tf_op jit(solution)/shard_map/ppermute | solution.py:460
  102.0 2.6 %collective-permute-done.34.refs_3_ = bf16[128,384]{1,0:T(8,128)(2,1)S(1)} collective-permute-done((bf16[128,384]{1,0:T(8,128)(2,1)S(1)}, bf16[128,384]{1,0:T(8,128)(2,1)S(1)}, u32[]{:S(2)}, u32[]{:S(2)}) %collective-permute-start.34) | collective-permute-done | bytes 98336 | tf_op jit(solution)/shard_map/ppermute | solution.py:460
  104.6 1.0 shard_map.114
  105.9 2.1 %shard_map.116 = (bf16[256,1536]{1,0:T(8,128)(2,1)}, bf16[256,1536]{1,0:T(8,128)(2,1)}) custom-call(s32[4]{0:T(128)S(1)} %pad_add_fusion.place, bf16[192,1536]{1,0:T(8,128)(2,1)S(1)} %get-tuple-element.127.refs_0_, bf16[192,1536]{1,0:T(8,128)(2,1)S(1)} %collective-permute-done.3.refs_1_, bf16[192,1536]{1,0:T(8,128)(2,1)S(1)} %get-tuple-element.85.refs_0_.refs_2_, ...), custom_call_target="tpu_custom_call" | custom-call | flops 1 | bytes 1 | tf_op jit(solution)/shard_map/pallas_call | solution.py:189
  108.0 4.3 %collective-permute-done.35.refs_3_ = bf16[128,768]{1,0:T(8,128)(2,1)S(1)} collective-permute-done((bf16[128,768]{1,0:T(8,128)(2,1)S(1)}, bf16[128,768]{1,0:T(8,128)(2,1)S(1)}, u32[]{:S(2)}, u32[]{:S(2)}) %collective-permute-start.35) | collective-permute-done | bytes 196640 | tf_op jit(solution)/shard_map/ppermute | solution.py:460
  112.3 1.6 %shard_map.115 = bf16[128,3072]{1,0:T(8,128)(2,1)} custom-call(s32[4]{0:T(128)S(1)} %pad_add_fusion.place, bf16[128,768]{1,0:T(8,128)(2,1)S(1)} %get-tuple-element.111.refs_0_, bf16[128,768]{1,0:T(8,128)(2,1)S(1)} %collective-permute-done.21.refs_1_, bf16[128,768]{1,0:T(8,128)(2,1)S(1)} %get-tuple-element.125.refs_2_, ...), custom_call_target="tpu_custom_call" | custom-call | flops 1 | bytes 1 | tf_op jit(solution)/shard_map/pallas_call | solution.py:447
  (57 shorter events, 10.9 us)
Async XLA Ops:
  0.7 1.0 copy-start
  1.7 1.0 copy-start.1
  3.9 3.6 %collective-permute-start = (bf16[128,384]{1,0:T(8,128)(2,1)S(1)}, bf16[128,384]{1,0:T(8,128)(2,1)S(1)}, u32[]{:S(2)}, u32[]{:S(2)}) collective-permute-start(bf16[128,384]{1,0:T(8,128)(2,1)S(1)} %get-tuple-element.68), channel_id=1, source_target_pairs={{0,2},{2,0},{4,6},{6,4},{8,10},{10,8},{12,14},{14,12},{16,18},{18,... | collective-permute-start | bytes 294920 | tf_op jit(solution)/shard_map/ppermute | solution.py:460
  4.6 7.4 %collective-permute-start.1 = (bf16[128,384]{1,0:T(8,128)(2,1)S(1)}, bf16[128,384]{1,0:T(8,128)(2,1)S(1)}, u32[]{:S(2)}, u32[]{:S(2)}) collective-permute-start(bf16[128,384]{1,0:T(8,128)(2,1)S(1)} %get-tuple-element.70), channel_id=1, source_target_pairs={{0,4},{2,6},{4,0},{6,2},{8,12},{10,14},{12,8},{14,10},{16,20},{18,... | collective-permute-start | bytes 294920 | tf_op jit(solution)/shard_map/ppermute | solution.py:460
  5.8 0.7 copy-start.3
  5.8 6.2 %collective-permute-start.2 = (bf16[128,384]{1,0:T(8,128)(2,1)S(1)}, bf16[128,384]{1,0:T(8,128)(2,1)S(1)}, u32[]{:S(2)}, u32[]{:S(2)}) collective-permute-start(bf16[128,384]{1,0:T(8,128)(2,1)S(1)} %get-tuple-element.71), channel_id=1, source_target_pairs={{0,6},{2,4},{4,2},{6,0},{8,14},{10,12},{12,10},{14,8},{16,22},{18,... | collective-permute-start | bytes 294920 | tf_op jit(solution)/shard_map/ppermute | solution.py:460
  6.8 0.7 copy-start.4
  12.0 14.6 %collective-permute-start.3 = (bf16[192,1536]{1,0:T(8,128)(2,1)S(1)}, bf16[192,1536]{1,0:T(8,128)(2,1)S(1)}, u32[]{:S(2)}, u32[]{:S(2)}) collective-permute-start(bf16[192,1536]{1,0:T(8,128)(2,1)S(1)} %get-tuple-element.78), channel_id=1, source_target_pairs={{0,1},{1,0},{2,3},{3,2},{4,5},{5,4},{6,7},{7,6},{8,9},{9,8},{10,11... | collective-permute-start | bytes 1769480 | tf_op jit(solution)/shard_map/ppermute | solution.py:460
  13.4 10.1 %collective-permute-start.10 = (bf16[512,384]{1,0:T(8,128)(2,1)S(1)}, bf16[512,384]{1,0:T(8,128)(2,1)S(1)}, u32[]{:S(2)}, u32[]{:S(2)}) collective-permute-start(bf16[512,384]{1,0:T(8,128)(2,1)S(1)} %shard_map.108.refs_6_), channel_id=1, source_target_pairs={{0,8},{2,10},{4,12},{6,14},{8,0},{10,2},{12,4},{14,6},{16,24},{18,... | collective-permute-start | bytes 1179656 | tf_op jit(solution)/shard_map/ppermute | solution.py:466
  13.6 2.5 %collective-permute-start.24 = (bf16[128,384]{1,0:T(8,128)(2,1)S(1)}, bf16[128,384]{1,0:T(8,128)(2,1)S(1)}, u32[]{:S(2)}, u32[]{:S(2)}) collective-permute-start(bf16[128,384]{1,0:T(8,128)(2,1)S(1)} %get-tuple-element.118), channel_id=1, source_target_pairs={{0,2},{2,0},{4,6},{6,4},{8,10},{10,8},{12,14},{14,12},{16,18},{18,... | collective-permute-start | bytes 294920 | tf_op jit(solution)/shard_map/ppermute | solution.py:460
  14.5 4.4 %collective-permute-start.25 = (bf16[128,384]{1,0:T(8,128)(2,1)S(1)}, bf16[128,384]{1,0:T(8,128)(2,1)S(1)}, u32[]{:S(2)}, u32[]{:S(2)}) collective-permute-start(bf16[128,384]{1,0:T(8,128)(2,1)S(1)} %get-tuple-element.119), channel_id=1, source_target_pairs={{0,4},{2,6},{4,0},{6,2},{8,12},{10,14},{12,8},{14,10},{16,20},{18,... | collective-permute-start | bytes 294920 | tf_op jit(solution)/shard_map/ppermute | solution.py:460
  15.4 6.1 %collective-permute-start.26 = (bf16[128,384]{1,0:T(8,128)(2,1)S(1)}, bf16[128,384]{1,0:T(8,128)(2,1)S(1)}, u32[]{:S(2)}, u32[]{:S(2)}) collective-permute-start(bf16[128,384]{1,0:T(8,128)(2,1)S(1)} %get-tuple-element.120), channel_id=1, source_target_pairs={{0,6},{2,4},{4,2},{6,0},{8,14},{10,12},{12,10},{14,8},{16,22},{18,... | collective-permute-start | bytes 294920 | tf_op jit(solution)/shard_map/ppermute | solution.py:460
  16.1 13.7 %collective-permute-start.11 = (bf16[512,384]{1,0:T(8,128)(2,1)S(1)}, bf16[512,384]{1,0:T(8,128)(2,1)S(1)}, u32[]{:S(2)}, u32[]{:S(2)}) collective-permute-start(bf16[512,384]{1,0:T(8,128)(2,1)S(1)} %shard_map.108.refs_6_), channel_id=1, source_target_pairs={{8,16},{10,18},{12,20},{14,22},{16,8},{18,10},{20,12},{22,14},{9,1... | collective-permute-start | bytes 1179656 | tf_op jit(solution)/shard_map/ppermute | solution.py:466
  21.5 7.1 %copy-start.5 = (bf16[192,1536]{1,0:T(8,128)(2,1)S(1)}, bf16[192,1536]{1,0:T(8,128)(2,1)}, u32[]{:S(2)}) copy-start(bf16[192,1536]{1,0:T(8,128)(2,1)} %get-tuple-element.86) | copy-start | bytes 1769476
  21.5 11.3 %collective-permute-start.27 = (bf16[512,384]{1,0:T(8,128)(2,1)S(1)}, bf16[512,384]{1,0:T(8,128)(2,1)S(1)}, u32[]{:S(2)}, u32[]{:S(2)}) collective-permute-start(bf16[512,384]{1,0:T(8,128)(2,1)S(1)} %shard_map.112.refs_6_), channel_id=1, source_target_pairs={{0,8},{2,10},{4,12},{6,14},{8,0},{10,2},{12,4},{14,6},{16,24},{18,... | collective-permute-start | bytes 1179656 | tf_op jit(solution)/shard_map/ppermute | solution.py:466
  23.5 10.9 %collective-permute-start.13 = (bf16[512,384]{1,0:T(8,128)(2,1)S(1)}, bf16[512,384]{1,0:T(8,128)(2,1)S(1)}, u32[]{:S(2)}, u32[]{:S(2)}) collective-permute-start(bf16[512,384]{1,0:T(8,128)(2,1)S(1)} %collective-permute-done.10.refs_7_), channel_id=1, source_target_pairs={{8,16},{10,18},{12,20},{14,22},{16,8},{18,10},{20,12},{22,14},{9,1... | collective-permute-start | bytes 1179656 | tf_op jit(solution)/shard_map/ppermute | solution.py:466
  27.3 7.7 %collective-permute-start.4 = (bf16[384,384]{1,0:T(8,128)(2,1)S(1)}, bf16[384,384]{1,0:T(8,128)(2,1)S(1)}, u32[]{:S(2)}, u32[]{:S(2)}) collective-permute-start(bf16[384,384]{1,0:T(8,128)(2,1)S(1)} %get-tuple-element.80), channel_id=1, source_target_pairs={{0,2},{2,0},{4,6},{6,4},{8,10},{10,8},{12,14},{14,12},{16,18},{18,... | collective-permute-start | bytes 884744 | tf_op jit(solution)/shard_map/ppermute | solution.py:460
  28.6 18.5 %collective-permute-start.7 = (bf16[192,1536]{1,0:T(8,128)(2,1)S(1)}, bf16[192,1536]{1,0:T(8,128)(2,1)S(1)}, u32[]{:S(2)}, u32[]{:S(2)}) collective-permute-start(bf16[192,1536]{1,0:T(8,128)(2,1)S(1)} %copy-done.5), channel_id=1, source_target_pairs={{0,1},{1,0},{2,3},{3,2},{4,5},{5,4},{6,7},{7,6},{8,9},{9,8},{10,11... | collective-permute-start | bytes 1769480 | tf_op jit(solution)/shard_map/ppermute | solution.py:460
  29.8 8.2 %collective-permute-start.5 = (bf16[384,384]{1,0:T(8,128)(2,1)S(1)}, bf16[384,384]{1,0:T(8,128)(2,1)S(1)}, u32[]{:S(2)}, u32[]{:S(2)}) collective-permute-start(bf16[384,384]{1,0:T(8,128)(2,1)S(1)} %get-tuple-element.81), channel_id=1, source_target_pairs={{0,4},{2,6},{4,0},{6,2},{8,12},{10,14},{12,8},{14,10},{16,20},{18,... | collective-permute-start | bytes 884744 | tf_op jit(solution)/shard_map/ppermute | solution.py:460
  32.7 12.4 %collective-permute-start.6 = (bf16[384,384]{1,0:T(8,128)(2,1)S(1)}, bf16[384,384]{1,0:T(8,128)(2,1)S(1)}, u32[]{:S(2)}, u32[]{:S(2)}) collective-permute-start(bf16[384,384]{1,0:T(8,128)(2,1)S(1)} %get-tuple-element.82), channel_id=1, source_target_pairs={{0,6},{2,4},{4,2},{6,0},{8,14},{10,12},{12,10},{14,8},{16,22},{18,... | collective-permute-start | bytes 884744 | tf_op jit(solution)/shard_map/ppermute | solution.py:460
  34.3 14.7 %collective-permute-start.28 = (bf16[512,384]{1,0:T(8,128)(2,1)S(1)}, bf16[512,384]{1,0:T(8,128)(2,1)S(1)}, u32[]{:S(2)}, u32[]{:S(2)}) collective-permute-start(bf16[512,384]{1,0:T(8,128)(2,1)S(1)} %shard_map.112.refs_6_), channel_id=1, source_target_pairs={{8,16},{10,18},{12,20},{14,22},{16,8},{18,10},{20,12},{22,14},{9,1... | collective-permute-start | bytes 1179656 | tf_op jit(solution)/shard_map/ppermute | solution.py:466
  35.0 15.2 %collective-permute-start.12 = (bf16[512,384]{1,0:T(8,128)(2,1)S(1)}, bf16[512,384]{1,0:T(8,128)(2,1)S(1)}, u32[]{:S(2)}, u32[]{:S(2)}) collective-permute-start(bf16[512,384]{1,0:T(8,128)(2,1)S(1)} %collective-permute-done.11.refs_8_), channel_id=1, source_target_pairs={{8,0},{10,2},{12,4},{14,6},{16,24},{18,26},{20,28},{22,30},{9,1},{... | collective-permute-start | bytes 1179656 | tf_op jit(solution)/shard_map/ppermute | solution.py:466
  38.1 15.0 %collective-permute-start.30 = (bf16[512,384]{1,0:T(8,128)(2,1)S(1)}, bf16[512,384]{1,0:T(8,128)(2,1)S(1)}, u32[]{:S(2)}, u32[]{:S(2)}) collective-permute-start(bf16[512,384]{1,0:T(8,128)(2,1)S(1)} %collective-permute-done.27.refs_7_), channel_id=1, source_target_pairs={{8,16},{10,18},{12,20},{14,22},{16,8},{18,10},{20,12},{22,14},{9,1... | collective-permute-start | bytes 1179656 | tf_op jit(solution)/shard_map/ppermute | solution.py:466
  45.2 13.5 %collective-permute-start.14 = (bf16[512,384]{1,0:T(8,128)(2,1)S(1)}, bf16[512,384]{1,0:T(8,128)(2,1)S(1)}, u32[]{:S(2)}, u32[]{:S(2)}) collective-permute-start(bf16[512,384]{1,0:T(8,128)(2,1)S(1)} %collective-permute-done.13.refs_10_), channel_id=1, source_target_pairs={{8,0},{10,2},{12,4},{14,6},{16,24},{18,26},{20,28},{22,30},{9,1},{... | collective-permute-start | bytes 1179656 | tf_op jit(solution)/shard_map/ppermute | solution.py:466
  47.7 17.8 %copy-start.2 = (s32[16]{0:T(128)S(1)}, s32[16]{0:T(128)}, u32[]{:S(2)}) copy-start(s32[16]{0:T(128)} %pages.3) | copy-start | bytes 196
  47.7 15.1 %collective-permute-start.8 = (bf16[256,384]{1,0:T(8,128)(2,1)S(1)}, bf16[256,384]{1,0:T(8,128)(2,1)S(1)}, u32[]{:S(2)}, u32[]{:S(2)}) collective-permute-start(bf16[256,384]{1,0:T(8,128)(2,1)S(1)} %shard_map.106), channel_id=1, source_target_pairs={{0,8},{2,10},{4,12},{6,14},{16,24},{18,26},{20,28},{22,30},{1,9},{... | collective-permute-start | bytes 589832 | tf_op jit(solution)/shard_map/ppermute | solution.py:466
  49.0 15.1 %collective-permute-start.9 = (bf16[256,384]{1,0:T(8,128)(2,1)S(1)}, bf16[256,384]{1,0:T(8,128)(2,1)S(1)}, u32[]{:S(2)}, u32[]{:S(2)}) collective-permute-start(bf16[256,384]{1,0:T(8,128)(2,1)S(1)} %shard_map.106), channel_id=1, source_target_pairs={{8,16},{10,18},{12,20},{14,22},{9,17},{11,19},{13,21},{15,23}} | collective-permute-start | bytes 589832 | tf_op jit(solution)/shard_map/ppermute | solution.py:466
  50.2 23.8 %collective-permute-start.18 = (bf16[384,384]{1,0:T(8,128)(2,1)S(1)}, bf16[384,384]{1,0:T(8,128)(2,1)S(1)}, u32[]{:S(2)}, u32[]{:S(2)}) collective-permute-start(bf16[384,384]{1,0:T(8,128)(2,1)S(1)} %get-tuple-element.108), channel_id=1, source_target_pairs={{0,2},{2,0},{4,6},{6,4},{8,10},{10,8},{12,14},{14,12},{16,18},{18,... | collective-permute-start | bytes 884744 | tf_op jit(solution)/shard_map/ppermute | solution.py:460
  53.0 22.7 %collective-permute-start.19 = (bf16[384,384]{1,0:T(8,128)(2,1)S(1)}, bf16[384,384]{1,0:T(8,128)(2,1)S(1)}, u32[]{:S(2)}, u32[]{:S(2)}) collective-permute-start(bf16[384,384]{1,0:T(8,128)(2,1)S(1)} %get-tuple-element.109), channel_id=1, source_target_pairs={{0,4},{2,6},{4,0},{6,2},{8,12},{10,14},{12,8},{14,10},{16,20},{18,... | collective-permute-start | bytes 884744 | tf_op jit(solution)/shard_map/ppermute | solution.py:460
  58.7 17.7 %collective-permute-start.20 = (bf16[384,384]{1,0:T(8,128)(2,1)S(1)}, bf16[384,384]{1,0:T(8,128)(2,1)S(1)}, u32[]{:S(2)}, u32[]{:S(2)}) collective-permute-start(bf16[384,384]{1,0:T(8,128)(2,1)S(1)} %get-tuple-element.110), channel_id=1, source_target_pairs={{0,6},{2,4},{4,2},{6,0},{8,14},{10,12},{12,10},{14,8},{16,22},{18,... | collective-permute-start | bytes 884744 | tf_op jit(solution)/shard_map/ppermute | solution.py:460
  62.9 23.5 %collective-permute-start.29 = (bf16[512,384]{1,0:T(8,128)(2,1)S(1)}, bf16[512,384]{1,0:T(8,128)(2,1)S(1)}, u32[]{:S(2)}, u32[]{:S(2)}) collective-permute-start(bf16[512,384]{1,0:T(8,128)(2,1)S(1)} %collective-permute-done.28.refs_8_), channel_id=1, source_target_pairs={{8,0},{10,2},{12,4},{14,6},{16,24},{18,26},{20,28},{22,30},{9,1},{... | collective-permute-start | bytes 1179656 | tf_op jit(solution)/shard_map/ppermute | solution.py:466
  64.2 22.2 %collective-permute-start.31 = (bf16[512,384]{1,0:T(8,128)(2,1)S(1)}, bf16[512,384]{1,0:T(8,128)(2,1)S(1)}, u32[]{:S(2)}, u32[]{:S(2)}) collective-permute-start(bf16[512,384]{1,0:T(8,128)(2,1)S(1)} %collective-permute-done.30.refs_10_), channel_id=1, source_target_pairs={{8,0},{10,2},{12,4},{14,6},{16,24},{18,26},{20,28},{22,30},{9,1},{... | collective-permute-start | bytes 1179656 | tf_op jit(solution)/shard_map/ppermute | solution.py:466
  74.1 4.2 %collective-permute-start.15 = (bf16[128,384]{1,0:T(8,128)(2,1)S(1)}, bf16[128,384]{1,0:T(8,128)(2,1)S(1)}, u32[]{:S(2)}, u32[]{:S(2)}) collective-permute-start(bf16[128,384]{1,0:T(8,128)(2,1)S(1)} %get-tuple-element.102), channel_id=1, source_target_pairs={{0,2},{2,0},{4,6},{6,4},{8,10},{10,8},{12,14},{14,12},{16,18},{18,... | collective-permute-start | bytes 294920 | tf_op jit(solution)/shard_map/ppermute | solution.py:460
  75.7 4.4 %collective-permute-start.16 = (bf16[128,384]{1,0:T(8,128)(2,1)S(1)}, bf16[128,384]{1,0:T(8,128)(2,1)S(1)}, u32[]{:S(2)}, u32[]{:S(2)}) collective-permute-start(bf16[128,384]{1,0:T(8,128)(2,1)S(1)} %get-tuple-element.103), channel_id=1, source_target_pairs={{0,4},{2,6},{4,0},{6,2},{8,12},{10,14},{12,8},{14,10},{16,20},{18,... | collective-permute-start | bytes 294920 | tf_op jit(solution)/shard_map/ppermute | solution.py:460
  77.0 9.4 %collective-permute-start.22 = (bf16[256,384]{1,0:T(8,128)(2,1)S(1)}, bf16[256,384]{1,0:T(8,128)(2,1)S(1)}, u32[]{:S(2)}, u32[]{:S(2)}) collective-permute-start(bf16[256,384]{1,0:T(8,128)(2,1)S(1)} %shard_map.111), channel_id=1, source_target_pairs={{0,8},{2,10},{4,12},{6,14},{16,24},{18,26},{20,28},{22,30},{1,9},{... | collective-permute-start | bytes 589832 | tf_op jit(solution)/shard_map/ppermute | solution.py:466
  78.3 8.1 %collective-permute-start.23 = (bf16[256,384]{1,0:T(8,128)(2,1)S(1)}, bf16[256,384]{1,0:T(8,128)(2,1)S(1)}, u32[]{:S(2)}, u32[]{:S(2)}) collective-permute-start(bf16[256,384]{1,0:T(8,128)(2,1)S(1)} %shard_map.111), channel_id=1, source_target_pairs={{8,16},{10,18},{12,20},{14,22},{9,17},{11,19},{13,21},{15,23}} | collective-permute-start | bytes 589832 | tf_op jit(solution)/shard_map/ppermute | solution.py:466
  80.1 5.2 %collective-permute-start.17 = (bf16[128,384]{1,0:T(8,128)(2,1)S(1)}, bf16[128,384]{1,0:T(8,128)(2,1)S(1)}, u32[]{:S(2)}, u32[]{:S(2)}) collective-permute-start(bf16[128,384]{1,0:T(8,128)(2,1)S(1)} %get-tuple-element.104), channel_id=1, source_target_pairs={{0,6},{2,4},{4,2},{6,0},{8,14},{10,12},{12,10},{14,8},{16,22},{18,... | collective-permute-start | bytes 294920 | tf_op jit(solution)/shard_map/ppermute | solution.py:460
  95.1 4.5 %collective-permute-start.32 = (bf16[128,384]{1,0:T(8,128)(2,1)S(1)}, bf16[128,384]{1,0:T(8,128)(2,1)S(1)}, u32[]{:S(2)}, u32[]{:S(2)}) collective-permute-start(bf16[128,384]{1,0:T(8,128)(2,1)S(1)} %get-tuple-element.122), channel_id=1, source_target_pairs={{0,2},{2,0},{4,6},{6,4},{8,10},{10,8},{12,14},{14,12},{16,18},{18,... | collective-permute-start | bytes 294920 | tf_op jit(solution)/shard_map/ppermute | solution.py:460
  97.7 4.4 %collective-permute-start.33 = (bf16[128,384]{1,0:T(8,128)(2,1)S(1)}, bf16[128,384]{1,0:T(8,128)(2,1)S(1)}, u32[]{:S(2)}, u32[]{:S(2)}) collective-permute-start(bf16[128,384]{1,0:T(8,128)(2,1)S(1)} %get-tuple-element.123), channel_id=1, source_target_pairs={{0,4},{2,6},{4,0},{6,2},{8,12},{10,14},{12,8},{14,10},{16,20},{18,... | collective-permute-start | bytes 294920 | tf_op jit(solution)/shard_map/ppermute | solution.py:460
  98.3 6.3 %collective-permute-start.34 = (bf16[128,384]{1,0:T(8,128)(2,1)S(1)}, bf16[128,384]{1,0:T(8,128)(2,1)S(1)}, u32[]{:S(2)}, u32[]{:S(2)}) collective-permute-start(bf16[128,384]{1,0:T(8,128)(2,1)S(1)} %get-tuple-element.124), channel_id=1, source_target_pairs={{0,6},{2,4},{4,2},{6,0},{8,14},{10,12},{12,10},{14,8},{16,22},{18,... | collective-permute-start | bytes 294920 | tf_op jit(solution)/shard_map/ppermute | solution.py:460
  99.4 8.6 %collective-permute-start.21 = (bf16[128,768]{1,0:T(8,128)(2,1)S(1)}, bf16[128,768]{1,0:T(8,128)(2,1)S(1)}, u32[]{:S(2)}, u32[]{:S(2)}) collective-permute-start(bf16[128,768]{1,0:T(8,128)(2,1)S(1)} %get-tuple-element.112), channel_id=1, source_target_pairs={{0,1},{1,0},{2,3},{3,2},{4,5},{5,4},{6,7},{7,6},{8,9},{9,8},{10,11... | collective-permute-start | bytes 589832 | tf_op jit(solution)/shard_map/ppermute | solution.py:460
  105.6 6.7 %collective-permute-start.35 = (bf16[128,768]{1,0:T(8,128)(2,1)S(1)}, bf16[128,768]{1,0:T(8,128)(2,1)S(1)}, u32[]{:S(2)}, u32[]{:S(2)}) collective-permute-start(bf16[128,768]{1,0:T(8,128)(2,1)S(1)} %get-tuple-element.126), channel_id=1, source_target_pairs={{0,1},{1,0},{2,3},{3,2},{4,5},{5,4},{6,7},{7,6},{8,9},{9,8},{10,11... | collective-permute-start | bytes 589832 | tf_op jit(solution)/shard_map/ppermute | solution.py:460
